TPU v7x, 128 devices: a whole 4x4x4 slice. The times are simulated.
128 devices in a mesh: inner: 16 (over y, x), outer: 8 (over z, core).
Axes of the slice: x: 4, y: 4, z: 4, core: 2. Of those that a mesh axis runs over, the one named last changes fastest.
Arguments:
- embedding: bfloat16 [393216, 4096], P(('inner', 'outer')), may hold values from -80 to 80
- test_matrix: bfloat16 [4096, 256], replicated, may hold values from -0.09375 to 0.09375
Outputs:
- projection: float32 [4096, 256], P(('inner', 'outer'))
All inputs are finite; a program needn't handle non-finite values.
Results may differ from a plain program's by a relative error of at most 0.00035.
Values sent between devices are 32-bit elements; how exact they have to be, the bound alone decides.
No kernel may reach another device: no remote copies, remote signals or barrier semaphores. Data moves between devices by JAX's collectives and lax.ppermute only.
A program may use at most 128 MiB of HBM per device.

v0:
```python
import jax
import jax.numpy as jnp
from jax import lax
from jax.sharding import PartitionSpec as P


def local(embedding, test_matrix):
    sketch = jnp.dot(embedding, test_matrix, preferred_element_type=jnp.float32)
    local_gram = jnp.dot(
        sketch.T, sketch, precision=lax.Precision.HIGHEST, preferred_element_type=jnp.float32
    )
    partial_gram = lax.psum(local_gram, "inner")
    gram = lax.psum(partial_gram, "outer")
    lower = jnp.linalg.cholesky(gram)
    basis = lax.linalg.triangular_solve(
        lower, sketch, left_side=False, lower=True, transpose_a=True
    ).astype(jnp.bfloat16)
    sectioned = lax.psum_scatter(
        lax.dot_general(
            embedding, basis, (((0,), (0,)), ((), ())), preferred_element_type=jnp.float32
        ),
        "inner",
        scatter_dimension=0,
        tiled=True,
    )
    projection = lax.psum_scatter(sectioned, "outer", scatter_dimension=0, tiled=True)
    return projection


def solution(mesh):
    return jax.shard_map(
        local,
        mesh=mesh,
        in_specs=(P(("inner", "outer"), None), P()),
        out_specs=P(("inner", "outer"), None),
        check_vma=False,
    )
```

profile of v0, /device:TPU:1, one launch (start us, length us, event | category | flops | bytes accessed | tf_op | source)
XLA Modules:
  0.0 372.0 jit_solution(11290697298177582486)
XLA Ops:
  6.5 1.6 copy-done
  8.1 11.8 %fusion.13 = f32[3072,256]{1,0:T(8,128)S(1)} fusion(bf16[3072,4096]{1,0:T(8,128)(2,1)} %param.2, bf16[4096,256]{1,0:T(8,128)(2,1)S(1)} %copy-done), kind=kOutput, calls=%fused_computation.34 | convolution fusion | flops 6442450944 | bytes 30408704 | tf_op jit(solution)/shard_map/dot_general | solution.py:8
  20.0 1.7 copy-done.1
  21.6 6.1 %fusion.14 = f32[256,256]{0,1:T(8,128)} fusion(f32[3072,256]{1,0:T(8,128)S(1)} %fusion.13), kind=kOutput, calls=%fused_computation.35 | convolution fusion | flops 2415919104 | bytes 3407872 | tf_op jit(solution)/shard_map/dot_general | solution.py:9
  27.7 0.0 all-reduce.4.cloned.1.call-update
  27.7 0.0 all-reduce.6.cloned.1.call-start
  27.8 86.0 %all-reduce.4.cloned.1.call-done = f32[256,256]{0,1:T(8,128)} async-done(((f32[256,256]{0,1:T(8,128)}), f32[256,256]{0,1:T(8,128)}) %all-reduce.4.cloned.1.call-update) | async-done | bytes 262160 | tf_op jit(solution)/shard_map/psum | solution.py:12
  113.8 0.2 reduce-scatter.5.cloned.1.call-start
  114.1 60.9 %all-reduce.6.cloned.1.call-done = f32[256,256]{0,1:T(8,128)} async-done(((f32[256,256]{0,1:T(8,128)}), f32[256,256]{0,1:T(8,128)}) %all-reduce.6.cloned.1.call-update) | async-done | bytes 262160 | tf_op jit(solution)/shard_map/psum | solution.py:13
  174.9 1.1 copy.7
  176.0 1.0 fusion.5
  177.0 11.7 %cholesky.50 = f32[128,128]{1,0:T(8,128)S(1)} custom-call(f32[128,128]{1,0:T(8,128)S(1)} %cholesky.118), custom_call_target="Cholesky" | custom-call | tf_op jit(solution)/shard_map/jit(cholesky)/cholesky | solution.py:14
  188.8 9.8 %custom-call.14 = f32[1,128,128]{1,2,0:T(8,128)S(1)} custom-call(f32[1,128,128]{2,1,0:T(8,128)S(1)} %get-tuple-element.26), custom_call_target="InvertDiagBlocksLowerTriangular" | custom-call | tf_op jit(solution)/shard_map/jit(cholesky)/cholesky | solution.py:14
  198.6 0.2 constant_dynamic-update-slice_fusion.1
  198.8 0.3 convolution_subtract_fusion.1
  199.1 11.7 %cholesky.105 = f32[128,128]{1,0:T(8,128)S(1)} custom-call(f32[128,128]{1,0:T(8,128)S(1)} %convolution_subtract_fusion.1), custom_call_target="Cholesky" | custom-call | tf_op jit(solution)/shard_map/jit(cholesky)/cholesky | solution.py:14
  210.9 0.7 compare_reduce_fusion
  212.7 0.1 triangular_solve.58
  212.8 3.8 %while.1 = (s32[]{:T(128)}, f32[256,256]{1,0:T(8,128)S(1)}, s32[2,2]{1,0:T(2,128)S(1)}, f32[2,128,128]{2,1,0:T(8,128)S(1)}, s32[]{:T(128)}) while((s32[]{:T(128)}, f32[256,256]{1,0:T(8,128)S(1)}, s32[2,2]{1,0:T(2,128)S(1)}, f32[2,128,128]{2,1,0:T(8,128)S(1)}, s32[]{:T(128)}) %tuple.24), condition=%wide.while_cond, body=%wide.while_body.sunk | while | flops 2 | bytes 131189 | solution.py:15
  213.0 0.6 fusion.25
  213.5 1.3 bitcast_dynamic-update-slice_fusion.2
  214.8 0.6 fusion.25
  215.4 1.3 bitcast_dynamic-update-slice_fusion.2
  216.6 19.7 %custom-call.15 = f32[2,128,128]{1,2,0:T(8,128)S(1)} custom-call(f32[2,128,128]{2,1,0:T(8,128)S(1)} %get-tuple-element.12), custom_call_target="InvertDiagBlocksLowerTriangular" | custom-call | tf_op jit(solution)/shard_map/triangular_solve | solution.py:15
  236.3 3.1 fusion.12
  239.5 2.6 convolution_subtract_fusion
  242.1 1.6 convolution_convert_fusion
  243.6 13.5 %convolution_bitcast_fusion = f32[4096,256]{0,1:T(8,128)} fusion(bf16[3072,4096]{1,0:T(8,128)(2,1)} %param.2, bf16[3072,128]{0,1:T(8,128)(2,1)S(1)} %convolution_convert_fusion, bf16[3072,128]{0,1:T(8,128)(2,1)S(1)} %get-tuple-element.29), kind=kOutput, calls=%fused_computation.2 | convolution fusion | flops 6445596672 | bytes 30932992 | tf_op jit(solution)/shard_map/dot_general | solution.py:19
  257.2 0.0 reduce-scatter.7.cloned.1.call-start
  257.3 76.9 %reduce-scatter.5.cloned.1.call-done = f32[256,256]{0,1:T(8,128)} async-done(((f32[4096,256]{0,1:T(8,128)}), f32[256,256]{0,1:T(8,128)}) %reduce-scatter.5.cloned.1.call-update) | async-done | bytes 262160 | tf_op jit(solution)/shard_map/reduce_scatter | solution.py:18
  334.2 1.8 copy.10
  336.0 29.5 %reduce-scatter.7.cloned.1.call-done = f32[32,256]{1,0:T(8,128)} async-done(((f32[256,256]{1,0:T(8,128)}), f32[32,256]{1,0:T(8,128)}) %reduce-scatter.7.cloned.1.call-update) | async-done | bytes 32784 | tf_op jit(solution)/shard_map/reduce_scatter | solution.py:26
  (17 shorter events, 0.2 us)
Async XLA Ops:
  6.5 1.6 copy-start
  6.5 107.3 %all-reduce.4.cloned.1.call-start = ((), (), s32[]{:S(2)}) async-start(), calls=%async_computation.2 | async-start | bytes 524288 | tf_op jit(solution)/shard_map/psum | solution.py:12
  20.0 1.7 copy-start.1
  27.7 147.2 %all-reduce.6.cloned.1.call-start = ((), (), s32[]{:S(2)}) async-start(), calls=%async_computation.3 | async-start | bytes 524288 | tf_op jit(solution)/shard_map/psum | solution.py:13
  113.8 220.3 %reduce-scatter.5.cloned.1.call-start = ((), (), s32[]{:S(2)}) async-start(), calls=%async_computation.4 | async-start | bytes 4456448 | tf_op jit(solution)/shard_map/reduce_scatter | solution.py:18
  236.3 3.1 copy-start.2
  257.2 108.3 %reduce-scatter.7.cloned.1.call-start = ((), (), s32[]{:S(2)}) async-start(), calls=%async_computation.5 | async-start | bytes 294912 | tf_op jit(solution)/shard_map/reduce_scatter | solution.py:26
Sparse Core Ops, SparseCore 0:
  27.8 85.9 all-reduce.3
  116.2 58.6 all-reduce.5
  257.3 76.8 reduce-scatter.4
  336.5 28.9 reduce-scatter.6
where the time goes:
time: 374 us; the launch traced here: 372 us
  waiting for transfers between devices  253 us (68%)
  other arithmetic  54.7 us (15%)
  matrix products  39.2 us (10%)
  between operations  14.4 us (4%)
  local copies, waits for them, and re-layouts  9.82 us (3%)
    psum x1, waiting for transfers between devices, local(): partial_gram = lax.psum(local_gram, 'inner')  86 us
    reduce_scatter x1, waiting for transfers between devices, local(): lax.psum_scatter(lax.dot_general(embedding, basis, (((0,), (0,)), ((), ()...  76.9 us
    psum x1, waiting for transfers between devices, local(): gram = lax.psum(partial_gram, 'outer')  60.9 us
    another operation x6, other arithmetic, local(): lower = jnp.linalg.cholesky(gram)  34 us
    reduce_scatter x1, waiting for transfers between devices, local(): lax.psum_scatter(sectioned, 'outer', scatter_dimension=0, tiled=True)  29.5 us
    another operation x3, other arithmetic, local(): lax.linalg.triangular_solve(lower, sketch, left_side=False, lower=True, t...  19.7 us
    dot_general x1, matrix products, local(): lax.dot_general(embedding, basis, (((0,), (0,)), ((), ())), preferred_ele...  13.5 us
    dot_general x1, matrix products, local(): sketch = jnp.dot(embedding, test_matrix, preferred_element_type=jnp.float32)  11.8 us
  transfers between devices with their start and end apart: 4, of which 4 were waited for; matrix products, arithmetic and copies ran while one was open for 0% of the time, Pallas kernels for 0%

commit v1 on v0

v1 whole, which is shorter than its diff:
```python
import jax
import jax.numpy as jnp
from jax import lax
from jax.experimental import pallas as pl
from jax.experimental.pallas import tpu as pltpu
from jax.sharding import Mesh, PartitionSpec as P

K = 256
B = 8
MIB = 1 << 20


def tree(terms):
    while len(terms) > 1:
        terms = [
            terms[i] + terms[i + 1] if i + 1 < len(terms) else terms[i]
            for i in range(0, len(terms), 2)
        ]
    return terms[0]


def sketch_kernel(e_ref, t_ref, st_ref, gram_ref, cross_ref):
    i = pl.program_id(0)
    s = jnp.dot(e_ref[...], t_ref[...], preferred_element_type=jnp.float32)
    hi = s.astype(jnp.bfloat16)
    rest = s - hi.astype(jnp.float32)
    mid = rest.astype(jnp.bfloat16)
    lo = (rest - mid.astype(jnp.float32)).astype(jnp.bfloat16)
    st = s.T
    hi_t = st.astype(jnp.bfloat16)
    mid_t = (st - hi_t.astype(jnp.float32)).astype(jnp.bfloat16)
    st_ref[0:K, :] = hi_t
    st_ref[K : 2 * K, :] = mid_t
    f32 = jnp.float32
    square = jnp.dot(hi_t, hi, preferred_element_type=f32) + jnp.dot(
        mid_t, mid, preferred_element_type=f32
    )
    cross = jnp.dot(hi_t, mid, preferred_element_type=f32) + jnp.dot(
        hi_t, lo, preferred_element_type=f32
    )

    @pl.when(i == 0)
    def _():
        gram_ref[...] = square
        cross_ref[...] = cross

    @pl.when(i > 0)
    def _():
        gram_ref[...] += square
        cross_ref[...] += cross

    @pl.when(i == pl.num_programs(0) - 1)
    def _():
        both = cross_ref[...]
        gram_ref[...] += both + both.T


def sketch_and_gram(e, t):
    rows, d = e.shape
    r = 512
    return pl.pallas_call(
        sketch_kernel,
        grid=(rows // r,),
        in_specs=[
            pl.BlockSpec((r, d), lambda i: (i, 0)),
            pl.BlockSpec((d, K), lambda i: (0, 0)),
        ],
        out_specs=[
            pl.BlockSpec((2 * K, r), lambda i: (0, i)),
            pl.BlockSpec((K, K), lambda i: (0, 0)),
        ],
        out_shape=[
            jax.ShapeDtypeStruct((2 * K, rows), jnp.bfloat16),
            jax.ShapeDtypeStruct((K, K), jnp.float32),
        ],
        scratch_shapes=[pltpu.VMEM((K, K), jnp.float32)],
        compiler_params=pltpu.CompilerParams(vmem_limit_bytes=40 * MIB),
        cost_estimate=pl.CostEstimate(
            flops=2 * rows * K * (d + 4 * K),
            bytes_accessed=rows * d * 2 + d * K * 2 + rows * K * 4,
            transcendentals=0,
        ),
        name="sketch",
    )(e, t)


def product_kernel(core_ref, e_ref, st_ref, keep_ref, send_ref):
    mt = jnp.dot(st_ref[...], e_ref[...], preferred_element_type=jnp.float32)
    m = (mt[0:K] + mt[K : 2 * K]).T
    m = m.reshape(keep_ref.shape[0], 2, 32, K)
    core = core_ref[0]

    @pl.when(core == 0)
    def _():
        keep_ref[...] = m[:, 0]
        send_ref[...] = m[:, 1]

    @pl.when(core != 0)
    def _():
        keep_ref[...] = m[:, 1]
        send_ref[...] = m[:, 0]


def product(core, e, st):
    rows, d = e.shape
    cols = 512
    n = cols // 64
    half = jax.ShapeDtypeStruct((d // 64, 32, K), jnp.float32)
    spec = pl.BlockSpec((n, 32, K), lambda i: (i, 0, 0))
    return pl.pallas_call(
        product_kernel,
        grid=(d // cols,),
        in_specs=[
            pl.BlockSpec(memory_space=pltpu.SMEM),
            pl.BlockSpec((rows, cols), lambda i: (0, i)),
            pl.BlockSpec((2 * K, rows), lambda i: (0, 0)),
        ],
        out_specs=[spec, spec],
        out_shape=[half, half],
        compiler_params=pltpu.CompilerParams(vmem_limit_bytes=40 * MIB),
        cost_estimate=pl.CostEstimate(
            flops=4 * rows * K * d,
            bytes_accessed=rows * d * 2 + rows * K * 4 + d * K * 4,
            transcendentals=0,
        ),
        name="product",
    )(core, e, st)


def small_inverse(d):
    n = len(d)
    d = [list(row) for row in d]
    l = [[None] * n for _ in range(n)]
    w = [[None] * n for _ in range(n)]
    for i in range(n):
        inv = lax.rsqrt(d[i][i])
        w[i][i] = inv
        for a in range(i + 1, n):
            l[a][i] = d[a][i] * inv
        for a in range(i + 1, n):
            for b in range(i + 1, a + 1):
                d[a][b] = d[a][b] - l[a][i] * l[b][i]
        for b in range(i):
            w[i][b] = -inv * tree([l[i][k] * w[k][b] for k in range(b, i)])
    return w


def inverse_factor_kernel(g_ref, x):
    x[...] = g_ref[...]
    lane = lax.broadcasted_iota(jnp.int32, (B, 128), 1)
    for j in range(K // B):
        b0 = j * B
        h, o = divmod(b0, 128)
        inside = (lane >= o) & (lane < o + B)
        panel = x[b0 : b0 + B, h * 128 : (h + 1) * 128]
        cols = [jnp.broadcast_to(panel[:, o + b : o + b + 1], (B, 128)) for b in range(B)]
        d = [
            [jnp.broadcast_to(cols[b][a : a + 1, :], (B, 128)) for b in range(a + 1)]
            for a in range(B)
        ]
        w = small_inverse(d)
        dinv = [[None] * B for _ in range(B)]
        for a in range(B):
            for b in range(a + 1):
                v = tree([w[k][a] * w[k][b] for k in range(a, B)])
                dinv[a][b] = dinv[b][a] = v
        rows = []
        for half in range(2):
            part = []
            for a in range(B):
                r = jnp.broadcast_to(
                    x[b0 + a : b0 + a + 1, half * 128 : (half + 1) * 128], (B, 128)
                )
                if half == h:
                    r = jnp.where(inside, jnp.where(lane == o + a, 1.0, 0.0), r)
                part.append(r)
            rows.append(part)
        y = [
            [tree([dinv[k][a] * rows[half][a] for a in range(B)]) for k in range(B)]
            for half in range(2)
        ]
        for r in range(j + 1, K // B):
            sl = slice(r * B, (r + 1) * B)
            old = [x[sl, 0:128], x[sl, 128:256]]
            c = [
                jnp.broadcast_to(old[h][:, o + k : o + k + 1], (B, 128)) for k in range(B)
            ]
            for half in range(2):
                base = old[half]
                if half == h:
                    base = jnp.where(inside, 0.0, base)
                x[sl, half * 128 : (half + 1) * 128] = base - tree(
                    [c[k] * y[half][k] for k in range(B)]
                )
        for half in range(2):
            for i in range(B):
                if half > h:
                    v = jnp.zeros((1, 128), jnp.float32)
                else:
                    v = tree([w[i][k] * rows[half][k] for k in range(i + 1)])
                    if half == h:
                        v = jnp.where(lane < o + B, v, 0.0)
                x[b0 + i : b0 + i + 1, half * 128 : (half + 1) * 128] = v[0:1, :]


def inverse_factor(g):
    return pl.pallas_call(
        inverse_factor_kernel,
        out_shape=jax.ShapeDtypeStruct((K, K), jnp.float32),
        in_specs=[pl.BlockSpec(memory_space=pltpu.VMEM)],
        out_specs=pl.BlockSpec(memory_space=pltpu.VMEM),
        compiler_params=pltpu.CompilerParams(vmem_limit_bytes=32 * MIB),
        cost_estimate=pl.CostEstimate(
            flops=12_000_000_000, bytes_accessed=1 << 19, transcendentals=256
        ),
        name="inverse_factor",
    )(g)


def finish_kernel(parts_ref, w_ref, out_ref):
    m = jnp.sum(parts_ref[...], axis=0)
    out_ref[...] = lax.dot_general(
        m,
        w_ref[...],
        (((1,), (1,)), ((), ())),
        precision=lax.Precision.HIGHEST,
        preferred_element_type=jnp.float32,
    )


def finish(parts, w):
    return pl.pallas_call(
        finish_kernel,
        out_shape=jax.ShapeDtypeStruct((32, K), jnp.float32),
        in_specs=[pl.BlockSpec(memory_space=pltpu.VMEM)] * 2,
        out_specs=pl.BlockSpec(memory_space=pltpu.VMEM),
        compiler_params=pltpu.CompilerParams(vmem_limit_bytes=32 * MIB),
        name="finish",
    )(parts, w)


def solution(mesh):
    chips = ("y", "x", "z")
    every = chips + ("core",)
    fine = Mesh(mesh.devices.reshape(4, 4, 4, 2), every)
    swap = [(0, 1), (1, 0)]

    def local(embedding, test_matrix):
        core = lax.axis_index("core").astype(jnp.int32).reshape(1)
        st, gram = sketch_and_gram(embedding, test_matrix)
        pieces = lax.all_to_all(gram.reshape(128, 2, K), every, 0, 0, tiled=True)
        keep, send = product(core, embedding, st)
        mine = keep + lax.ppermute(send, "core", swap)
        parts = lax.all_to_all(mine, chips, 0, 0, tiled=True)
        rows = jnp.sum(pieces, axis=0)
        gram = lax.all_to_all(
            jnp.broadcast_to(rows, (128, 2, K)), every, 0, 0, tiled=True
        ).reshape(K, K)
        return finish(parts, inverse_factor(gram))

    return jax.shard_map(
        local,
        mesh=fine,
        in_specs=(P(every, None), P()),
        out_specs=P(every, None),
        check_vma=False,
    )
```

time: 374 us -> 111 us (0.30)
  waiting for transfers between devices: 253 us -> 24.1 us
  other arithmetic: 54.7 us -> 3.43 us
  Pallas kernels: 0 us -> 46.3 us
  matrix products: 39.2 us -> 0 us
  blocking collectives: 0 us -> 20.9 us
  between operations: 14.4 us -> 0.06 us
  starting transfers between devices: 0.3 us -> 11.1 us
  local copies, waits for them, and re-layouts: 9.82 us -> 2.69 us
    psum x2 -> x0, waiting for transfers between devices: 147 us -> none  [the longest x1 86 us: local(): partial_gram = lax.psum(local_gram, 'inner')]
    reduce_scatter x2 -> x0, waiting for transfers between devices: 106 us -> none  [the longest x1 76.9 us: local(): lax.psum_scatter(lax.dot_general(embedding, basis, (((0,), (0,)), ((), ()...]
    another operation x9 -> x0, other arithmetic: 53.7 us -> none  [the longest x6 34 us: local(): lower = jnp.linalg.cholesky(gram)]
    pallas_call x0 -> x4, Pallas kernels: none -> 46.3 us  [the longest x1 18.4 us: product(): pl.pallas_call(product_kernel, grid=(d // cols,), in_specs=[pl.BlockSpec(...]
    dot_general x3 -> x0, matrix products: 31.4 us -> none  [the longest x1 13.5 us: local(): lax.dot_general(embedding, basis, (((0,), (0,)), ((), ())), preferred_ele...]
    all_to_all x0 -> x2, waiting for transfers between devices: none -> 24.1 us  [the longest x1 16.4 us: local(): parts = lax.all_to_all(mine, chips, 0, 0, tiled=True)]
    all_to_all x0 -> x1, blocking collectives: none -> 20.9 us  [local(): pieces = lax.all_to_all(gram.reshape(128, 2, K), every, 0, 0, tiled=True)]
    all_to_all x0 -> x2, starting transfers between devices: none -> 9.8 us  [the longest x1 5.32 us: local(): parts = lax.all_to_all(mine, chips, 0, 0, tiled=True)]
  transfers between devices with their start and end apart: 4 -> 3, of which waited for: 4 -> 2; matrix products, arithmetic and copies ran while one was open for 0% -> 4% of each run, Pallas kernels for 0% -> 10%
where the time goes in v1:
time: 111 us; the launch traced here: 109 us
  Pallas kernels  46.3 us (42%)
  waiting for transfers between devices  24.1 us (22%)
  blocking collectives  20.9 us (19%)
  starting transfers between devices  11.1 us (10%)
  other arithmetic  3.43 us (3%)
  local copies, waits for them, and re-layouts  2.69 us (2%)
    all_to_all x1, blocking collectives, local(): pieces = lax.all_to_all(gram.reshape(128, 2, K), every, 0, 0, tiled=True)  20.9 us
    pallas_call x1, Pallas kernels, product(): pl.pallas_call(product_kernel, grid=(d // cols,), in_specs=[pl.BlockSpec(...  18.4 us
    all_to_all x1, waiting for transfers between devices, local(): parts = lax.all_to_all(mine, chips, 0, 0, tiled=True)  16.4 us
    pallas_call x1, Pallas kernels, sketch_and_gram(): pl.pallas_call(sketch_kernel, grid=(rows // r,), in_specs=[pl.BlockSpec((...  15.8 us
    pallas_call x1, Pallas kernels, inverse_factor(): pl.pallas_call(inverse_factor_kernel, out_shape=jax.ShapeDtypeStruct((K,...  11.1 us
    all_to_all x1, waiting for transfers between devices, local(): lax.all_to_all(jnp.broadcast_to(rows, (128, 2, K)), every, 0, 0, tiled=True)  7.69 us
    all_to_all x1, starting transfers between devices, local(): parts = lax.all_to_all(mine, chips, 0, 0, tiled=True)  5.32 us
    all_to_all x1, starting transfers between devices, local(): lax.all_to_all(jnp.broadcast_to(rows, (128, 2, K)), every, 0, 0, tiled=True)  4.49 us
  transfers between devices with their start and end apart: 3, of which 2 were waited for; matrix products, arithmetic and copies ran while one was open for 4% of the time, Pallas kernels for 10%

profile of v1, /device:TPU:1, one launch (start us, length us, event | category | flops | bytes accessed | tf_op | source)
XLA Modules:
  0.0 108.6 jit_solution(857258041643569947)
XLA Ops:
  0.0 0.0 copy-start
  0.0 1.6 %copy-done = bf16[4096,256]{1,0:T(8,128)(2,1)S(1)} copy-done((bf16[4096,256]{1,0:T(8,128)(2,1)S(1)}, bf16[4096,256]{1,0:T(8,128)(2,1)}, u32[]{:S(2)}) %copy-start) | copy-done | bytes 2097176
  1.6 15.8 %sketch.1 = (bf16[512,3072]{1,0:T(8,128)(2,1)S(1)}, f32[256,256]{1,0:T(8,128)S(1)}) custom-call(bf16[3072,4096]{1,0:T(8,128)(2,1)} %e_ref.3, bf16[4096,256]{1,0:T(8,128)(2,1)S(1)} %copy-done), custom_call_target="tpu_custom_call" | custom-call | flops 8053063680 | bytes 30408704 | tf_op jit(solution)/shard_map/sketch/pallas_call | solution.py:61
  17.4 18.4 %product.1 = (f32[64,32,256]{2,1,0:T(8,128)S(1)}, f32[64,32,256]{2,1,0:T(8,128)}) custom-call(s32[1]{0:T(128)} %bitcast.core_ref, bf16[3072,4096]{1,0:T(8,128)(2,1)} %e_ref.3, bf16[512,3072]{1,0:T(8,128)(2,1)S(1)} %get-tuple-element.9.st_ref), custom_call_target="tpu_custom_call" | custom-call | flops 12884901888 | bytes 32505856 | tf_op jit(solution)/shard_map/product/pallas_call | solution.py:110
  35.8 1.3 %collective-permute-start = (f32[64,32,256]{2,1,0:T(8,128)}, f32[64,32,256]{2,1,0:T(8,128)}, u32[]{:S(2)}, u32[]{:S(2)}) collective-permute-start(f32[64,32,256]{2,1,0:T(8,128)} %get-tuple-element.11), channel_id=1, source_target_pairs={{0,1},{1,0},{2,3},{3,2},{4,5},{5,4},{6,7},{7,6},{8,9},{9,8},{10,11... | collective-permute-start | bytes 6291464 | tf_op jit(solution)/shard_map/ppermute | solution.py:253
  37.1 0.1 reshape.10
  37.3 20.9 %all_to_all.15 = f32[128,2,256]{2,1,0:T(2,128)S(1)} all-to-all(f32[128,2,256]{2,1,0:T(2,128)S(1)} %reshape.10), channel_id=1, replica_groups=mesh['y'=4,'x'=4,'z'=4,'core'=2] {'y','x','z','core'}, dimensions={0} | all-to-all | bytes 524288 | tf_op jit(solution)/shard_map/all_to_all | solution.py:251
  58.2 0.1 reduce_sum.9
  58.4 0.8 broadcast_in_dim.3
  59.1 4.5 %all-to-all-start.2 = ((f32[128,2,256]{2,1,0:T(2,128)}), f32[128,2,256]{2,1,0:T(2,128)S(1)}, u32[]{:S(2)}, u32[]{:S(2)}) async-start(f32[128,2,256]{2,1,0:T(2,128)} %broadcast_in_dim.3), calls=%async_computation.2 | async-start | bytes 524288 | tf_op jit(solution)/shard_map/all_to_all | solution.py:256
  63.6 0.0 collective-permute-done
  63.6 3.3 %add.3 = f32[64,32,256]{2,1,0:T(8,128)} add(f32[64,32,256]{2,1,0:T(8,128)S(1)} %get-tuple-element.10, f32[64,32,256]{2,1,0:T(8,128)} %collective-permute-done) | non-fusion elementwise | flops 524288 | bytes 6291456 | tf_op jit(solution)/shard_map/add | solution.py:253
  66.9 7.7 %all-to-all-done.2 = f32[128,2,256]{2,1,0:T(2,128)S(1)} async-done(((f32[128,2,256]{2,1,0:T(2,128)}), f32[128,2,256]{2,1,0:T(2,128)S(1)}, u32[]{:S(2)}, u32[]{:S(2)}) %all-to-all-start.2) | async-done | bytes 262176 | tf_op jit(solution)/shard_map/all_to_all | solution.py:256
  74.6 5.3 %all-to-all-start = ((f32[64,32,256]{2,1,0:T(8,128)}), f32[64,32,256]{2,1,0:T(8,128)S(1)}, u32[]{:S(2)}, u32[]{:S(2)}) async-start(f32[64,32,256]{2,1,0:T(8,128)} %add.3), calls=%async_computation | async-start | bytes 4194304 | tf_op jit(solution)/shard_map/all_to_all | solution.py:254
  79.9 0.2 reshape.11.g_ref
  80.1 11.1 %inverse_factor.1.w_ref = f32[256,256]{1,0:T(8,128)S(1)} custom-call(f32[256,256]{1,0:T(8,128)S(1)} %reshape.11.g_ref), custom_call_target="tpu_custom_call" | custom-call | flops 12000000000 | bytes 524288 | tf_op jit(solution)/shard_map/inverse_factor/pallas_call | solution.py:207
  91.2 16.4 %all-to-all-done.parts_ref = f32[64,32,256]{2,1,0:T(8,128)S(1)} async-done(((f32[64,32,256]{2,1,0:T(8,128)}), f32[64,32,256]{2,1,0:T(8,128)S(1)}, u32[]{:S(2)}, u32[]{:S(2)}) %all-to-all-start) | async-done | bytes 2097184 | tf_op jit(solution)/shard_map/all_to_all | solution.py:254
  107.6 1.0 finish.1
Async XLA Ops:
  0.0 1.6 %copy-start = (bf16[4096,256]{1,0:T(8,128)(2,1)S(1)}, bf16[4096,256]{1,0:T(8,128)(2,1)}, u32[]{:S(2)}) copy-start(bf16[4096,256]{1,0:T(8,128)(2,1)} %t_ref.1) | copy-start | bytes 6291460
  35.8 27.8 %collective-permute-start = (f32[64,32,256]{2,1,0:T(8,128)}, f32[64,32,256]{2,1,0:T(8,128)}, u32[]{:S(2)}, u32[]{:S(2)}) collective-permute-start(f32[64,32,256]{2,1,0:T(8,128)} %get-tuple-element.11), channel_id=1, source_target_pairs={{0,1},{1,0},{2,3},{3,2},{4,5},{5,4},{6,7},{7,6},{8,9},{9,8},{10,11... | collective-permute-start | bytes 6291464 | tf_op jit(solution)/shard_map/ppermute | solution.py:253
  59.1 15.5 %all-to-all-start.2 = ((f32[128,2,256]{2,1,0:T(2,128)}), f32[128,2,256]{2,1,0:T(2,128)S(1)}, u32[]{:S(2)}, u32[]{:S(2)}) async-start(f32[128,2,256]{2,1,0:T(2,128)} %broadcast_in_dim.3), calls=%async_computation.2 | async-start | bytes 524288 | tf_op jit(solution)/shard_map/all_to_all | solution.py:256
  74.6 33.0 %all-to-all-start = ((f32[64,32,256]{2,1,0:T(8,128)}), f32[64,32,256]{2,1,0:T(8,128)S(1)}, u32[]{:S(2)}, u32[]{:S(2)}) async-start(f32[64,32,256]{2,1,0:T(8,128)} %add.3), calls=%async_computation | async-start | bytes 4194304 | tf_op jit(solution)/shard_map/all_to_all | solution.py:254

commit v2 on v0

v2 whole, which is shorter than its diff:
```python
import functools

import jax
import jax.numpy as jnp
from jax import lax
from jax.experimental import pallas as pl
from jax.experimental.pallas import tpu as pltpu
from jax.sharding import Mesh, PartitionSpec as P

K = 256
B = 8
HALF = K // 2
MIB = 1 << 20


def tree(terms):
    while len(terms) > 1:
        terms = [
            terms[i] + terms[i + 1] if i + 1 < len(terms) else terms[i]
            for i in range(0, len(terms), 2)
        ]
    return terms[0]


ROWS_STEP = 512
COLS_STEP = 1024
CHIPS_STEP = COLS_STEP // 64
PACKED = 3
OVER_ROWS = (((0,), (0,)), ((), ()))


def local_kernel(
    steps, place_ref, e_ref, t_ref, keep_0, keep_1, send_0, send_1, gram_keep_ref,
    gram_send_ref, held, s_ref, gram, parts, sem,
):
    i = pl.program_id(0)
    f32 = jnp.float32
    x, z, core = place_ref[1], place_ref[2], place_ref[3]
    last = steps - 1
    short = ROWS_STEP // 2

    def span(step, rows):
        start = jnp.where(step == 0, 0, step * ROWS_STEP - short)
        return pl.ds(pl.multiple_of(start, short), rows)

    def fetch(step, rows):
        r = span(step, rows)
        return pltpu.make_async_copy(e_ref.at[r], held.at[r], sem.at[step])

    def sketch(rows):
        fetch(i, rows).wait()

        @pl.when(i + 2 < last)
        def _():
            fetch(i + 2, ROWS_STEP).start()

        @pl.when(i + 2 == last)
        def _():
            fetch(i + 2, short).start()

        r = span(i, rows)
        s = jnp.dot(held[r, :], t_ref[...], preferred_element_type=f32)
        hi = s.astype(jnp.bfloat16)
        s_ref[r, 0:K] = hi
        s_ref[r, K : 2 * K] = (s - hi.astype(f32)).astype(jnp.bfloat16)

    @pl.when(i == 0)
    def _():
        fetch(0, short).start()
        fetch(1, ROWS_STEP).start()

    @pl.when((i == 0) | (i == last))
    def _():
        sketch(short)

    @pl.when((i > 0) & (i < last))
    def _():
        sketch(ROWS_STEP)

    @pl.when(i == steps)
    def _():
        g = lax.dot_general(s_ref[...], s_ref[...], OVER_ROWS, preferred_element_type=f32)
        gram[...] = (g[0:K, 0:K] + g[K:, K:]) + (g[0:K, K:] + g[K:, 0:K])

        def pack(out, c):
            diagonal = gram[c * HALF : (c + 1) * HALF, c * HALF : (c + 1) * HALF]
            below = gram[HALF + 64 * c : HALF + 64 * (c + 1), 0:HALF]
            out[:, :, 0:HALF] = diagonal[0:96].reshape(PACKED, 32, HALF)
            out[0, :, HALF:K] = diagonal[96:128]
            out[1:3, :, HALF:K] = below.reshape(2, 32, HALF)

        @pl.when(core == 0)
        def _():
            pack(gram_keep_ref, 0)
            pack(gram_send_ref, 1)

        @pl.when(core != 0)
        def _():
            pack(gram_keep_ref, 1)
            pack(gram_send_ref, 0)

    @pl.when(i >= steps)
    def _():
        c = pl.ds(pl.multiple_of((i - steps) * COLS_STEP, COLS_STEP), COLS_STEP)
        m = lax.dot_general(held[:, c], s_ref[...], OVER_ROWS, preferred_element_type=f32)
        parts[...] = (m[:, 0:K] + m[:, K : 2 * K]).reshape(CHIPS_STEP, 2, 32, K)
        for f, (keep_ref, send_ref) in enumerate(((keep_0, send_0), (keep_1, send_1))):
            for n in range(4):
                for g in range(2):
                    by_zero = 4 * flip(flip(x, f), 2 * g) + ((z + n) & 3)
                    by_one = 4 * flip(flip(x, 2 * f), g) + n
                    zero = core == 0
                    keep_ref[0, n, g] = parts[jnp.where(zero, by_zero, by_one), core]
                    send_ref[0, n, g] = parts[jnp.where(zero, by_one, by_zero), 1 - core]


def blocks(*lead):
    return jax.ShapeDtypeStruct(lead + (32, K), jnp.float32)


def local_products(place, e, t):
    rows, d = e.shape
    steps = rows // ROWS_STEP + 1

    def column(i):
        return jnp.maximum(i - steps, 0)

    def mine(i, p):
        return (jnp.where(p[3] == 0, column(i), (column(i) - p[0]) & 3), 0, 0, 0, 0)

    def theirs(i, p):
        return (jnp.where(p[3] != 0, column(i), (column(i) - p[0]) & 3), 0, 0, 0, 0)

    block = (1, 4, 2, 32, K)
    whole = pl.BlockSpec((PACKED, 32, K), lambda i, p: (0, 0, 0))
    return pl.pallas_call(
        functools.partial(local_kernel, steps),
        grid_spec=pltpu.PrefetchScalarGridSpec(
            num_scalar_prefetch=1,
            grid=(steps + d // COLS_STEP,),
            in_specs=[
                pl.BlockSpec(memory_space=pl.ANY),
                pl.BlockSpec((d, K), lambda i, p: (0, 0)),
            ],
            out_specs=[pl.BlockSpec(block, mine)] * 2
            + [pl.BlockSpec(block, theirs)] * 2
            + [whole] * 2,
            scratch_shapes=[
                pltpu.VMEM((rows, d), jnp.bfloat16),
                pltpu.VMEM((rows, 2 * K), jnp.bfloat16),
                pltpu.VMEM((K, K), jnp.float32),
                pltpu.VMEM((CHIPS_STEP, 2, 32, K), jnp.float32),
                pltpu.SemaphoreType.DMA((steps,)),
            ],
        ),
        out_shape=[blocks(4, 4, 2)] * 4 + [blocks(PACKED)] * 2,
        compiler_params=pltpu.CompilerParams(vmem_limit_bytes=46 * MIB),
        cost_estimate=pl.CostEstimate(
            flops=6 * rows * K * d + 8 * rows * K * K,
            bytes_accessed=rows * d * 2 + d * K * 6,
            transcendentals=0,
        ),
        name="local_products",
    )(place, e, t)


def one_step(kernel, name, out_shape):
    vmem = pl.BlockSpec(memory_space=pltpu.VMEM)

    def call(*args, scratch=()):
        return pl.pallas_call(
            kernel,
            out_shape=out_shape,
            in_specs=[vmem] * len(args),
            out_specs=[vmem] * len(out_shape),
            scratch_shapes=list(scratch),
            compiler_params=pltpu.CompilerParams(vmem_limit_bytes=20 * MIB),
            name=name,
        )(*args)

    return call


def piece_at(core, d, o):
    return jnp.where(core == 0, o, d), jnp.where(core == 0, d, o)


def message_kernel(d, keep_ref, got_ref, gk_ref, gg_ref, out_ref):
    for o in range(4):
        a, n = piece_at(lax.axis_index("core"), d, o)
        out_ref[2 * o : 2 * o + 2] = keep_ref[a, n] + got_ref[a, n]
    out_ref[8:] = gk_ref[...] + gg_ref[...]


def message(d, keep, got, gk, gg):
    kernel = functools.partial(message_kernel, d)
    return one_step(kernel, "message", [blocks(8 + PACKED)])(keep, got, gk, gg)[0]


def second_kernel(keep_ref, got_ref, gk_ref, gg_ref, *refs):
    arrived, own, out, m = refs[:7], refs[7], refs[8:15], refs[15]
    core = lax.axis_index("core")
    for o in range(4):
        a, n = piece_at(core, 0, o)
        m[o] = (keep_ref[a, n] + got_ref[a, n]) + tree(
            [r[2 * o : 2 * o + 2] for r in arrived]
        )
    gram = (gk_ref[...] + gg_ref[...]) + tree([r[8:] for r in arrived])
    at = jnp.where(core == 0, lax.axis_index("y"), lax.axis_index("z"))
    own[...] = m[at, 0]
    for ref, (e, g) in zip(out, MOVES):
        ref[0] = m[(at + e) & 3, g]
        ref[1:] = gram


def second(keep, got, gk, gg, arrived):
    outs = [blocks()] + [blocks(1 + PACKED)] * 7
    scratch = [pltpu.VMEM((4, 2, 32, K), jnp.float32)]
    return one_step(second_kernel, "second", outs)(
        keep, got, gk, gg, *arrived, scratch=scratch
    )


def last_kernel(own_ref, sent_ref, *refs):
    arrived, m_ref, g_ref = refs[:7], refs[7], refs[8]
    m_ref[...] = own_ref[...] + tree([r[0] for r in arrived])
    g_ref[...] = sent_ref[1:] + tree([r[1:] for r in arrived])


def last(own, sent, arrived):
    return one_step(last_kernel, "last", [blocks(), blocks(PACKED)])(own, sent, *arrived)


def small_inverse(d):
    n = len(d)
    d = [list(row) for row in d]
    l = [[None] * n for _ in range(n)]
    w = [[None] * n for _ in range(n)]
    for i in range(n):
        inv = lax.rsqrt(d[i][i])
        w[i][i] = inv
        for a in range(i + 1, n):
            l[a][i] = d[a][i] * inv
        for a in range(i + 1, n):
            for b in range(i + 1, a + 1):
                d[a][b] = d[a][b] - l[a][i] * l[b][i]
        for b in range(i):
            w[i][b] = -inv * tree([l[i][k] * w[k][b] for k in range(b, i)])
    return w


def chol_inverse(x):
    lane = lax.broadcasted_iota(jnp.int32, (B, HALF), 1)
    n = HALF // B

    def spread(j):
        o = j * B
        panel = x[o : o + B, :]
        cols = [
            jnp.broadcast_to(panel[:, o + b : o + b + 1], (B, HALF)) for b in range(B)
        ]
        return [
            [jnp.broadcast_to(cols[b][a : a + 1, :], (B, HALF)) for b in range(a + 1)]
            for a in range(B)
        ]

    w = small_inverse(spread(0))
    for j in range(n):
        o = j * B
        inside = (lane >= o) & (lane < o + B)
        rows = []
        for a in range(B):
            r = jnp.broadcast_to(x[o + a : o + a + 1, :], (B, HALF))
            rows.append(jnp.where(inside, jnp.where(lane == o + a, 1.0, 0.0), r))
        v = [tree([w[i][k] * rows[k] for k in range(i + 1)]) for i in range(B)]
        if j + 1 < n:
            y = [tree([w[i][k] * v[i] for i in range(k, B)]) for k in range(B)]
        for r in range(j + 1, n):
            sl = slice(r * B, (r + 1) * B)
            old = x[sl, :]
            c = [jnp.broadcast_to(old[:, o + k : o + k + 1], (B, HALF)) for k in range(B)]
            x[sl, :] = jnp.where(inside, 0.0, old) - tree([c[k] * y[k] for k in range(B)])
            if r == j + 1:
                w = small_inverse(spread(r))
        for i in range(B):
            x[o + i : o + i + 1, :] = jnp.where(lane < o + B, v[i], 0.0)[0:1, :]


def times_transposed(a, b):
    return lax.dot_general(
        a,
        b,
        (((1,), (1,)), ((), ())),
        precision=lax.Precision.HIGHEST,
        preferred_element_type=jnp.float32,
    )


def finish_kernel(m_ref, own_ref, other_ref, out_ref, a, b):
    core = lax.axis_index("core")
    zero = jnp.where(core == 0, own_ref[...], other_ref[...])
    one = jnp.where(core == 0, other_ref[...], own_ref[...])

    def unpack(packed):
        left = packed[:, :, 0:HALF].reshape(96, HALF)
        right = packed[:, :, HALF:K].reshape(96, HALF)
        return jnp.concatenate([left, right[0:32]], axis=0), right[32:96]

    a[...], upper = unpack(zero)
    corner, lower = unpack(one)
    below = jnp.concatenate([upper, lower], axis=0)
    chol_inverse(a)
    factor = times_transposed(below, a[...])
    b[...] = corner - times_transposed(factor, factor)
    first = times_transposed(m_ref[:, 0:HALF], a[...])
    rest = m_ref[:, HALF:K] - times_transposed(first, factor)
    chol_inverse(b)
    out_ref[:, 0:HALF] = first
    out_ref[:, HALF:K] = times_transposed(rest, b[...])


def finish(m, own, other):
    vmem = pl.BlockSpec(memory_space=pltpu.VMEM)
    return pl.pallas_call(
        finish_kernel,
        out_shape=blocks(),
        in_specs=[vmem] * 3,
        out_specs=vmem,
        scratch_shapes=[pltpu.VMEM((HALF, HALF), jnp.float32)] * 2,
        compiler_params=pltpu.CompilerParams(vmem_limit_bytes=32 * MIB),
        name="finish",
    )(m, own, other)


MOVES = [(2, 1), (1, 1), (3, 1), (0, 1), (2, 0), (1, 0), (3, 0)]


def flip(x, how):
    return x ^ (0, 1, 3)[how]


def step_pairs(step, move):
    d, f = move
    pairs = []
    for source in range(128):
        y, x, z, core = source // 32, source // 8 % 4, source // 2 % 4, source % 2
        if core == step:
            z = (z + d) % 4
            x = flip(x, f)
        else:
            y = (y + d) % 4
            x = flip(x, 2 * f)
        pairs.append((source, ((y * 4 + x) * 4 + z) * 2 + core))
    return pairs


def solution(mesh):
    every = ("y", "x", "z", "core")
    fine = Mesh(mesh.devices.reshape(4, 4, 4, 2), every)
    swap = [(0, 1), (1, 0)]

    def send_all(step, messages):
        return [
            lax.ppermute(m, every, step_pairs(step, move))
            for m, move in zip(messages, MOVES)
        ]

    def local(embedding, test_matrix):
        place = jnp.stack([lax.axis_index(a) for a in every]).astype(jnp.int32)
        *halves, gk, gs = local_products(place, embedding, test_matrix)
        keep, send = halves[:2], halves[2:]
        gg = lax.ppermute(gs, "core", swap)
        later, gg = lax.optimization_barrier((send[0], gg))
        got = [lax.ppermute(s, "core", swap) for s in (later, send[1])]
        messages = [message(d, keep[f], got[f], gk, gg) for d, f in MOVES]
        arrived = send_all(0, messages)
        own, *messages = second(keep[0], got[0], gk, gg, arrived)
        arrived = send_all(1, messages)
        m, g = last(own, messages[0], arrived)
        return finish(m, g, lax.ppermute(g, "core", swap))

    return jax.shard_map(
        local,
        mesh=fine,
        in_specs=(P(every, None), P()),
        out_specs=P(every, None),
        check_vma=False,
    )
```

time: 374 us -> 89.3 us (0.24)
  waiting for transfers between devices: 253 us -> 20.3 us
  other arithmetic: 54.7 us -> 0.08 us
  matrix products: 39.2 us -> 0 us
  Pallas kernels: 0 us -> 39 us
  starting transfers between devices: 0.3 us -> 28.1 us
  between operations: 14.4 us -> 0.09 us
  local copies, waits for them, and re-layouts: 9.82 us -> 1.59 us
    psum x2 -> x0, waiting for transfers between devices: 147 us -> none  [the longest x1 86 us: local(): partial_gram = lax.psum(local_gram, 'inner')]
    reduce_scatter x2 -> x0, waiting for transfers between devices: 106 us -> none  [the longest x1 76.9 us: local(): lax.psum_scatter(lax.dot_general(embedding, basis, (((0,), (0,)), ((), ()...]
    another operation x9 -> x1, other arithmetic: 53.7 us -> 0.08 us  [local(): place = jnp.stack([lax.axis_index(a) for a in every]).astype(jnp.int32)]
    pallas_call x0 -> x11, Pallas kernels: none -> 39 us  [the longest x1 27 us: local_products(): pl.pallas_call(functools.partial(local_kernel, steps), grid_spec=pltpu.Pr...]
    dot_general x3 -> x0, matrix products: 31.4 us -> none  [the longest x1 13.5 us: local(): lax.dot_general(embedding, basis, (((0,), (0,)), ((), ())), preferred_ele...]
    ppermute x0 -> x18, starting transfers between devices: none -> 28.1 us  [the longest x14 21.9 us: send_all(): lax.ppermute(m, every, step_pairs(step, move))]
    ppermute x0 -> x18, waiting for transfers between devices: none -> 20.3 us  [the longest x14 17 us: send_all(): lax.ppermute(m, every, step_pairs(step, move))]
    another operation x5 -> x0, matrix products: 7.75 us -> none  [the longest x3 7.28 us: local(): lax.linalg.triangular_solve(lower, sketch, left_side=False, lower=True, t...]
  transfers between devices with their start and end apart: 4 -> 18, of which waited for: 4 -> 10; matrix products, arithmetic and copies ran while one was open for 0% -> 0% of each run, Pallas kernels for 0% -> 0%
where the time goes in v2:
time: 89.3 us; the launch traced here: 89.1 us
  Pallas kernels  39 us (44%)
  starting transfers between devices  28.1 us (31%)
  waiting for transfers between devices  20.3 us (23%)
  local copies, waits for them, and re-layouts  1.59 us (2%)
    pallas_call x1, Pallas kernels, local_products(): pl.pallas_call(functools.partial(local_kernel, steps), grid_spec=pltpu.Pr...  27 us
    ppermute x14, starting transfers between devices, send_all(): lax.ppermute(m, every, step_pairs(step, move))  21.9 us
    ppermute x14, waiting for transfers between devices, send_all(): lax.ppermute(m, every, step_pairs(step, move))  17 us
    pallas_call x1, Pallas kernels, finish(): pl.pallas_call(finish_kernel, out_shape=blocks(), in_specs=[vmem] * 3, ou...  11.5 us
    ppermute x1, starting transfers between devices, local(): return finish(m, g, lax.ppermute(g, 'core', swap))  4.26 us
    ppermute x1, waiting for transfers between devices, local(): gg = lax.ppermute(gs, 'core', swap)  2.33 us
    ppermute x2, starting transfers between devices, local(): got = [lax.ppermute(s, 'core', swap) for s in (later, send[1])]  1.86 us
  transfers between devices with their start and end apart: 18, of which 10 were waited for; matrix products, arithmetic and copies ran while one was open for 0% of the time, Pallas kernels for 0%

profile of v2, /device:TPU:1, one launch (start us, length us, event | category | flops | bytes accessed | tf_op | source)
XLA Modules:
  0.0 89.1 jit_solution(8866032131625075735)
XLA Ops:
  0.0 0.1 pad_add_fusion.place_ref
  0.1 1.6 %copy-done = bf16[4096,256]{1,0:T(8,128)(2,1)S(1)} copy-done((bf16[4096,256]{1,0:T(8,128)(2,1)S(1)}, bf16[4096,256]{1,0:T(8,128)(2,1)}, u32[]{:S(2)}) %copy-start) | copy-done | bytes 2097176
  1.7 27.0 %local_products.1 = (f32[4,4,2,32,256]{4,3,2,1,0:T(8,128)S(1)}, f32[4,4,2,32,256]{4,3,2,1,0:T(8,128)S(1)}, f32[4,4,2,32,256]{4,3,2,1,0:T(8,128)S(1)}, f32[4,4,2,...) custom-call(s32[4]{0:T(128)S(1)} %pad_add_fusion.place_ref, ...), custom_call_target="tpu_custom_call" | custom-call | flops 20937965568 | bytes 31457280 | tf_op jit(solution)/shard_map/local_products/pallas_call | solution.py:136
  28.6 1.5 %collective-permute-start.2 = (f32[4,4,2,32,256]{4,3,2,1,0:T(8,128)S(1)}, f32[4,4,2,32,256]{4,3,2,1,0:T(8,128)S(1)}, u32[]{:S(2)}, u32[]{:S(2)}) collective-permute-start(f32[4,4,2,32,256]{4,3,2,1,0:T(8,128)S(1)} %get-tuple-element.30), channel_id=1, source_target_pairs={{0,1},{1,0},{2,3},{3,2},{4,5},{5,4},{6,7},{7,6},{8,9},{9,8},{10,11... | collective-permute-start | bytes 3145736 | tf_op jit(solution)/shard_map/ppermute | solution.py:374
  30.1 0.1 collective-permute-start
  30.2 2.3 %collective-permute-done.gg_ref = f32[3,32,256]{2,1,0:T(8,128)S(1)} collective-permute-done((f32[3,32,256]{2,1,0:T(8,128)S(1)}, f32[3,32,256]{2,1,0:T(8,128)S(1)}, u32[]{:S(2)}, u32[]{:S(2)}) %collective-permute-start) | collective-permute-done | bytes 98336 | tf_op jit(solution)/shard_map/ppermute | solution.py:372
  32.5 0.4 collective-permute-start.1
  33.0 5.3 %collective-permute-start.3 = (f32[11,32,256]{2,1,0:T(8,128)S(1)}, f32[11,32,256]{2,1,0:T(8,128)S(1)}, u32[]{:S(2)}, u32[]{:S(2)}) collective-permute-start(f32[11,32,256]{2,1,0:T(8,128)S(1)} %message.7), channel_id=1, source_target_pairs={{0,12},{1,89},{2,14},{3,91},{4,8},{5,93},{6,10},{7,95},{8,4},{9,81... | collective-permute-start | bytes 1081352 | tf_op jit(solution)/shard_map/ppermute | solution.py:364
  38.3 0.4 collective-permute-start.4
  38.7 4.5 %collective-permute-start.5 = (f32[11,32,256]{2,1,0:T(8,128)S(1)}, f32[11,32,256]{2,1,0:T(8,128)S(1)}, u32[]{:S(2)}, u32[]{:S(2)}) collective-permute-start(f32[11,32,256]{2,1,0:T(8,128)S(1)} %message.9), channel_id=1, source_target_pairs={{0,14},{1,121},{2,8},{3,123},{4,10},{5,125},{6,12},{7,127},{8,6},{... | collective-permute-start | bytes 1081352 | tf_op jit(solution)/shard_map/ppermute | solution.py:364
  43.3 0.3 collective-permute-start.6
  43.6 0.1 collective-permute-start.7
  43.8 0.7 collective-permute-start.8
  44.6 3.8 %collective-permute-done.4.refs_1_ = f32[11,32,256]{2,1,0:T(8,128)S(1)} collective-permute-done((f32[11,32,256]{2,1,0:T(8,128)S(1)}, f32[11,32,256]{2,1,0:T(8,128)S(1)}, u32[]{:S(2)}, u32[]{:S(2)}) %collective-permute-start.4) | collective-permute-done | bytes 360480 | tf_op jit(solution)/shard_map/ppermute | solution.py:364
  48.4 3.5 %collective-permute-done.5.refs_2_ = f32[11,32,256]{2,1,0:T(8,128)S(1)} collective-permute-done((f32[11,32,256]{2,1,0:T(8,128)S(1)}, f32[11,32,256]{2,1,0:T(8,128)S(1)}, u32[]{:S(2)}, u32[]{:S(2)}) %collective-permute-start.5) | collective-permute-done | bytes 360480 | tf_op jit(solution)/shard_map/ppermute | solution.py:364
  51.9 3.8 %collective-permute-done.6.refs_3_ = f32[11,32,256]{2,1,0:T(8,128)S(1)} collective-permute-done((f32[11,32,256]{2,1,0:T(8,128)S(1)}, f32[11,32,256]{2,1,0:T(8,128)S(1)}, u32[]{:S(2)}, u32[]{:S(2)}) %collective-permute-start.6) | collective-permute-done | bytes 360480 | tf_op jit(solution)/shard_map/ppermute | solution.py:364
  55.7 1.2 %collective-permute-done.9.refs_6_ = f32[11,32,256]{2,1,0:T(8,128)S(1)} collective-permute-done((f32[11,32,256]{2,1,0:T(8,128)S(1)}, f32[11,32,256]{2,1,0:T(8,128)S(1)}, u32[]{:S(2)}, u32[]{:S(2)}) %collective-permute-start.9) | collective-permute-done | bytes 360480 | tf_op jit(solution)/shard_map/ppermute | solution.py:364
  57.0 0.2 second.1
  57.2 2.5 %collective-permute-start.10 = (f32[4,32,256]{2,1,0:T(8,128)S(1)}, f32[4,32,256]{2,1,0:T(8,128)S(1)}, u32[]{:S(2)}, u32[]{:S(2)}) collective-permute-start(f32[4,32,256]{2,1,0:T(8,128)S(1)} %get-tuple-element.32.sent_ref), channel_id=1, source_target_pairs={{0,88},{1,13},{2,90},{3,15},{4,92},{5,9},{6,94},{7,11},{8,80},{9,5... | collective-permute-start | bytes 393224 | tf_op jit(solution)/shard_map/ppermute | solution.py:364
  59.7 2.8 %collective-permute-start.11 = (f32[4,32,256]{2,1,0:T(8,128)S(1)}, f32[4,32,256]{2,1,0:T(8,128)S(1)}, u32[]{:S(2)}, u32[]{:S(2)}) collective-permute-start(f32[4,32,256]{2,1,0:T(8,128)S(1)} %get-tuple-element.33), channel_id=1, source_target_pairs={{0,56},{1,11},{2,58},{3,13},{4,60},{5,15},{6,62},{7,9},{8,48},{9,3... | collective-permute-start | bytes 393224 | tf_op jit(solution)/shard_map/ppermute | solution.py:364
  62.5 0.8 collective-permute-start.12
  63.3 2.3 %collective-permute-start.13 = (f32[4,32,256]{2,1,0:T(8,128)S(1)}, f32[4,32,256]{2,1,0:T(8,128)S(1)}, u32[]{:S(2)}, u32[]{:S(2)}) collective-permute-start(f32[4,32,256]{2,1,0:T(8,128)S(1)} %get-tuple-element.35), channel_id=1, source_target_pairs={{0,24},{1,9},{2,26},{3,11},{4,28},{5,13},{6,30},{7,15},{8,16},{9,1... | collective-permute-start | bytes 393224 | tf_op jit(solution)/shard_map/ppermute | solution.py:364
  65.6 0.1 collective-permute-start.15
  65.7 0.5 collective-permute-done.11.refs_1_
  66.2 2.1 %collective-permute-start.16 = (f32[4,32,256]{2,1,0:T(8,128)S(1)}, f32[4,32,256]{2,1,0:T(8,128)S(1)}, u32[]{:S(2)}, u32[]{:S(2)}) collective-permute-start(f32[4,32,256]{2,1,0:T(8,128)S(1)} %get-tuple-element.38), channel_id=1, source_target_pairs={{0,96},{1,7},{2,98},{3,1},{4,100},{5,3},{6,102},{7,5},{8,104},{9,1... | collective-permute-start | bytes 393224 | tf_op jit(solution)/shard_map/ppermute | solution.py:364
  68.3 1.4 %collective-permute-done.13.refs_3_ = f32[4,32,256]{2,1,0:T(8,128)S(1)} collective-permute-done((f32[4,32,256]{2,1,0:T(8,128)S(1)}, f32[4,32,256]{2,1,0:T(8,128)S(1)}, u32[]{:S(2)}, u32[]{:S(2)}) %collective-permute-start.13) | collective-permute-done | bytes 131104 | tf_op jit(solution)/shard_map/ppermute | solution.py:364
  69.7 1.4 %collective-permute-done.14.refs_4_ = f32[4,32,256]{2,1,0:T(8,128)S(1)} collective-permute-done((f32[4,32,256]{2,1,0:T(8,128)S(1)}, f32[4,32,256]{2,1,0:T(8,128)S(1)}, u32[]{:S(2)}, u32[]{:S(2)}) %collective-permute-start.14) | collective-permute-done | bytes 131104 | tf_op jit(solution)/shard_map/ppermute | solution.py:364
  71.1 1.3 %collective-permute-done.15.refs_5_ = f32[4,32,256]{2,1,0:T(8,128)S(1)} collective-permute-done((f32[4,32,256]{2,1,0:T(8,128)S(1)}, f32[4,32,256]{2,1,0:T(8,128)S(1)}, u32[]{:S(2)}, u32[]{:S(2)}) %collective-permute-start.15) | collective-permute-done | bytes 131104 | tf_op jit(solution)/shard_map/ppermute | solution.py:364
  72.4 0.1 last.1
  72.4 4.3 %collective-permute-start.17 = (f32[3,32,256]{2,1,0:T(8,128)S(1)}, f32[3,32,256]{2,1,0:T(8,128)S(1)}, u32[]{:S(2)}, u32[]{:S(2)}) collective-permute-start(f32[3,32,256]{2,1,0:T(8,128)S(1)} %get-tuple-element.40.own_ref), channel_id=1, source_target_pairs={{0,1},{1,0},{2,3},{3,2},{4,5},{5,4},{6,7},{7,6},{8,9},{9,8},{10,11... | collective-permute-start | bytes 294920 | tf_op jit(solution)/shard_map/ppermute | solution.py:380
  76.7 0.9 %collective-permute-done.17.other_ref = f32[3,32,256]{2,1,0:T(8,128)S(1)} collective-permute-done((f32[3,32,256]{2,1,0:T(8,128)S(1)}, f32[3,32,256]{2,1,0:T(8,128)S(1)}, u32[]{:S(2)}, u32[]{:S(2)}) %collective-permute-start.17) | collective-permute-done | bytes 98336 | tf_op jit(solution)/shard_map/ppermute | solution.py:380
  77.6 11.5 %finish.1 = f32[32,256]{1,0:T(8,128)} custom-call(f32[32,256]{1,0:T(8,128)S(1)} %get-tuple-element.39.m_ref, f32[3,32,256]{2,1,0:T(8,128)S(1)} %get-tuple-element.40.own_ref, f32[3,32,256]{2,1,0:T(8,128)S(1)} %collective-permute-done.17.other_ref), custom_call_target="tpu_custom_call" | custom-call | tf_op jit(solution)/shard_map/finish/pallas_call | solution.py:324
  (18 shorter events, 0.3 us)
Async XLA Ops:
  0.1 1.6 %copy-start = (bf16[4096,256]{1,0:T(8,128)(2,1)S(1)}, bf16[4096,256]{1,0:T(8,128)(2,1)}, u32[]{:S(2)}) copy-start(bf16[4096,256]{1,0:T(8,128)(2,1)} %t_ref.1) | copy-start | bytes 6291460
  28.6 4.3 %collective-permute-start.2 = (f32[4,4,2,32,256]{4,3,2,1,0:T(8,128)S(1)}, f32[4,4,2,32,256]{4,3,2,1,0:T(8,128)S(1)}, u32[]{:S(2)}, u32[]{:S(2)}) collective-permute-start(f32[4,4,2,32,256]{4,3,2,1,0:T(8,128)S(1)} %get-tuple-element.30), channel_id=1, source_target_pairs={{0,1},{1,0},{2,3},{3,2},{4,5},{5,4},{6,7},{7,6},{8,9},{9,8},{10,11... | collective-permute-start | bytes 3145736 | tf_op jit(solution)/shard_map/ppermute | solution.py:374
  30.1 2.4 %collective-permute-start = (f32[3,32,256]{2,1,0:T(8,128)S(1)}, f32[3,32,256]{2,1,0:T(8,128)S(1)}, u32[]{:S(2)}, u32[]{:S(2)}) collective-permute-start(f32[3,32,256]{2,1,0:T(8,128)S(1)} %get-tuple-element.25), channel_id=1, source_target_pairs={{0,1},{1,0},{2,3},{3,2},{4,5},{5,4},{6,7},{7,6},{8,9},{9,8},{10,11... | collective-permute-start | bytes 294920 | tf_op jit(solution)/shard_map/ppermute | solution.py:372
  32.5 11.0 %collective-permute-start.1 = (f32[4,4,2,32,256]{4,3,2,1,0:T(8,128)S(1)}, f32[4,4,2,32,256]{4,3,2,1,0:T(8,128)S(1)}, u32[]{:S(2)}, u32[]{:S(2)}) collective-permute-start(f32[4,4,2,32,256]{4,3,2,1,0:T(8,128)S(1)} %get-tuple-element.26), channel_id=1, source_target_pairs={{0,1},{1,0},{2,3},{3,2},{4,5},{5,4},{6,7},{7,6},{8,9},{9,8},{10,11... | collective-permute-start | bytes 3145736 | tf_op jit(solution)/shard_map/ppermute | solution.py:374
  33.0 10.9 %collective-permute-start.3 = (f32[11,32,256]{2,1,0:T(8,128)S(1)}, f32[11,32,256]{2,1,0:T(8,128)S(1)}, u32[]{:S(2)}, u32[]{:S(2)}) collective-permute-start(f32[11,32,256]{2,1,0:T(8,128)S(1)} %message.7), channel_id=1, source_target_pairs={{0,12},{1,89},{2,14},{3,91},{4,8},{5,93},{6,10},{7,95},{8,4},{9,81... | collective-permute-start | bytes 1081352 | tf_op jit(solution)/shard_map/ppermute | solution.py:364
  38.3 10.1 %collective-permute-start.4 = (f32[11,32,256]{2,1,0:T(8,128)S(1)}, f32[11,32,256]{2,1,0:T(8,128)S(1)}, u32[]{:S(2)}, u32[]{:S(2)}) collective-permute-start(f32[11,32,256]{2,1,0:T(8,128)S(1)} %message.8), channel_id=1, source_target_pairs={{0,10},{1,57},{2,12},{3,59},{4,14},{5,61},{6,8},{7,63},{8,2},{9,49... | collective-permute-start | bytes 1081352 | tf_op jit(solution)/shard_map/ppermute | solution.py:364
  38.7 13.2 %collective-permute-start.5 = (f32[11,32,256]{2,1,0:T(8,128)S(1)}, f32[11,32,256]{2,1,0:T(8,128)S(1)}, u32[]{:S(2)}, u32[]{:S(2)}) collective-permute-start(f32[11,32,256]{2,1,0:T(8,128)S(1)} %message.9), channel_id=1, source_target_pairs={{0,14},{1,121},{2,8},{3,123},{4,10},{5,125},{6,12},{7,127},{8,6},{... | collective-permute-start | bytes 1081352 | tf_op jit(solution)/shard_map/ppermute | solution.py:364
  43.3 12.4 %collective-permute-start.6 = (f32[11,32,256]{2,1,0:T(8,128)S(1)}, f32[11,32,256]{2,1,0:T(8,128)S(1)}, u32[]{:S(2)}, u32[]{:S(2)}) collective-permute-start(f32[11,32,256]{2,1,0:T(8,128)S(1)} %message.10), channel_id=1, source_target_pairs={{0,8},{1,25},{2,10},{3,27},{4,12},{5,29},{6,14},{7,31},{8,0},{9,17... | collective-permute-start | bytes 1081352 | tf_op jit(solution)/shard_map/ppermute | solution.py:364
  43.6 12.1 %collective-permute-start.7 = (f32[11,32,256]{2,1,0:T(8,128)S(1)}, f32[11,32,256]{2,1,0:T(8,128)S(1)}, u32[]{:S(2)}, u32[]{:S(2)}) collective-permute-start(f32[11,32,256]{2,1,0:T(8,128)S(1)} %message.11), channel_id=1, source_target_pairs={{0,4},{1,65},{2,6},{3,67},{4,0},{5,69},{6,2},{7,71},{8,12},{9,73},... | collective-permute-start | bytes 1081352 | tf_op jit(solution)/shard_map/ppermute | solution.py:364
  43.8 11.9 %collective-permute-start.8 = (f32[11,32,256]{2,1,0:T(8,128)S(1)}, f32[11,32,256]{2,1,0:T(8,128)S(1)}, u32[]{:S(2)}, u32[]{:S(2)}) collective-permute-start(f32[11,32,256]{2,1,0:T(8,128)S(1)} %message.12), channel_id=1, source_target_pairs={{0,2},{1,33},{2,4},{3,35},{4,6},{5,37},{6,0},{7,39},{8,10},{9,41},... | collective-permute-start | bytes 1081352 | tf_op jit(solution)/shard_map/ppermute | solution.py:364
  48.4 8.6 %collective-permute-start.9 = (f32[11,32,256]{2,1,0:T(8,128)S(1)}, f32[11,32,256]{2,1,0:T(8,128)S(1)}, u32[]{:S(2)}, u32[]{:S(2)}) collective-permute-start(f32[11,32,256]{2,1,0:T(8,128)S(1)} %message.13), channel_id=1, source_target_pairs={{0,6},{1,97},{2,0},{3,99},{4,2},{5,101},{6,4},{7,103},{8,14},{9,10... | collective-permute-start | bytes 1081352 | tf_op jit(solution)/shard_map/ppermute | solution.py:364
  57.2 8.4 %collective-permute-start.10 = (f32[4,32,256]{2,1,0:T(8,128)S(1)}, f32[4,32,256]{2,1,0:T(8,128)S(1)}, u32[]{:S(2)}, u32[]{:S(2)}) collective-permute-start(f32[4,32,256]{2,1,0:T(8,128)S(1)} %get-tuple-element.32.sent_ref), channel_id=1, source_target_pairs={{0,88},{1,13},{2,90},{3,15},{4,92},{5,9},{6,94},{7,11},{8,80},{9,5... | collective-permute-start | bytes 393224 | tf_op jit(solution)/shard_map/ppermute | solution.py:364
  59.7 6.5 %collective-permute-start.11 = (f32[4,32,256]{2,1,0:T(8,128)S(1)}, f32[4,32,256]{2,1,0:T(8,128)S(1)}, u32[]{:S(2)}, u32[]{:S(2)}) collective-permute-start(f32[4,32,256]{2,1,0:T(8,128)S(1)} %get-tuple-element.33), channel_id=1, source_target_pairs={{0,56},{1,11},{2,58},{3,13},{4,60},{5,15},{6,62},{7,9},{8,48},{9,3... | collective-permute-start | bytes 393224 | tf_op jit(solution)/shard_map/ppermute | solution.py:364
  62.5 5.8 %collective-permute-start.12 = (f32[4,32,256]{2,1,0:T(8,128)S(1)}, f32[4,32,256]{2,1,0:T(8,128)S(1)}, u32[]{:S(2)}, u32[]{:S(2)}) collective-permute-start(f32[4,32,256]{2,1,0:T(8,128)S(1)} %get-tuple-element.34), channel_id=1, source_target_pairs={{0,120},{1,15},{2,122},{3,9},{4,124},{5,11},{6,126},{7,13},{8,112}... | collective-permute-start | bytes 393224 | tf_op jit(solution)/shard_map/ppermute | solution.py:364
  63.3 6.4 %collective-permute-start.13 = (f32[4,32,256]{2,1,0:T(8,128)S(1)}, f32[4,32,256]{2,1,0:T(8,128)S(1)}, u32[]{:S(2)}, u32[]{:S(2)}) collective-permute-start(f32[4,32,256]{2,1,0:T(8,128)S(1)} %get-tuple-element.35), channel_id=1, source_target_pairs={{0,24},{1,9},{2,26},{3,11},{4,28},{5,13},{6,30},{7,15},{8,16},{9,1... | collective-permute-start | bytes 393224 | tf_op jit(solution)/shard_map/ppermute | solution.py:364
  65.6 5.4 %collective-permute-start.14 = (f32[4,32,256]{2,1,0:T(8,128)S(1)}, f32[4,32,256]{2,1,0:T(8,128)S(1)}, u32[]{:S(2)}, u32[]{:S(2)}) collective-permute-start(f32[4,32,256]{2,1,0:T(8,128)S(1)} %get-tuple-element.36), channel_id=1, source_target_pairs={{0,64},{1,5},{2,66},{3,7},{4,68},{5,1},{6,70},{7,3},{8,72},{9,13},... | collective-permute-start | bytes 393224 | tf_op jit(solution)/shard_map/ppermute | solution.py:364
  65.6 6.7 %collective-permute-start.15 = (f32[4,32,256]{2,1,0:T(8,128)S(1)}, f32[4,32,256]{2,1,0:T(8,128)S(1)}, u32[]{:S(2)}, u32[]{:S(2)}) collective-permute-start(f32[4,32,256]{2,1,0:T(8,128)S(1)} %get-tuple-element.37), channel_id=1, source_target_pairs={{0,32},{1,3},{2,34},{3,5},{4,36},{5,7},{6,38},{7,1},{8,40},{9,11},... | collective-permute-start | bytes 393224 | tf_op jit(solution)/shard_map/ppermute | solution.py:364
  66.2 6.1 %collective-permute-start.16 = (f32[4,32,256]{2,1,0:T(8,128)S(1)}, f32[4,32,256]{2,1,0:T(8,128)S(1)}, u32[]{:S(2)}, u32[]{:S(2)}) collective-permute-start(f32[4,32,256]{2,1,0:T(8,128)S(1)} %get-tuple-element.38), channel_id=1, source_target_pairs={{0,96},{1,7},{2,98},{3,1},{4,100},{5,3},{6,102},{7,5},{8,104},{9,1... | collective-permute-start | bytes 393224 | tf_op jit(solution)/shard_map/ppermute | solution.py:364
  72.4 5.2 %collective-permute-start.17 = (f32[3,32,256]{2,1,0:T(8,128)S(1)}, f32[3,32,256]{2,1,0:T(8,128)S(1)}, u32[]{:S(2)}, u32[]{:S(2)}) collective-permute-start(f32[3,32,256]{2,1,0:T(8,128)S(1)} %get-tuple-element.40.own_ref), channel_id=1, source_target_pairs={{0,1},{1,0},{2,3},{3,2},{4,5},{5,4},{6,7},{7,6},{8,9},{9,8},{10,11... | collective-permute-start | bytes 294920 | tf_op jit(solution)/shard_map/ppermute | solution.py:380

commit v3 on v2

--- a/solution.py
+++ b/solution.py
@@ -22,7 +22,7 @@
     return terms[0]
 
 
-ROWS_STEP = 512
+ROWS_STEP = 768
 COLS_STEP = 1024
 CHIPS_STEP = COLS_STEP // 64
 PACKED = 3
@@ -31,56 +31,45 @@
 
 def local_kernel(
     steps, place_ref, e_ref, t_ref, keep_0, keep_1, send_0, send_1, gram_keep_ref,
-    gram_send_ref, held, s_ref, gram, parts, sem,
+    gram_send_ref, held, t_held, s_ref, gram, parts, sem, t_sem,
 ):
     i = pl.program_id(0)
     f32 = jnp.float32
     x, z, core = place_ref[1], place_ref[2], place_ref[3]
-    last = steps - 1
-    short = ROWS_STEP // 2
-
-    def span(step, rows):
-        start = jnp.where(step == 0, 0, step * ROWS_STEP - short)
-        return pl.ds(pl.multiple_of(start, short), rows)
-
-    def fetch(step, rows):
-        r = span(step, rows)
+
+    def fetch(step):
+        r = pl.ds(pl.multiple_of(step * ROWS_STEP, ROWS_STEP), ROWS_STEP)
         return pltpu.make_async_copy(e_ref.at[r], held.at[r], sem.at[step])
 
-    def sketch(rows):
-        fetch(i, rows).wait()
-
-        @pl.when(i + 2 < last)
+    @pl.when(i == 0)
+    def _():
+        table = pltpu.make_async_copy(t_ref, t_held, t_sem)
+        table.start()
+        fetch(0).start()
+        table.wait()
+        fetch(1).start()
+
+    @pl.when(i < steps)
+    def _():
+        fetch(i).wait()
+
+        @pl.when(i + 2 < steps)
         def _():
-            fetch(i + 2, ROWS_STEP).start()
-
-        @pl.when(i + 2 == last)
-        def _():
-            fetch(i + 2, short).start()
-
-        r = span(i, rows)
-        s = jnp.dot(held[r, :], t_ref[...], preferred_element_type=f32)
+            fetch(i + 2).start()
+
+        r = pl.ds(pl.multiple_of(i * ROWS_STEP, ROWS_STEP), ROWS_STEP)
+        s = jnp.dot(held[r, :], t_held[...], preferred_element_type=f32)
         hi = s.astype(jnp.bfloat16)
         s_ref[r, 0:K] = hi
         s_ref[r, K : 2 * K] = (s - hi.astype(f32)).astype(jnp.bfloat16)
 
-    @pl.when(i == 0)
-    def _():
-        fetch(0, short).start()
-        fetch(1, ROWS_STEP).start()
-
-    @pl.when((i == 0) | (i == last))
-    def _():
-        sketch(short)
-
-    @pl.when((i > 0) & (i < last))
-    def _():
-        sketch(ROWS_STEP)
-
     @pl.when(i == steps)
     def _():
-        g = lax.dot_general(s_ref[...], s_ref[...], OVER_ROWS, preferred_element_type=f32)
-        gram[...] = (g[0:K, 0:K] + g[K:, K:]) + (g[0:K, K:] + g[K:, 0:K])
+        g = lax.dot_general(
+            s_ref[:, 0:K], s_ref[...], OVER_ROWS, preferred_element_type=f32
+        )
+        mixed = g[:, K : 2 * K]
+        gram[...] = g[:, 0:K] + (mixed + mixed.T)
 
         def pack(out, c):
             diagonal = gram[c * HALF : (c + 1) * HALF, c * HALF : (c + 1) * HALF]
@@ -120,7 +109,7 @@
 
 def local_products(place, e, t):
     rows, d = e.shape
-    steps = rows // ROWS_STEP + 1
+    steps = rows // ROWS_STEP
 
     def column(i):
         return jnp.maximum(i - steps, 0)
@@ -140,17 +129,19 @@
             grid=(steps + d // COLS_STEP,),
             in_specs=[
                 pl.BlockSpec(memory_space=pl.ANY),
-                pl.BlockSpec((d, K), lambda i, p: (0, 0)),
+                pl.BlockSpec(memory_space=pl.ANY),
             ],
             out_specs=[pl.BlockSpec(block, mine)] * 2
             + [pl.BlockSpec(block, theirs)] * 2
             + [whole] * 2,
             scratch_shapes=[
                 pltpu.VMEM((rows, d), jnp.bfloat16),
+                pltpu.VMEM((d, K), jnp.bfloat16),
                 pltpu.VMEM((rows, 2 * K), jnp.bfloat16),
                 pltpu.VMEM((K, K), jnp.float32),
                 pltpu.VMEM((CHIPS_STEP, 2, 32, K), jnp.float32),
                 pltpu.SemaphoreType.DMA((steps,)),
+                pltpu.SemaphoreType.DMA,
             ],
         ),
         out_shape=[blocks(4, 4, 2)] * 4 + [blocks(PACKED)] * 2,
@@ -161,7 +152,7 @@
             transcendentals=0,
         ),
         name="local_products",
-    )(place, e, t)
+    )(place, e, pltpu.with_memory_space_constraint(t, pltpu.HBM))
 
 
 def one_step(kernel, name, out_shape):
@@ -198,33 +189,42 @@
 
 
 def second_kernel(keep_ref, got_ref, gk_ref, gg_ref, *refs):
-    arrived, own, out, m = refs[:7], refs[7], refs[8:15], refs[15]
-    core = lax.axis_index("core")
+    arrived, own, out = refs[:7], refs[7], refs[8]
     for o in range(4):
-        a, n = piece_at(core, 0, o)
-        m[o] = (keep_ref[a, n] + got_ref[a, n]) + tree(
+        a, n = piece_at(lax.axis_index("core"), 0, o)
+        m = (keep_ref[a, n] + got_ref[a, n]) + tree(
             [r[2 * o : 2 * o + 2] for r in arrived]
         )
-    gram = (gk_ref[...] + gg_ref[...]) + tree([r[8:] for r in arrived])
-    at = jnp.where(core == 0, lax.axis_index("y"), lax.axis_index("z"))
-    own[...] = m[at, 0]
-    for ref, (e, g) in zip(out, MOVES):
-        ref[0] = m[(at + e) & 3, g]
+        own[o] = m[0]
+        out[o] = m[1]
+    out[4:] = (gk_ref[...] + gg_ref[...]) + tree([r[8:] for r in arrived])
+
+
+def second(keep, got, gk, gg, arrived):
+    outs = [blocks(4), blocks(4 + PACKED)]
+    return one_step(second_kernel, "second", outs)(keep, got, gk, gg, *arrived)
+
+
+def third_kernel(own_ref, sent, got, own, *refs):
+    out, m = refs[:-1], refs[-1]
+    m[...] = own_ref[...] + got[0:4]
+    gram = sent[4:] + got[4:]
+    at = jnp.where(lax.axis_index("core") == 0, lax.axis_index("y"), lax.axis_index("z"))
+    own[...] = m[at]
+    for ref, d in zip(out, DISTANCES):
+        ref[0] = m[(at + d) & 3]
         ref[1:] = gram
 
 
-def second(keep, got, gk, gg, arrived):
-    outs = [blocks()] + [blocks(1 + PACKED)] * 7
-    scratch = [pltpu.VMEM((4, 2, 32, K), jnp.float32)]
-    return one_step(second_kernel, "second", outs)(
-        keep, got, gk, gg, *arrived, scratch=scratch
-    )
-
-
-def last_kernel(own_ref, sent_ref, *refs):
-    arrived, m_ref, g_ref = refs[:7], refs[7], refs[8]
-    m_ref[...] = own_ref[...] + tree([r[0] for r in arrived])
-    g_ref[...] = sent_ref[1:] + tree([r[1:] for r in arrived])
+def third(own, sent, got):
+    outs = [blocks()] + [blocks(1 + PACKED)] * 3
+    scratch = [pltpu.VMEM((4, 32, K), jnp.float32)]
+    return one_step(third_kernel, "third", outs)(own, sent, got, scratch=scratch)
+
+
+def last_kernel(own_ref, sent, a, b, c, m_ref, g_ref):
+    m_ref[...] = own_ref[...] + (a[0] + b[0] + c[0])
+    g_ref[...] = sent[1:] + (a[1:] + b[1:] + c[1:])
 
 
 def last(own, sent, arrived):
@@ -249,6 +249,10 @@
     return w
 
 
+def across(v, lane):
+    return jnp.take_along_axis(v, jnp.full(v.shape, lane, jnp.int32), axis=1)
+
+
 def chol_inverse(x):
     lane = lax.broadcasted_iota(jnp.int32, (B, HALF), 1)
     n = HALF // B
@@ -256,9 +260,7 @@
     def spread(j):
         o = j * B
         panel = x[o : o + B, :]
-        cols = [
-            jnp.broadcast_to(panel[:, o + b : o + b + 1], (B, HALF)) for b in range(B)
-        ]
+        cols = [across(panel, o + b) for b in range(B)]
         return [
             [jnp.broadcast_to(cols[b][a : a + 1, :], (B, HALF)) for b in range(a + 1)]
             for a in range(B)
@@ -278,7 +280,7 @@
         for r in range(j + 1, n):
             sl = slice(r * B, (r + 1) * B)
             old = x[sl, :]
-            c = [jnp.broadcast_to(old[:, o + k : o + k + 1], (B, HALF)) for k in range(B)]
+            c = [across(old, o + k) for k in range(B)]
             x[sl, :] = jnp.where(inside, 0.0, old) - tree([c[k] * y[k] for k in range(B)])
             if r == j + 1:
                 w = small_inverse(spread(r))
@@ -333,6 +335,7 @@
 
 
 MOVES = [(2, 1), (1, 1), (3, 1), (0, 1), (2, 0), (1, 0), (3, 0)]
+DISTANCES = (2, 1, 3)
 
 
 def flip(x, how):
@@ -359,23 +362,22 @@
     fine = Mesh(mesh.devices.reshape(4, 4, 4, 2), every)
     swap = [(0, 1), (1, 0)]
 
-    def send_all(step, messages):
-        return [
-            lax.ppermute(m, every, step_pairs(step, move))
-            for m, move in zip(messages, MOVES)
-        ]
+    def send(step, message, move):
+        return lax.ppermute(message, every, step_pairs(step, move))
 
     def local(embedding, test_matrix):
         place = jnp.stack([lax.axis_index(a) for a in every]).astype(jnp.int32)
         *halves, gk, gs = local_products(place, embedding, test_matrix)
-        keep, send = halves[:2], halves[2:]
+        keep, other = halves[:2], halves[2:]
         gg = lax.ppermute(gs, "core", swap)
-        later, gg = lax.optimization_barrier((send[0], gg))
-        got = [lax.ppermute(s, "core", swap) for s in (later, send[1])]
+        later, gg = lax.optimization_barrier((other[0], gg))
+        got = [lax.ppermute(s, "core", swap) for s in (later, other[1])]
         messages = [message(d, keep[f], got[f], gk, gg) for d, f in MOVES]
-        arrived = send_all(0, messages)
-        own, *messages = second(keep[0], got[0], gk, gg, arrived)
-        arrived = send_all(1, messages)
+        arrived = [send(0, m, move) for m, move in zip(messages, MOVES)]
+        own, message_2 = second(keep[0], got[0], gk, gg, arrived)
+        arrived = send(1, message_2, (0, 1))
+        own, *messages = third(own, message_2, arrived)
+        arrived = [send(1, m, (d, 0)) for m, d in zip(messages, DISTANCES)]
         m, g = last(own, messages[0], arrived)
         return finish(m, g, lax.ppermute(g, "core", swap))
 

time: 89.3 us -> 82.4 us (0.923)
  starting transfers between devices: 28.1 us -> 23 us
  Pallas kernels: 39 us -> 35.8 us
  waiting for transfers between devices: 20.3 us -> 23.2 us
  local copies, waits for them, and re-layouts: 1.59 us -> 0 us
    ppermute x16 -> x13, starting transfers between devices: 23.8 us -> 19.6 us  [the longest x11 17.7 us: send(): return lax.ppermute(message, every, step_pairs(step, move))]
    ppermute x16 -> x13, waiting for transfers between devices: 17 us -> 19.9 us  [the longest x11 19.9 us: send(): return lax.ppermute(message, every, step_pairs(step, move))]
    pallas_call x1, Pallas kernels: 11.5 us -> 8.59 us  [finish(): pl.pallas_call(finish_kernel, out_shape=blocks(), in_specs=[vmem] * 3, ou...]
    unnamed x2 -> x0, local copies, waits for them, and re-layouts: 1.59 us -> none
    ppermute x1, starting transfers between devices: 4.26 us -> 3.35 us  [local(): return finish(m, g, lax.ppermute(g, 'core', swap))]
  transfers between devices with their start and end apart: 18 -> 15, of which waited for: 10 -> 8; matrix products, arithmetic and copies ran while one was open for 0% -> 0% of each run, Pallas kernels for 0% -> 0%
where the time goes in v3:
time: 82.4 us; the launch traced here: 82.3 us
  Pallas kernels  35.8 us (43%)
  waiting for transfers between devices  23.2 us (28%)
  starting transfers between devices  23 us (28%)
    pallas_call x1, Pallas kernels, local_products(): pl.pallas_call(functools.partial(local_kernel, steps), grid_spec=pltpu.Pr...  26.8 us
    ppermute x11, waiting for transfers between devices, send(): return lax.ppermute(message, every, step_pairs(step, move))  19.9 us
    ppermute x11, starting transfers between devices, send(): return lax.ppermute(message, every, step_pairs(step, move))  17.7 us
    pallas_call x1, Pallas kernels, finish(): pl.pallas_call(finish_kernel, out_shape=blocks(), in_specs=[vmem] * 3, ou...  8.59 us
    ppermute x1, starting transfers between devices, local(): return finish(m, g, lax.ppermute(g, 'core', swap))  3.35 us
    ppermute x1, waiting for transfers between devices, local(): gg = lax.ppermute(gs, 'core', swap)  2.33 us
    ppermute x2, starting transfers between devices, local(): got = [lax.ppermute(s, 'core', swap) for s in (later, other[1])]  1.87 us
  transfers between devices with their start and end apart: 15, of which 8 were waited for; matrix products, arithmetic and copies ran while one was open for 0% of the time, Pallas kernels for 0%

profile of v3, /device:TPU:1, one launch (start us, length us, event | category | flops | bytes accessed | tf_op | source)
XLA Modules:
  0.0 82.3 jit_solution(17967761776196089165)
XLA Ops:
  0.0 0.1 pad_add_fusion.place_ref
  0.1 26.8 %local_products.1 = (f32[4,4,2,32,256]{4,3,2,1,0:T(8,128)S(1)}, f32[4,4,2,32,256]{4,3,2,1,0:T(8,128)S(1)}, f32[4,4,2,32,256]{4,3,2,1,0:T(8,128)S(1)}, f32[4,4,2,...) custom-call(s32[4]{0:T(128)S(1)} %pad_add_fusion.place_ref, ...), custom_call_target="tpu_custom_call" | custom-call | flops 20937965568 | bytes 31457280 | tf_op jit(solution)/shard_map/local_products/pallas_call | solution.py:125
  26.8 1.5 %collective-permute-start.2 = (f32[4,4,2,32,256]{4,3,2,1,0:T(8,128)S(1)}, f32[4,4,2,32,256]{4,3,2,1,0:T(8,128)S(1)}, u32[]{:S(2)}, u32[]{:S(2)}) collective-permute-start(f32[4,4,2,32,256]{4,3,2,1,0:T(8,128)S(1)} %get-tuple-element.28), channel_id=1, source_target_pairs={{0,1},{1,0},{2,3},{3,2},{4,5},{5,4},{6,7},{7,6},{8,9},{9,8},{10,11... | collective-permute-start | bytes 3145736 | tf_op jit(solution)/shard_map/ppermute | solution.py:374
  28.3 0.1 collective-permute-start
  28.4 2.3 %collective-permute-done.gg_ref = f32[3,32,256]{2,1,0:T(8,128)S(1)} collective-permute-done((f32[3,32,256]{2,1,0:T(8,128)S(1)}, f32[3,32,256]{2,1,0:T(8,128)S(1)}, u32[]{:S(2)}, u32[]{:S(2)}) %collective-permute-start) | collective-permute-done | bytes 98336 | tf_op jit(solution)/shard_map/ppermute | solution.py:372
  30.8 0.4 collective-permute-start.1
  31.1 0.0 collective-permute-done.2.got_ref
  31.2 5.3 %collective-permute-start.3 = (f32[11,32,256]{2,1,0:T(8,128)S(1)}, f32[11,32,256]{2,1,0:T(8,128)S(1)}, u32[]{:S(2)}, u32[]{:S(2)}) collective-permute-start(f32[11,32,256]{2,1,0:T(8,128)S(1)} %message.7), channel_id=1, source_target_pairs={{0,12},{1,89},{2,14},{3,91},{4,8},{5,93},{6,10},{7,95},{8,4},{9,81... | collective-permute-start | bytes 1081352 | tf_op jit(solution)/shard_map/ppermute | solution.py:366
  36.5 0.4 collective-permute-start.4
  36.9 4.5 %collective-permute-start.5 = (f32[11,32,256]{2,1,0:T(8,128)S(1)}, f32[11,32,256]{2,1,0:T(8,128)S(1)}, u32[]{:S(2)}, u32[]{:S(2)}) collective-permute-start(f32[11,32,256]{2,1,0:T(8,128)S(1)} %message.9), channel_id=1, source_target_pairs={{0,14},{1,121},{2,8},{3,123},{4,10},{5,125},{6,12},{7,127},{8,6},{... | collective-permute-start | bytes 1081352 | tf_op jit(solution)/shard_map/ppermute | solution.py:366
  41.5 0.3 collective-permute-start.6
  41.8 0.0 collective-permute-done.1.got_ref
  41.8 0.1 collective-permute-start.7
  42.0 0.0 collective-permute-done.3.refs_0_
  42.0 0.7 collective-permute-start.8
  42.8 3.8 %collective-permute-done.4.refs_1_ = f32[11,32,256]{2,1,0:T(8,128)S(1)} collective-permute-done((f32[11,32,256]{2,1,0:T(8,128)S(1)}, f32[11,32,256]{2,1,0:T(8,128)S(1)}, u32[]{:S(2)}, u32[]{:S(2)}) %collective-permute-start.4) | collective-permute-done | bytes 360480 | tf_op jit(solution)/shard_map/ppermute | solution.py:366
  46.6 0.0 collective-permute-start.9
  46.6 3.6 %collective-permute-done.5.refs_2_ = f32[11,32,256]{2,1,0:T(8,128)S(1)} collective-permute-done((f32[11,32,256]{2,1,0:T(8,128)S(1)}, f32[11,32,256]{2,1,0:T(8,128)S(1)}, u32[]{:S(2)}, u32[]{:S(2)}) %collective-permute-start.5) | collective-permute-done | bytes 360480 | tf_op jit(solution)/shard_map/ppermute | solution.py:366
  50.1 3.8 %collective-permute-done.6.refs_3_ = f32[11,32,256]{2,1,0:T(8,128)S(1)} collective-permute-done((f32[11,32,256]{2,1,0:T(8,128)S(1)}, f32[11,32,256]{2,1,0:T(8,128)S(1)}, u32[]{:S(2)}, u32[]{:S(2)}) %collective-permute-start.6) | collective-permute-done | bytes 360480 | tf_op jit(solution)/shard_map/ppermute | solution.py:366
  54.0 0.0 collective-permute-done.7.refs_4_
  54.0 1.2 %collective-permute-done.9.refs_6_ = f32[11,32,256]{2,1,0:T(8,128)S(1)} collective-permute-done((f32[11,32,256]{2,1,0:T(8,128)S(1)}, f32[11,32,256]{2,1,0:T(8,128)S(1)}, u32[]{:S(2)}, u32[]{:S(2)}) %collective-permute-start.9) | collective-permute-done | bytes 360480 | tf_op jit(solution)/shard_map/ppermute | solution.py:366
  55.2 0.1 second.1
  55.3 0.1 collective-permute-start.10
  55.4 5.2 %collective-permute-done.10.got = f32[7,32,256]{2,1,0:T(8,128)S(1)} collective-permute-done((f32[7,32,256]{2,1,0:T(8,128)S(1)}, f32[7,32,256]{2,1,0:T(8,128)S(1)}, u32[]{:S(2)}, u32[]{:S(2)}) %collective-permute-start.10) | collective-permute-done | bytes 229408 | tf_op jit(solution)/shard_map/ppermute | solution.py:366
  60.6 3.7 %collective-permute-start.11 = (f32[4,32,256]{2,1,0:T(8,128)S(1)}, f32[4,32,256]{2,1,0:T(8,128)S(1)}, u32[]{:S(2)}, u32[]{:S(2)}) collective-permute-start(f32[4,32,256]{2,1,0:T(8,128)S(1)} %get-tuple-element.32.sent), channel_id=1, source_target_pairs={{0,64},{1,5},{2,66},{3,7},{4,68},{5,1},{6,70},{7,3},{8,72},{9,13},... | collective-permute-start | bytes 393224 | tf_op jit(solution)/shard_map/ppermute | solution.py:366
  64.3 0.7 collective-permute-start.12
  65.0 1.9 %collective-permute-start.13 = (f32[4,32,256]{2,1,0:T(8,128)S(1)}, f32[4,32,256]{2,1,0:T(8,128)S(1)}, u32[]{:S(2)}, u32[]{:S(2)}) collective-permute-start(f32[4,32,256]{2,1,0:T(8,128)S(1)} %get-tuple-element.34), channel_id=1, source_target_pairs={{0,96},{1,7},{2,98},{3,1},{4,100},{5,3},{6,102},{7,5},{8,104},{9,1... | collective-permute-start | bytes 393224 | tf_op jit(solution)/shard_map/ppermute | solution.py:366
  67.0 0.0 collective-permute-done.11.a
  67.0 2.3 %collective-permute-done.12.b = f32[4,32,256]{2,1,0:T(8,128)S(1)} collective-permute-done((f32[4,32,256]{2,1,0:T(8,128)S(1)}, f32[4,32,256]{2,1,0:T(8,128)S(1)}, u32[]{:S(2)}, u32[]{:S(2)}) %collective-permute-start.12) | collective-permute-done | bytes 131104 | tf_op jit(solution)/shard_map/ppermute | solution.py:366
  69.4 3.4 %collective-permute-start.14 = (f32[3,32,256]{2,1,0:T(8,128)S(1)}, f32[3,32,256]{2,1,0:T(8,128)S(1)}, u32[]{:S(2)}, u32[]{:S(2)}) collective-permute-start(f32[3,32,256]{2,1,0:T(8,128)S(1)} %get-tuple-element.36.own_ref), channel_id=1, source_target_pairs={{0,1},{1,0},{2,3},{3,2},{4,5},{5,4},{6,7},{7,6},{8,9},{9,8},{10,11... | collective-permute-start | bytes 294920 | tf_op jit(solution)/shard_map/ppermute | solution.py:382
  72.7 0.9 %collective-permute-done.14.other_ref = f32[3,32,256]{2,1,0:T(8,128)S(1)} collective-permute-done((f32[3,32,256]{2,1,0:T(8,128)S(1)}, f32[3,32,256]{2,1,0:T(8,128)S(1)}, u32[]{:S(2)}, u32[]{:S(2)}) %collective-permute-start.14) | collective-permute-done | bytes 98336 | tf_op jit(solution)/shard_map/ppermute | solution.py:382
  73.7 8.6 %finish.1 = f32[32,256]{1,0:T(8,128)} custom-call(f32[32,256]{1,0:T(8,128)S(1)} %get-tuple-element.35.m_ref, f32[3,32,256]{2,1,0:T(8,128)S(1)} %get-tuple-element.36.own_ref, f32[3,32,256]{2,1,0:T(8,128)S(1)} %collective-permute-done.14.other_ref), custom_call_target="tpu_custom_call" | custom-call | tf_op jit(solution)/shard_map/finish/pallas_call | solution.py:326
  (11 shorter events, 0.4 us)
Async XLA Ops:
  26.8 4.3 %collective-permute-start.2 = (f32[4,4,2,32,256]{4,3,2,1,0:T(8,128)S(1)}, f32[4,4,2,32,256]{4,3,2,1,0:T(8,128)S(1)}, u32[]{:S(2)}, u32[]{:S(2)}) collective-permute-start(f32[4,4,2,32,256]{4,3,2,1,0:T(8,128)S(1)} %get-tuple-element.28), channel_id=1, source_target_pairs={{0,1},{1,0},{2,3},{3,2},{4,5},{5,4},{6,7},{7,6},{8,9},{9,8},{10,11... | collective-permute-start | bytes 3145736 | tf_op jit(solution)/shard_map/ppermute | solution.py:374
  28.3 2.4 %collective-permute-start = (f32[3,32,256]{2,1,0:T(8,128)S(1)}, f32[3,32,256]{2,1,0:T(8,128)S(1)}, u32[]{:S(2)}, u32[]{:S(2)}) collective-permute-start(f32[3,32,256]{2,1,0:T(8,128)S(1)} %get-tuple-element.23), channel_id=1, source_target_pairs={{0,1},{1,0},{2,3},{3,2},{4,5},{5,4},{6,7},{7,6},{8,9},{9,8},{10,11... | collective-permute-start | bytes 294920 | tf_op jit(solution)/shard_map/ppermute | solution.py:372
  30.8 11.0 %collective-permute-start.1 = (f32[4,4,2,32,256]{4,3,2,1,0:T(8,128)S(1)}, f32[4,4,2,32,256]{4,3,2,1,0:T(8,128)S(1)}, u32[]{:S(2)}, u32[]{:S(2)}) collective-permute-start(f32[4,4,2,32,256]{4,3,2,1,0:T(8,128)S(1)} %get-tuple-element.24), channel_id=1, source_target_pairs={{0,1},{1,0},{2,3},{3,2},{4,5},{5,4},{6,7},{7,6},{8,9},{9,8},{10,11... | collective-permute-start | bytes 3145736 | tf_op jit(solution)/shard_map/ppermute | solution.py:374
  31.2 10.8 %collective-permute-start.3 = (f32[11,32,256]{2,1,0:T(8,128)S(1)}, f32[11,32,256]{2,1,0:T(8,128)S(1)}, u32[]{:S(2)}, u32[]{:S(2)}) collective-permute-start(f32[11,32,256]{2,1,0:T(8,128)S(1)} %message.7), channel_id=1, source_target_pairs={{0,12},{1,89},{2,14},{3,91},{4,8},{5,93},{6,10},{7,95},{8,4},{9,81... | collective-permute-start | bytes 1081352 | tf_op jit(solution)/shard_map/ppermute | solution.py:366
  36.5 10.1 %collective-permute-start.4 = (f32[11,32,256]{2,1,0:T(8,128)S(1)}, f32[11,32,256]{2,1,0:T(8,128)S(1)}, u32[]{:S(2)}, u32[]{:S(2)}) collective-permute-start(f32[11,32,256]{2,1,0:T(8,128)S(1)} %message.8), channel_id=1, source_target_pairs={{0,10},{1,57},{2,12},{3,59},{4,14},{5,61},{6,8},{7,63},{8,2},{9,49... | collective-permute-start | bytes 1081352 | tf_op jit(solution)/shard_map/ppermute | solution.py:366
  36.9 13.2 %collective-permute-start.5 = (f32[11,32,256]{2,1,0:T(8,128)S(1)}, f32[11,32,256]{2,1,0:T(8,128)S(1)}, u32[]{:S(2)}, u32[]{:S(2)}) collective-permute-start(f32[11,32,256]{2,1,0:T(8,128)S(1)} %message.9), channel_id=1, source_target_pairs={{0,14},{1,121},{2,8},{3,123},{4,10},{5,125},{6,12},{7,127},{8,6},{... | collective-permute-start | bytes 1081352 | tf_op jit(solution)/shard_map/ppermute | solution.py:366
  41.5 12.5 %collective-permute-start.6 = (f32[11,32,256]{2,1,0:T(8,128)S(1)}, f32[11,32,256]{2,1,0:T(8,128)S(1)}, u32[]{:S(2)}, u32[]{:S(2)}) collective-permute-start(f32[11,32,256]{2,1,0:T(8,128)S(1)} %message.10), channel_id=1, source_target_pairs={{0,8},{1,25},{2,10},{3,27},{4,12},{5,29},{6,14},{7,31},{8,0},{9,17... | collective-permute-start | bytes 1081352 | tf_op jit(solution)/shard_map/ppermute | solution.py:366
  41.8 12.1 %collective-permute-start.7 = (f32[11,32,256]{2,1,0:T(8,128)S(1)}, f32[11,32,256]{2,1,0:T(8,128)S(1)}, u32[]{:S(2)}, u32[]{:S(2)}) collective-permute-start(f32[11,32,256]{2,1,0:T(8,128)S(1)} %message.11), channel_id=1, source_target_pairs={{0,4},{1,65},{2,6},{3,67},{4,0},{5,69},{6,2},{7,71},{8,12},{9,73},... | collective-permute-start | bytes 1081352 | tf_op jit(solution)/shard_map/ppermute | solution.py:366
  42.0 11.9 %collective-permute-start.8 = (f32[11,32,256]{2,1,0:T(8,128)S(1)}, f32[11,32,256]{2,1,0:T(8,128)S(1)}, u32[]{:S(2)}, u32[]{:S(2)}) collective-permute-start(f32[11,32,256]{2,1,0:T(8,128)S(1)} %message.12), channel_id=1, source_target_pairs={{0,2},{1,33},{2,4},{3,35},{4,6},{5,37},{6,0},{7,39},{8,10},{9,41},... | collective-permute-start | bytes 1081352 | tf_op jit(solution)/shard_map/ppermute | solution.py:366
  46.6 8.6 %collective-permute-start.9 = (f32[11,32,256]{2,1,0:T(8,128)S(1)}, f32[11,32,256]{2,1,0:T(8,128)S(1)}, u32[]{:S(2)}, u32[]{:S(2)}) collective-permute-start(f32[11,32,256]{2,1,0:T(8,128)S(1)} %message.13), channel_id=1, source_target_pairs={{0,6},{1,97},{2,0},{3,99},{4,2},{5,101},{6,4},{7,103},{8,14},{9,10... | collective-permute-start | bytes 1081352 | tf_op jit(solution)/shard_map/ppermute | solution.py:366
  55.3 5.2 %collective-permute-start.10 = (f32[7,32,256]{2,1,0:T(8,128)S(1)}, f32[7,32,256]{2,1,0:T(8,128)S(1)}, u32[]{:S(2)}, u32[]{:S(2)}) collective-permute-start(f32[7,32,256]{2,1,0:T(8,128)S(1)} %get-tuple-element.30.sent), channel_id=1, source_target_pairs={{0,24},{1,9},{2,26},{3,11},{4,28},{5,13},{6,30},{7,15},{8,16},{9,1... | collective-permute-start | bytes 688136 | tf_op jit(solution)/shard_map/ppermute | solution.py:366
  60.6 6.4 %collective-permute-start.11 = (f32[4,32,256]{2,1,0:T(8,128)S(1)}, f32[4,32,256]{2,1,0:T(8,128)S(1)}, u32[]{:S(2)}, u32[]{:S(2)}) collective-permute-start(f32[4,32,256]{2,1,0:T(8,128)S(1)} %get-tuple-element.32.sent), channel_id=1, source_target_pairs={{0,64},{1,5},{2,66},{3,7},{4,68},{5,1},{6,70},{7,3},{8,72},{9,13},... | collective-permute-start | bytes 393224 | tf_op jit(solution)/shard_map/ppermute | solution.py:366
  64.3 5.0 %collective-permute-start.12 = (f32[4,32,256]{2,1,0:T(8,128)S(1)}, f32[4,32,256]{2,1,0:T(8,128)S(1)}, u32[]{:S(2)}, u32[]{:S(2)}) collective-permute-start(f32[4,32,256]{2,1,0:T(8,128)S(1)} %get-tuple-element.33), channel_id=1, source_target_pairs={{0,32},{1,3},{2,34},{3,5},{4,36},{5,7},{6,38},{7,1},{8,40},{9,11},... | collective-permute-start | bytes 393224 | tf_op jit(solution)/shard_map/ppermute | solution.py:366
  65.0 4.3 %collective-permute-start.13 = (f32[4,32,256]{2,1,0:T(8,128)S(1)}, f32[4,32,256]{2,1,0:T(8,128)S(1)}, u32[]{:S(2)}, u32[]{:S(2)}) collective-permute-start(f32[4,32,256]{2,1,0:T(8,128)S(1)} %get-tuple-element.34), channel_id=1, source_target_pairs={{0,96},{1,7},{2,98},{3,1},{4,100},{5,3},{6,102},{7,5},{8,104},{9,1... | collective-permute-start | bytes 393224 | tf_op jit(solution)/shard_map/ppermute | solution.py:366
  69.4 4.3 %collective-permute-start.14 = (f32[3,32,256]{2,1,0:T(8,128)S(1)}, f32[3,32,256]{2,1,0:T(8,128)S(1)}, u32[]{:S(2)}, u32[]{:S(2)}) collective-permute-start(f32[3,32,256]{2,1,0:T(8,128)S(1)} %get-tuple-element.36.own_ref), channel_id=1, source_target_pairs={{0,1},{1,0},{2,3},{3,2},{4,5},{5,4},{6,7},{7,6},{8,9},{9,8},{10,11... | collective-permute-start | bytes 294920 | tf_op jit(solution)/shard_map/ppermute | solution.py:382

commit v4 on v3

v4 whole, which is shorter than its diff:
```python
import functools

import jax
import jax.numpy as jnp
from jax import lax
from jax.experimental import pallas as pl
from jax.experimental.pallas import tpu as pltpu
from jax.sharding import Mesh, PartitionSpec as P

K = 256
B = 8
HALF = K // 2
MIB = 1 << 20


def tree(terms):
    while len(terms) > 1:
        terms = [
            terms[i] + terms[i + 1] if i + 1 < len(terms) else terms[i]
            for i in range(0, len(terms), 2)
        ]
    return terms[0]


ROWS_STEP = 768
COLS_STEP = 1024
CHIPS_STEP = COLS_STEP // 64
PACKED = 3
OVER_ROWS = (((0,), (0,)), ((), ()))


def local_kernel(
    steps, place_ref, e_ref, t_ref, keep_ref, s0, s1, s2, s3, gram_keep_ref,
    gram_send_ref, held, t_held, s_ref, gram, parts, sem, t_sem,
):
    i = pl.program_id(0)
    f32 = jnp.float32
    x, z, core = place_ref[1], place_ref[2], place_ref[3]

    def fetch(step):
        r = pl.ds(pl.multiple_of(step * ROWS_STEP, ROWS_STEP), ROWS_STEP)
        return pltpu.make_async_copy(e_ref.at[r], held.at[r], sem.at[step])

    @pl.when(i == 0)
    def _():
        table = pltpu.make_async_copy(t_ref, t_held, t_sem)
        table.start()
        fetch(0).start()
        table.wait()
        fetch(1).start()

    @pl.when(i < steps)
    def _():
        fetch(i).wait()

        @pl.when(i + 2 < steps)
        def _():
            fetch(i + 2).start()

        r = pl.ds(pl.multiple_of(i * ROWS_STEP, ROWS_STEP), ROWS_STEP)
        s = jnp.dot(held[r, :], t_held[...], preferred_element_type=f32)
        hi = s.astype(jnp.bfloat16)
        s_ref[r, 0:K] = hi
        s_ref[r, K : 2 * K] = (s - hi.astype(f32)).astype(jnp.bfloat16)

    @pl.when(i == steps)
    def _():
        g = lax.dot_general(
            s_ref[:, 0:K], s_ref[...], OVER_ROWS, preferred_element_type=f32
        )
        mixed = g[:, K : 2 * K]
        gram[...] = g[:, 0:K] + (mixed + mixed.T)

        def pack(out, c):
            diagonal = gram[c * HALF : (c + 1) * HALF, c * HALF : (c + 1) * HALF]
            below = gram[HALF + 64 * c : HALF + 64 * (c + 1), 0:HALF]
            out[:, :, 0:HALF] = diagonal[0:96].reshape(PACKED, 32, HALF)
            out[0, :, HALF:K] = diagonal[96:128]
            out[1:3, :, HALF:K] = below.reshape(2, 32, HALF)

        @pl.when(core == 0)
        def _():
            pack(gram_keep_ref, 0)
            pack(gram_send_ref, 1)

        @pl.when(core != 0)
        def _():
            pack(gram_keep_ref, 1)
            pack(gram_send_ref, 0)

    @pl.when(i >= steps)
    def _():
        c = pl.ds(pl.multiple_of((i - steps) * COLS_STEP, COLS_STEP), COLS_STEP)
        m = lax.dot_general(held[:, c], s_ref[...], OVER_ROWS, preferred_element_type=f32)
        parts[...] = (m[:, 0:K] + m[:, K : 2 * K]).reshape(CHIPS_STEP, 2, 32, K)
        for k, send_ref in enumerate((s0, s1, s2, s3)):
            for o in range(4):
                by_z = 4 * o + ((z + k) & 3)
                by_x = 4 * ((x + k) & 3) + o
                keep_ref[k, 0, o] = parts[jnp.where(core == 0, by_z, by_x), core]
                send_ref[0, o] = parts[jnp.where(core == 0, by_x, by_z), 1 - core]


def blocks(*lead):
    return jax.ShapeDtypeStruct(lead + (32, K), jnp.float32)


def local_products(place, e, t):
    rows, d = e.shape
    steps = rows // ROWS_STEP

    def column(i):
        return jnp.maximum(i - steps, 0)

    kept = pl.BlockSpec((4, 1, 4, 32, K), lambda i: (0, column(i), 0, 0, 0))
    sent = pl.BlockSpec((1, 4, 32, K), lambda i: (column(i), 0, 0, 0))
    whole = pl.BlockSpec((PACKED, 32, K), lambda i: (0, 0, 0))
    return pl.pallas_call(
        functools.partial(local_kernel, steps),
        grid_spec=pl.GridSpec(
            grid=(steps + d // COLS_STEP,),
            in_specs=[
                pl.BlockSpec(memory_space=pltpu.SMEM),
                pl.BlockSpec(memory_space=pl.ANY),
                pl.BlockSpec(memory_space=pl.ANY),
            ],
            out_specs=[kept] + [sent] * 4 + [whole] * 2,
            scratch_shapes=[
                pltpu.VMEM((rows, d), jnp.bfloat16),
                pltpu.VMEM((d, K), jnp.bfloat16),
                pltpu.VMEM((rows, 2 * K), jnp.bfloat16),
                pltpu.VMEM((K, K), jnp.float32),
                pltpu.VMEM((CHIPS_STEP, 2, 32, K), jnp.float32),
                pltpu.SemaphoreType.DMA((steps,)),
                pltpu.SemaphoreType.DMA,
            ],
        ),
        out_shape=[blocks(4, 4, 4)] + [blocks(4, 4)] * 4 + [blocks(PACKED)] * 2,
        compiler_params=pltpu.CompilerParams(vmem_limit_bytes=46 * MIB),
        cost_estimate=pl.CostEstimate(
            flops=6 * rows * K * d + 8 * rows * K * K,
            bytes_accessed=rows * d * 2 + d * K * 6,
            transcendentals=0,
        ),
        name="local_products",
    )(place, e, pltpu.with_memory_space_constraint(t, pltpu.HBM))


def one_step(kernel, name, out_shape):
    vmem = pl.BlockSpec(memory_space=pltpu.VMEM)

    def call(*args, scratch=()):
        return pl.pallas_call(
            kernel,
            out_shape=out_shape,
            in_specs=[vmem] * len(args),
            out_specs=[vmem] * len(out_shape),
            scratch_shapes=list(scratch),
            compiler_params=pltpu.CompilerParams(vmem_limit_bytes=20 * MIB),
            name=name,
        )(*args)

    return call


def message_kernel(k, keep_ref, got_ref, gk_ref, gg_ref, out_ref):
    out_ref[0:16] = (keep_ref[k] + got_ref[...]).reshape(16, 32, K)
    out_ref[16:] = gk_ref[...] + gg_ref[...]


def message(k, keep, got, gk, gg):
    kernel = functools.partial(message_kernel, k)
    return one_step(kernel, "message", [blocks(16 + PACKED)])(keep, got, gk, gg)[0]


def second_kernel(keep_ref, got_ref, gk_ref, gg_ref, a, b, c, own, *refs):
    out, m = refs[:-1], refs[-1]
    core = lax.axis_index("core")
    y, z = lax.axis_index("y"), lax.axis_index("z")
    m[...] = (keep_ref[0] + got_ref[...]) + (a[0:16] + b[0:16] + c[0:16]).reshape(
        4, 4, 32, K
    )
    gram = (gk_ref[...] + gg_ref[...]) + (a[16:] + b[16:] + c[16:])
    for ref, k in zip((own,) + out, (0,) + DISTANCES):
        for i in range(4):
            first = jnp.where(core == 0, (y + k) & 3, i)
            other = jnp.where(core == 0, i, (z + k) & 3)
            ref[i] = m[first, other]
    for ref in out:
        ref[4:] = gram


def second(keep, got, gk, gg, arrived):
    outs = [blocks(4)] + [blocks(4 + PACKED)] * 3
    scratch = [pltpu.VMEM((4, 4, 32, K), jnp.float32)]
    return one_step(second_kernel, "second", outs)(
        keep, got, gk, gg, *arrived, scratch=scratch
    )


def third_kernel(own_ref, sent, a, b, c, own, *refs):
    out, m = refs[:-1], refs[-1]
    m[...] = own_ref[...] + (a[0:4] + b[0:4] + c[0:4])
    gram = sent[4:] + (a[4:] + b[4:] + c[4:])
    at = jnp.where(lax.axis_index("core") == 0, lax.axis_index("x"), lax.axis_index("y"))
    own[...] = m[at]
    for ref, k in zip(out, DISTANCES):
        ref[0] = m[(at + k) & 3]
        ref[1:] = gram


def third(own, sent, arrived):
    outs = [blocks()] + [blocks(1 + PACKED)] * 3
    scratch = [pltpu.VMEM((4, 32, K), jnp.float32)]
    return one_step(third_kernel, "third", outs)(own, sent, *arrived, scratch=scratch)


def last_kernel(own_ref, sent, a, b, c, m_ref, g_ref):
    m_ref[...] = own_ref[...] + (a[0] + b[0] + c[0])
    g_ref[...] = sent[1:] + (a[1:] + b[1:] + c[1:])


def last(own, sent, arrived):
    return one_step(last_kernel, "last", [blocks(), blocks(PACKED)])(own, sent, *arrived)


def across(v, lane):
    return jnp.take_along_axis(v, jnp.full(v.shape, lane, jnp.int32), axis=1)


def chol_inverse(x):
    lane = lax.broadcasted_iota(jnp.int32, (B, HALF), 1)
    n = HALF // B
    for j in range(n):
        o = j * B
        inside = (lane >= o) & (lane < o + B)
        panel = x[o : o + B, :]
        cols = [across(panel, o + b) for b in range(B)]
        d = [
            [jnp.broadcast_to(cols[b][a : a + 1, :], (B, HALF)) for b in range(a + 1)]
            for a in range(B)
        ]
        rows = []
        for a in range(B):
            r = jnp.broadcast_to(x[o + a : o + a + 1, :], (B, HALF))
            rows.append(jnp.where(inside, jnp.where(lane == o + a, 1.0, 0.0), r))
        more = j + 1 < n
        if more:
            old = x[o + B : o + 2 * B, :]
            c = [across(old, o + k) for k in range(B)]
            following = jnp.where(inside, 0.0, old)
        l = [[None] * B for _ in range(B)]
        scale, v = [], []
        for i in range(B):
            inv = lax.rsqrt(d[i][i])
            scale.append(inv)
            for a in range(i + 1, B):
                l[a][i] = d[a][i] * inv
            for a in range(i + 1, B):
                for b in range(i + 1, a + 1):
                    d[a][b] = d[a][b] - l[a][i] * l[b][i]
            v.append(rows[i] * inv)
            for a in range(i + 1, B):
                rows[a] = rows[a] - l[a][i] * v[i]
            if more:
                scaled = c[i] * inv
                for a in range(i + 1, B):
                    c[a] = c[a] - l[a][i] * scaled
                following = following - scaled * v[i]
        if more:
            x[o + B : o + 2 * B, :] = following
        if j + 2 < n:
            y = [None] * B
            for i in reversed(range(B)):
                t = v[i]
                for a in range(i + 1, B):
                    t = t - l[a][i] * y[a]
                y[i] = t * scale[i]
            for r in range(j + 2, n):
                sl = slice(r * B, (r + 1) * B)
                old = x[sl, :]
                c = [across(old, o + k) for k in range(B)]
                x[sl, :] = jnp.where(inside, 0.0, old) - tree([c[k] * y[k] for k in range(B)])
        for i in range(B):
            x[o + i : o + i + 1, :] = jnp.where(lane < o + B, v[i], 0.0)[0:1, :]


def times_transposed(a, b):
    return lax.dot_general(
        a,
        b,
        (((1,), (1,)), ((), ())),
        precision=lax.Precision.HIGHEST,
        preferred_element_type=jnp.float32,
    )


def finish_kernel(m_ref, own_ref, other_ref, out_ref, a, b):
    core = lax.axis_index("core")
    zero = jnp.where(core == 0, own_ref[...], other_ref[...])
    one = jnp.where(core == 0, other_ref[...], own_ref[...])

    def unpack(packed):
        left = packed[:, :, 0:HALF].reshape(96, HALF)
        right = packed[:, :, HALF:K].reshape(96, HALF)
        return jnp.concatenate([left, right[0:32]], axis=0), right[32:96]

    a[...], upper = unpack(zero)
    corner, lower = unpack(one)
    below = jnp.concatenate([upper, lower], axis=0)
    chol_inverse(a)
    factor = times_transposed(below, a[...])
    b[...] = corner - times_transposed(factor, factor)
    first = times_transposed(m_ref[:, 0:HALF], a[...])
    rest = m_ref[:, HALF:K] - times_transposed(first, factor)
    chol_inverse(b)
    out_ref[:, 0:HALF] = first
    out_ref[:, HALF:K] = times_transposed(rest, b[...])


def finish(m, own, other):
    vmem = pl.BlockSpec(memory_space=pltpu.VMEM)
    return pl.pallas_call(
        finish_kernel,
        out_shape=blocks(),
        in_specs=[vmem] * 3,
        out_specs=vmem,
        scratch_shapes=[pltpu.VMEM((HALF, HALF), jnp.float32)] * 2,
        compiler_params=pltpu.CompilerParams(vmem_limit_bytes=32 * MIB),
        name="finish",
    )(m, own, other)


DISTANCES = (2, 1, 3)


def ring_pairs(axes, distance):
    pairs = []
    for source in range(128):
        place = {"y": source // 32, "x": source // 8 % 4, "z": source // 2 % 4}
        core = source % 2
        place[axes[core]] = (place[axes[core]] + distance) % 4
        target = ((place["y"] * 4 + place["x"]) * 4 + place["z"]) * 2 + core
        pairs.append((source, target))
    return pairs


def solution(mesh):
    every = ("y", "x", "z", "core")
    fine = Mesh(mesh.devices.reshape(4, 4, 4, 2), every)
    swap = [(0, 1), (1, 0)]

    def along(axes, messages):
        return [
            lax.ppermute(m, every, ring_pairs(axes, k)) for m, k in zip(messages, DISTANCES)
        ]

    def local(embedding, test_matrix):
        place = jnp.stack([lax.axis_index(a) for a in every]).astype(jnp.int32)
        keep, *send, gk, gs = local_products(place, embedding, test_matrix)
        got = [None] * 4
        got[2] = lax.ppermute(send[2], "core", swap)
        gg = lax.ppermute(gs, "core", swap)
        send[1], send[3], send[0], gg = lax.optimization_barrier(
            (send[1], send[3], send[0], gg)
        )
        for k in (1, 3, 0):
            got[k] = lax.ppermute(send[k], "core", swap)
        messages = [message(k, keep, got[k], gk, gg) for k in DISTANCES]
        arrived = along(("z", "x"), messages)
        own, *messages = second(keep, got[0], gk, gg, arrived)
        arrived = along(("y", "z"), messages)
        own, *messages_3 = third(own, messages[0], arrived)
        arrived = along(("x", "y"), messages_3)
        m, g = last(own, messages_3[0], arrived)
        return finish(m, g, lax.ppermute(g, "core", swap))

    return jax.shard_map(
        local,
        mesh=fine,
        in_specs=(P(every, None), P()),
        out_specs=P(every, None),
        check_vma=False,
    )
```

time: 82.4 us -> 81.1 us (0.984)
  starting transfers between devices: 23 us -> 21.7 us
    ppermute x13, starting transfers between devices: 19.6 us -> 16.2 us  [the longest x9 13.8 us: along(): lax.ppermute(m, every, ring_pairs(axes, k))]
    ppermute x13, waiting for transfers between devices: 19.9 us -> 21.9 us  [the longest x9 19.9 us: along(): lax.ppermute(m, every, ring_pairs(axes, k))]
    ppermute x1, waiting for transfers between devices: 2.33 us -> 0.85 us  [local(): gg = lax.ppermute(gs, 'core', swap)]
    ppermute x1, starting transfers between devices: 0.09 us -> 1.49 us  [local(): gg = lax.ppermute(gs, 'core', swap)]
  transfers between devices with their start and end apart: 15 -> 15, of which waited for: 8 -> 11; matrix products, arithmetic and copies ran while one was open for 0% -> 0% of each run, Pallas kernels for 0% -> 0%
where the time goes in v4:
time: 81.1 us; the launch traced here: 81 us
  Pallas kernels  35.5 us (44%)
  waiting for transfers between devices  23.7 us (29%)
  starting transfers between devices  21.7 us (27%)
    pallas_call x1, Pallas kernels, local_products(): pl.pallas_call(functools.partial(local_kernel, steps), grid_spec=pl.GridS...  27 us
    ppermute x9, waiting for transfers between devices, along(): lax.ppermute(m, every, ring_pairs(axes, k))  19.9 us
    ppermute x9, starting transfers between devices, along(): lax.ppermute(m, every, ring_pairs(axes, k))  13.8 us
    pallas_call x1, Pallas kernels, finish(): pl.pallas_call(finish_kernel, out_shape=blocks(), in_specs=[vmem] * 3, ou...  7.93 us
    ppermute x1, starting transfers between devices, local(): return finish(m, g, lax.ppermute(g, 'core', swap))  3.93 us
    ppermute x3, starting transfers between devices, local(): got[k] = lax.ppermute(send[k], 'core', swap)  2.34 us
  transfers between devices with their start and end apart: 15, of which 11 were waited for; matrix products, arithmetic and copies ran while one was open for 0% of the time, Pallas kernels for 0%

profile of v4, /device:TPU:1, one launch (start us, length us, event | category | flops | bytes accessed | tf_op | source)
XLA Modules:
  0.0 81.0 jit_solution(4169950308847066193)
XLA Ops:
  0.0 0.1 pad_add_fusion.place_ref
  0.1 27.0 %local_products.1 = (f32[4,4,4,32,256]{4,3,2,1,0:T(8,128)S(1)}, f32[4,4,32,256]{3,2,1,0:T(8,128)S(1)}, f32[4,4,32,256]{3,2,1,0:T(8,128)S(1)}, f32[4,4,32,256]{3,...) custom-call(s32[4]{0:T(128)S(1)} %pad_add_fusion.place_ref, ...), custom_call_target="tpu_custom_call" | custom-call | flops 20937965568 | bytes 31457280 | tf_op jit(solution)/shard_map/local_products/pallas_call | solution.py:118
  27.1 1.5 %collective-permute-start = (f32[3,32,256]{2,1,0:T(8,128)S(1)}, f32[3,32,256]{2,1,0:T(8,128)S(1)}, u32[]{:S(2)}, u32[]{:S(2)}) collective-permute-start(f32[3,32,256]{2,1,0:T(8,128)S(1)} %get-tuple-element.30), channel_id=1, source_target_pairs={{0,1},{1,0},{2,3},{3,2},{4,5},{5,4},{6,7},{7,6},{8,9},{9,8},{10,11... | collective-permute-start | bytes 294920 | tf_op jit(solution)/shard_map/ppermute | solution.py:363
  28.6 0.1 collective-permute-start.2
  28.7 0.9 %collective-permute-done.gg_ref = f32[3,32,256]{2,1,0:T(8,128)S(1)} collective-permute-done((f32[3,32,256]{2,1,0:T(8,128)S(1)}, f32[3,32,256]{2,1,0:T(8,128)S(1)}, u32[]{:S(2)}, u32[]{:S(2)}) %collective-permute-start) | collective-permute-done | bytes 98336 | tf_op jit(solution)/shard_map/ppermute | solution.py:363
  29.5 0.4 collective-permute-start.6
  29.9 0.2 collective-permute-start.4
  30.0 0.5 collective-permute-done.2.got_ref
  30.5 0.1 message.3
  30.6 2.9 %collective-permute-start.3 = (f32[19,32,256]{2,1,0:T(8,128)S(1)}, f32[19,32,256]{2,1,0:T(8,128)S(1)}, u32[]{:S(2)}, u32[]{:S(2)}) collective-permute-start(f32[19,32,256]{2,1,0:T(8,128)S(1)} %message.3), channel_id=1, source_target_pairs={{0,4},{1,17},{2,6},{3,19},{4,0},{5,21},{6,2},{7,23},{8,12},{9,25},... | collective-permute-start | bytes 1867784 | tf_op jit(solution)/shard_map/ppermute | solution.py:355
  33.6 0.9 %collective-permute-start.7 = (f32[19,32,256]{2,1,0:T(8,128)S(1)}, f32[19,32,256]{2,1,0:T(8,128)S(1)}, u32[]{:S(2)}, u32[]{:S(2)}) collective-permute-start(f32[19,32,256]{2,1,0:T(8,128)S(1)} %message.5), channel_id=1, source_target_pairs={{0,6},{1,25},{2,0},{3,27},{4,2},{5,29},{6,4},{7,31},{8,14},{9,1},{... | collective-permute-start | bytes 1867784 | tf_op jit(solution)/shard_map/ppermute | solution.py:355
  34.6 0.7 collective-permute-start.5
  35.2 1.8 %collective-permute-start.1 = (f32[4,4,32,256]{3,2,1,0:T(8,128)S(1)}, f32[4,4,32,256]{3,2,1,0:T(8,128)S(1)}, u32[]{:S(2)}, u32[]{:S(2)}) collective-permute-start(f32[4,4,32,256]{3,2,1,0:T(8,128)S(1)} %get-tuple-element.31), channel_id=1, source_target_pairs={{0,1},{1,0},{2,3},{3,2},{4,5},{5,4},{6,7},{7,6},{8,9},{9,8},{10,11... | collective-permute-start | bytes 1572872 | tf_op jit(solution)/shard_map/ppermute | solution.py:368
  37.1 1.5 %collective-permute-done.1.got_ref = f32[4,4,32,256]{3,2,1,0:T(8,128)S(1)} collective-permute-done((f32[4,4,32,256]{3,2,1,0:T(8,128)S(1)}, f32[4,4,32,256]{3,2,1,0:T(8,128)S(1)}, u32[]{:S(2)}, u32[]{:S(2)}) %collective-permute-start.1) | collective-permute-done | bytes 524320 | tf_op jit(solution)/shard_map/ppermute | solution.py:368
  38.6 3.0 %collective-permute-done.3.a = f32[19,32,256]{2,1,0:T(8,128)S(1)} collective-permute-done((f32[19,32,256]{2,1,0:T(8,128)S(1)}, f32[19,32,256]{2,1,0:T(8,128)S(1)}, u32[]{:S(2)}, u32[]{:S(2)}) %collective-permute-start.3) | collective-permute-done | bytes 622624 | tf_op jit(solution)/shard_map/ppermute | solution.py:355
  41.6 6.8 %collective-permute-done.7.c = f32[19,32,256]{2,1,0:T(8,128)S(1)} collective-permute-done((f32[19,32,256]{2,1,0:T(8,128)S(1)}, f32[19,32,256]{2,1,0:T(8,128)S(1)}, u32[]{:S(2)}, u32[]{:S(2)}) %collective-permute-start.7) | collective-permute-done | bytes 622624 | tf_op jit(solution)/shard_map/ppermute | solution.py:355
  48.4 0.3 second.1
  48.7 1.7 %collective-permute-start.9 = (f32[7,32,256]{2,1,0:T(8,128)S(1)}, f32[7,32,256]{2,1,0:T(8,128)S(1)}, u32[]{:S(2)}, u32[]{:S(2)}) collective-permute-start(f32[7,32,256]{2,1,0:T(8,128)S(1)} %get-tuple-element.39), channel_id=1, source_target_pairs={{0,32},{1,3},{2,34},{3,5},{4,36},{5,7},{6,38},{7,1},{8,40},{9,11},... | collective-permute-start | bytes 688136 | tf_op jit(solution)/shard_map/ppermute | solution.py:355
  50.4 2.2 %collective-permute-start.10 = (f32[7,32,256]{2,1,0:T(8,128)S(1)}, f32[7,32,256]{2,1,0:T(8,128)S(1)}, u32[]{:S(2)}, u32[]{:S(2)}) collective-permute-start(f32[7,32,256]{2,1,0:T(8,128)S(1)} %get-tuple-element.40), channel_id=1, source_target_pairs={{0,96},{1,7},{2,98},{3,1},{4,100},{5,3},{6,102},{7,5},{8,104},{9,1... | collective-permute-start | bytes 688136 | tf_op jit(solution)/shard_map/ppermute | solution.py:355
  52.6 1.2 %collective-permute-start.8 = (f32[7,32,256]{2,1,0:T(8,128)S(1)}, f32[7,32,256]{2,1,0:T(8,128)S(1)}, u32[]{:S(2)}, u32[]{:S(2)}) collective-permute-start(f32[7,32,256]{2,1,0:T(8,128)S(1)} %get-tuple-element.38.sent), channel_id=1, source_target_pairs={{0,64},{1,5},{2,66},{3,7},{4,68},{5,1},{6,70},{7,3},{8,72},{9,13},... | collective-permute-start | bytes 688136 | tf_op jit(solution)/shard_map/ppermute | solution.py:355
  53.9 2.4 %collective-permute-done.9.b = f32[7,32,256]{2,1,0:T(8,128)S(1)} collective-permute-done((f32[7,32,256]{2,1,0:T(8,128)S(1)}, f32[7,32,256]{2,1,0:T(8,128)S(1)}, u32[]{:S(2)}, u32[]{:S(2)}) %collective-permute-start.9) | collective-permute-done | bytes 229408 | tf_op jit(solution)/shard_map/ppermute | solution.py:355
  56.3 1.8 %collective-permute-done.10.c = f32[7,32,256]{2,1,0:T(8,128)S(1)} collective-permute-done((f32[7,32,256]{2,1,0:T(8,128)S(1)}, f32[7,32,256]{2,1,0:T(8,128)S(1)}, u32[]{:S(2)}, u32[]{:S(2)}) %collective-permute-start.10) | collective-permute-done | bytes 229408 | tf_op jit(solution)/shard_map/ppermute | solution.py:355
  58.1 1.8 %collective-permute-done.8.a = f32[7,32,256]{2,1,0:T(8,128)S(1)} collective-permute-done((f32[7,32,256]{2,1,0:T(8,128)S(1)}, f32[7,32,256]{2,1,0:T(8,128)S(1)}, u32[]{:S(2)}, u32[]{:S(2)}) %collective-permute-start.8) | collective-permute-done | bytes 229408 | tf_op jit(solution)/shard_map/ppermute | solution.py:355
  59.9 0.1 third.1
  60.0 1.1 %collective-permute-start.12 = (f32[4,32,256]{2,1,0:T(8,128)S(1)}, f32[4,32,256]{2,1,0:T(8,128)S(1)}, u32[]{:S(2)}, u32[]{:S(2)}) collective-permute-start(f32[4,32,256]{2,1,0:T(8,128)S(1)} %get-tuple-element.43), channel_id=1, source_target_pairs={{0,8},{1,33},{2,10},{3,35},{4,12},{5,37},{6,14},{7,39},{8,16},{9,4... | collective-permute-start | bytes 393224 | tf_op jit(solution)/shard_map/ppermute | solution.py:355
  61.0 1.8 %collective-permute-start.13 = (f32[4,32,256]{2,1,0:T(8,128)S(1)}, f32[4,32,256]{2,1,0:T(8,128)S(1)}, u32[]{:S(2)}, u32[]{:S(2)}) collective-permute-start(f32[4,32,256]{2,1,0:T(8,128)S(1)} %get-tuple-element.44), channel_id=1, source_target_pairs={{0,24},{1,97},{2,26},{3,99},{4,28},{5,101},{6,30},{7,103},{8,0},{9... | collective-permute-start | bytes 393224 | tf_op jit(solution)/shard_map/ppermute | solution.py:355
  62.8 1.3 %collective-permute-start.11 = (f32[4,32,256]{2,1,0:T(8,128)S(1)}, f32[4,32,256]{2,1,0:T(8,128)S(1)}, u32[]{:S(2)}, u32[]{:S(2)}) collective-permute-start(f32[4,32,256]{2,1,0:T(8,128)S(1)} %get-tuple-element.42.sent), channel_id=1, source_target_pairs={{0,16},{1,65},{2,18},{3,67},{4,20},{5,69},{6,22},{7,71},{8,24},{9,... | collective-permute-start | bytes 393224 | tf_op jit(solution)/shard_map/ppermute | solution.py:355
  64.1 1.0 %collective-permute-done.12.b = f32[4,32,256]{2,1,0:T(8,128)S(1)} collective-permute-done((f32[4,32,256]{2,1,0:T(8,128)S(1)}, f32[4,32,256]{2,1,0:T(8,128)S(1)}, u32[]{:S(2)}, u32[]{:S(2)}) %collective-permute-start.12) | collective-permute-done | bytes 131104 | tf_op jit(solution)/shard_map/ppermute | solution.py:355
  65.1 3.0 %collective-permute-done.11.a = f32[4,32,256]{2,1,0:T(8,128)S(1)} collective-permute-done((f32[4,32,256]{2,1,0:T(8,128)S(1)}, f32[4,32,256]{2,1,0:T(8,128)S(1)}, u32[]{:S(2)}, u32[]{:S(2)}) %collective-permute-start.11) | collective-permute-done | bytes 131104 | tf_op jit(solution)/shard_map/ppermute | solution.py:355
  68.2 3.9 %collective-permute-start.14 = (f32[3,32,256]{2,1,0:T(8,128)S(1)}, f32[3,32,256]{2,1,0:T(8,128)S(1)}, u32[]{:S(2)}, u32[]{:S(2)}) collective-permute-start(f32[3,32,256]{2,1,0:T(8,128)S(1)} %get-tuple-element.46.own_ref), channel_id=1, source_target_pairs={{0,1},{1,0},{2,3},{3,2},{4,5},{5,4},{6,7},{7,6},{8,9},{9,8},{10,11... | collective-permute-start | bytes 294920 | tf_op jit(solution)/shard_map/ppermute | solution.py:376
  72.1 0.9 %collective-permute-done.14.other_ref = f32[3,32,256]{2,1,0:T(8,128)S(1)} collective-permute-done((f32[3,32,256]{2,1,0:T(8,128)S(1)}, f32[3,32,256]{2,1,0:T(8,128)S(1)}, u32[]{:S(2)}, u32[]{:S(2)}) %collective-permute-start.14) | collective-permute-done | bytes 98336 | tf_op jit(solution)/shard_map/ppermute | solution.py:376
  73.1 7.9 %finish.1 = f32[32,256]{1,0:T(8,128)} custom-call(f32[32,256]{1,0:T(8,128)S(1)} %get-tuple-element.45.m_ref, f32[3,32,256]{2,1,0:T(8,128)S(1)} %get-tuple-element.46.own_ref, f32[3,32,256]{2,1,0:T(8,128)S(1)} %collective-permute-done.14.other_ref), custom_call_target="tpu_custom_call" | custom-call | tf_op jit(solution)/shard_map/finish/pallas_call | solution.py:323
  (7 shorter events, 0.2 us)
Async XLA Ops:
  27.1 2.4 %collective-permute-start = (f32[3,32,256]{2,1,0:T(8,128)S(1)}, f32[3,32,256]{2,1,0:T(8,128)S(1)}, u32[]{:S(2)}, u32[]{:S(2)}) collective-permute-start(f32[3,32,256]{2,1,0:T(8,128)S(1)} %get-tuple-element.30), channel_id=1, source_target_pairs={{0,1},{1,0},{2,3},{3,2},{4,5},{5,4},{6,7},{7,6},{8,9},{9,8},{10,11... | collective-permute-start | bytes 294920 | tf_op jit(solution)/shard_map/ppermute | solution.py:363
  28.6 1.9 %collective-permute-start.2 = (f32[4,4,32,256]{3,2,1,0:T(8,128)S(1)}, f32[4,4,32,256]{3,2,1,0:T(8,128)S(1)}, u32[]{:S(2)}, u32[]{:S(2)}) collective-permute-start(f32[4,4,32,256]{3,2,1,0:T(8,128)S(1)} %get-tuple-element.34), channel_id=1, source_target_pairs={{0,1},{1,0},{2,3},{3,2},{4,5},{5,4},{6,7},{7,6},{8,9},{9,8},{10,11... | collective-permute-start | bytes 1572872 | tf_op jit(solution)/shard_map/ppermute | solution.py:362
  29.5 4.0 %collective-permute-start.6 = (f32[4,4,32,256]{3,2,1,0:T(8,128)S(1)}, f32[4,4,32,256]{3,2,1,0:T(8,128)S(1)}, u32[]{:S(2)}, u32[]{:S(2)}) collective-permute-start(f32[4,4,32,256]{3,2,1,0:T(8,128)S(1)} %get-tuple-element.36), channel_id=1, source_target_pairs={{0,1},{1,0},{2,3},{3,2},{4,5},{5,4},{6,7},{7,6},{8,9},{9,8},{10,11... | collective-permute-start | bytes 1572872 | tf_op jit(solution)/shard_map/ppermute | solution.py:368
  29.9 4.6 %collective-permute-start.4 = (f32[4,4,32,256]{3,2,1,0:T(8,128)S(1)}, f32[4,4,32,256]{3,2,1,0:T(8,128)S(1)}, u32[]{:S(2)}, u32[]{:S(2)}) collective-permute-start(f32[4,4,32,256]{3,2,1,0:T(8,128)S(1)} %get-tuple-element.35), channel_id=1, source_target_pairs={{0,1},{1,0},{2,3},{3,2},{4,5},{5,4},{6,7},{7,6},{8,9},{9,8},{10,11... | collective-permute-start | bytes 1572872 | tf_op jit(solution)/shard_map/ppermute | solution.py:368
  30.6 11.0 %collective-permute-start.3 = (f32[19,32,256]{2,1,0:T(8,128)S(1)}, f32[19,32,256]{2,1,0:T(8,128)S(1)}, u32[]{:S(2)}, u32[]{:S(2)}) collective-permute-start(f32[19,32,256]{2,1,0:T(8,128)S(1)} %message.3), channel_id=1, source_target_pairs={{0,4},{1,17},{2,6},{3,19},{4,0},{5,21},{6,2},{7,23},{8,12},{9,25},... | collective-permute-start | bytes 1867784 | tf_op jit(solution)/shard_map/ppermute | solution.py:355
  33.6 14.9 %collective-permute-start.7 = (f32[19,32,256]{2,1,0:T(8,128)S(1)}, f32[19,32,256]{2,1,0:T(8,128)S(1)}, u32[]{:S(2)}, u32[]{:S(2)}) collective-permute-start(f32[19,32,256]{2,1,0:T(8,128)S(1)} %message.5), channel_id=1, source_target_pairs={{0,6},{1,25},{2,0},{3,27},{4,2},{5,29},{6,4},{7,31},{8,14},{9,1},{... | collective-permute-start | bytes 1867784 | tf_op jit(solution)/shard_map/ppermute | solution.py:355
  34.6 13.9 %collective-permute-start.5 = (f32[19,32,256]{2,1,0:T(8,128)S(1)}, f32[19,32,256]{2,1,0:T(8,128)S(1)}, u32[]{:S(2)}, u32[]{:S(2)}) collective-permute-start(f32[19,32,256]{2,1,0:T(8,128)S(1)} %message.4), channel_id=1, source_target_pairs={{0,2},{1,9},{2,4},{3,11},{4,6},{5,13},{6,0},{7,15},{8,10},{9,17},{... | collective-permute-start | bytes 1867784 | tf_op jit(solution)/shard_map/ppermute | solution.py:355
  35.2 3.4 %collective-permute-start.1 = (f32[4,4,32,256]{3,2,1,0:T(8,128)S(1)}, f32[4,4,32,256]{3,2,1,0:T(8,128)S(1)}, u32[]{:S(2)}, u32[]{:S(2)}) collective-permute-start(f32[4,4,32,256]{3,2,1,0:T(8,128)S(1)} %get-tuple-element.31), channel_id=1, source_target_pairs={{0,1},{1,0},{2,3},{3,2},{4,5},{5,4},{6,7},{7,6},{8,9},{9,8},{10,11... | collective-permute-start | bytes 1572872 | tf_op jit(solution)/shard_map/ppermute | solution.py:368
  48.7 7.5 %collective-permute-start.9 = (f32[7,32,256]{2,1,0:T(8,128)S(1)}, f32[7,32,256]{2,1,0:T(8,128)S(1)}, u32[]{:S(2)}, u32[]{:S(2)}) collective-permute-start(f32[7,32,256]{2,1,0:T(8,128)S(1)} %get-tuple-element.39), channel_id=1, source_target_pairs={{0,32},{1,3},{2,34},{3,5},{4,36},{5,7},{6,38},{7,1},{8,40},{9,11},... | collective-permute-start | bytes 688136 | tf_op jit(solution)/shard_map/ppermute | solution.py:355
  50.4 7.6 %collective-permute-start.10 = (f32[7,32,256]{2,1,0:T(8,128)S(1)}, f32[7,32,256]{2,1,0:T(8,128)S(1)}, u32[]{:S(2)}, u32[]{:S(2)}) collective-permute-start(f32[7,32,256]{2,1,0:T(8,128)S(1)} %get-tuple-element.40), channel_id=1, source_target_pairs={{0,96},{1,7},{2,98},{3,1},{4,100},{5,3},{6,102},{7,5},{8,104},{9,1... | collective-permute-start | bytes 688136 | tf_op jit(solution)/shard_map/ppermute | solution.py:355
  52.6 7.3 %collective-permute-start.8 = (f32[7,32,256]{2,1,0:T(8,128)S(1)}, f32[7,32,256]{2,1,0:T(8,128)S(1)}, u32[]{:S(2)}, u32[]{:S(2)}) collective-permute-start(f32[7,32,256]{2,1,0:T(8,128)S(1)} %get-tuple-element.38.sent), channel_id=1, source_target_pairs={{0,64},{1,5},{2,66},{3,7},{4,68},{5,1},{6,70},{7,3},{8,72},{9,13},... | collective-permute-start | bytes 688136 | tf_op jit(solution)/shard_map/ppermute | solution.py:355
  60.0 5.2 %collective-permute-start.12 = (f32[4,32,256]{2,1,0:T(8,128)S(1)}, f32[4,32,256]{2,1,0:T(8,128)S(1)}, u32[]{:S(2)}, u32[]{:S(2)}) collective-permute-start(f32[4,32,256]{2,1,0:T(8,128)S(1)} %get-tuple-element.43), channel_id=1, source_target_pairs={{0,8},{1,33},{2,10},{3,35},{4,12},{5,37},{6,14},{7,39},{8,16},{9,4... | collective-permute-start | bytes 393224 | tf_op jit(solution)/shard_map/ppermute | solution.py:355
  61.0 4.1 %collective-permute-start.13 = (f32[4,32,256]{2,1,0:T(8,128)S(1)}, f32[4,32,256]{2,1,0:T(8,128)S(1)}, u32[]{:S(2)}, u32[]{:S(2)}) collective-permute-start(f32[4,32,256]{2,1,0:T(8,128)S(1)} %get-tuple-element.44), channel_id=1, source_target_pairs={{0,24},{1,97},{2,26},{3,99},{4,28},{5,101},{6,30},{7,103},{8,0},{9... | collective-permute-start | bytes 393224 | tf_op jit(solution)/shard_map/ppermute | solution.py:355
  62.8 5.3 %collective-permute-start.11 = (f32[4,32,256]{2,1,0:T(8,128)S(1)}, f32[4,32,256]{2,1,0:T(8,128)S(1)}, u32[]{:S(2)}, u32[]{:S(2)}) collective-permute-start(f32[4,32,256]{2,1,0:T(8,128)S(1)} %get-tuple-element.42.sent), channel_id=1, source_target_pairs={{0,16},{1,65},{2,18},{3,67},{4,20},{5,69},{6,22},{7,71},{8,24},{9,... | collective-permute-start | bytes 393224 | tf_op jit(solution)/shard_map/ppermute | solution.py:355
  68.2 4.9 %collective-permute-start.14 = (f32[3,32,256]{2,1,0:T(8,128)S(1)}, f32[3,32,256]{2,1,0:T(8,128)S(1)}, u32[]{:S(2)}, u32[]{:S(2)}) collective-permute-start(f32[3,32,256]{2,1,0:T(8,128)S(1)} %get-tuple-element.46.own_ref), channel_id=1, source_target_pairs={{0,1},{1,0},{2,3},{3,2},{4,5},{5,4},{6,7},{7,6},{8,9},{9,8},{10,11... | collective-permute-start | bytes 294920 | tf_op jit(solution)/shard_map/ppermute | solution.py:376

commit v5 on v4

--- a/solution.py
+++ b/solution.py
@@ -25,7 +25,7 @@
 ROWS_STEP = 768
 COLS_STEP = 1024
 CHIPS_STEP = COLS_STEP // 64
-PACKED = 3
+PACKED = 80
 OVER_ROWS = (((0,), (0,)), ((), ()))
 
 
@@ -72,11 +72,14 @@
         gram[...] = g[:, 0:K] + (mixed + mixed.T)
 
         def pack(out, c):
-            diagonal = gram[c * HALF : (c + 1) * HALF, c * HALF : (c + 1) * HALF]
-            below = gram[HALF + 64 * c : HALF + 64 * (c + 1), 0:HALF]
-            out[:, :, 0:HALF] = diagonal[0:96].reshape(PACKED, 32, HALF)
-            out[0, :, HALF:K] = diagonal[96:128]
-            out[1:3, :, HALF:K] = below.reshape(2, 32, HALF)
+            own = slice(c * HALF, (c + 1) * HALF)
+            diagonal = gram[own, own]
+            out[0:64, 0:HALF] = gram[HALF + 64 * c : HALF + 64 * (c + 1), 0:HALF]
+            out[0:64, HALF:K] = diagonal[64:HALF]
+            corner = diagonal[0:64, 0:64]
+            out[64:PACKED, :] = jnp.concatenate(
+                [corner[16 * q : 16 * (q + 1)] for q in range(4)], axis=1
+            )
 
         @pl.when(core == 0)
         def _():
@@ -105,6 +108,10 @@
     return jax.ShapeDtypeStruct(lead + (32, K), jnp.float32)
 
 
+def flat(n):
+    return jax.ShapeDtypeStruct((32 * n + PACKED, K), jnp.float32)
+
+
 def local_products(place, e, t):
     rows, d = e.shape
     steps = rows // ROWS_STEP
@@ -114,7 +121,7 @@
 
     kept = pl.BlockSpec((4, 1, 4, 32, K), lambda i: (0, column(i), 0, 0, 0))
     sent = pl.BlockSpec((1, 4, 32, K), lambda i: (column(i), 0, 0, 0))
-    whole = pl.BlockSpec((PACKED, 32, K), lambda i: (0, 0, 0))
+    whole = pl.BlockSpec((PACKED, K), lambda i: (0, 0))
     return pl.pallas_call(
         functools.partial(local_kernel, steps),
         grid_spec=pl.GridSpec(
@@ -135,7 +142,7 @@
                 pltpu.SemaphoreType.DMA,
             ],
         ),
-        out_shape=[blocks(4, 4, 4)] + [blocks(4, 4)] * 4 + [blocks(PACKED)] * 2,
+        out_shape=[blocks(4, 4, 4)] + [blocks(4, 4)] * 4 + [flat(0)] * 2,
         compiler_params=pltpu.CompilerParams(vmem_limit_bytes=46 * MIB),
         cost_estimate=pl.CostEstimate(
             flops=6 * rows * K * d + 8 * rows * K * K,
@@ -164,34 +171,34 @@
 
 
 def message_kernel(k, keep_ref, got_ref, gk_ref, gg_ref, out_ref):
-    out_ref[0:16] = (keep_ref[k] + got_ref[...]).reshape(16, 32, K)
-    out_ref[16:] = gk_ref[...] + gg_ref[...]
+    out_ref[0:512] = (keep_ref[k] + got_ref[...]).reshape(512, K)
+    out_ref[512:] = gk_ref[...] + gg_ref[...]
 
 
 def message(k, keep, got, gk, gg):
     kernel = functools.partial(message_kernel, k)
-    return one_step(kernel, "message", [blocks(16 + PACKED)])(keep, got, gk, gg)[0]
+    return one_step(kernel, "message", [flat(16)])(keep, got, gk, gg)[0]
 
 
 def second_kernel(keep_ref, got_ref, gk_ref, gg_ref, a, b, c, own, *refs):
     out, m = refs[:-1], refs[-1]
     core = lax.axis_index("core")
     y, z = lax.axis_index("y"), lax.axis_index("z")
-    m[...] = (keep_ref[0] + got_ref[...]) + (a[0:16] + b[0:16] + c[0:16]).reshape(
+    m[...] = (keep_ref[0] + got_ref[...]) + (a[0:512] + b[0:512] + c[0:512]).reshape(
         4, 4, 32, K
     )
-    gram = (gk_ref[...] + gg_ref[...]) + (a[16:] + b[16:] + c[16:])
+    gram = (gk_ref[...] + gg_ref[...]) + (a[512:] + b[512:] + c[512:])
     for ref, k in zip((own,) + out, (0,) + DISTANCES):
         for i in range(4):
             first = jnp.where(core == 0, (y + k) & 3, i)
             other = jnp.where(core == 0, i, (z + k) & 3)
-            ref[i] = m[first, other]
+            ref[32 * i : 32 * (i + 1)] = m[first, other]
     for ref in out:
-        ref[4:] = gram
+        ref[128:] = gram
 
 
 def second(keep, got, gk, gg, arrived):
-    outs = [blocks(4)] + [blocks(4 + PACKED)] * 3
+    outs = [jax.ShapeDtypeStruct((128, K), jnp.float32)] + [flat(4)] * 3
     scratch = [pltpu.VMEM((4, 4, 32, K), jnp.float32)]
     return one_step(second_kernel, "second", outs)(
         keep, got, gk, gg, *arrived, scratch=scratch
@@ -200,28 +207,28 @@
 
 def third_kernel(own_ref, sent, a, b, c, own, *refs):
     out, m = refs[:-1], refs[-1]
-    m[...] = own_ref[...] + (a[0:4] + b[0:4] + c[0:4])
-    gram = sent[4:] + (a[4:] + b[4:] + c[4:])
+    m[...] = (own_ref[...] + (a[0:128] + b[0:128] + c[0:128])).reshape(4, 32, K)
+    gram = sent[128:] + (a[128:] + b[128:] + c[128:])
     at = jnp.where(lax.axis_index("core") == 0, lax.axis_index("x"), lax.axis_index("y"))
     own[...] = m[at]
     for ref, k in zip(out, DISTANCES):
-        ref[0] = m[(at + k) & 3]
-        ref[1:] = gram
+        ref[0:32] = m[(at + k) & 3]
+        ref[32:] = gram
 
 
 def third(own, sent, arrived):
-    outs = [blocks()] + [blocks(1 + PACKED)] * 3
+    outs = [blocks()] + [flat(1)] * 3
     scratch = [pltpu.VMEM((4, 32, K), jnp.float32)]
     return one_step(third_kernel, "third", outs)(own, sent, *arrived, scratch=scratch)
 
 
 def last_kernel(own_ref, sent, a, b, c, m_ref, g_ref):
-    m_ref[...] = own_ref[...] + (a[0] + b[0] + c[0])
-    g_ref[...] = sent[1:] + (a[1:] + b[1:] + c[1:])
+    m_ref[...] = own_ref[...] + (a[0:32] + b[0:32] + c[0:32])
+    g_ref[...] = sent[32:] + (a[32:] + b[32:] + c[32:])
 
 
 def last(own, sent, arrived):
-    return one_step(last_kernel, "last", [blocks(), blocks(PACKED)])(own, sent, *arrived)
+    return one_step(last_kernel, "last", [blocks(), flat(0)])(own, sent, *arrived)
 
 
 def across(v, lane):
@@ -301,9 +308,10 @@
     one = jnp.where(core == 0, other_ref[...], own_ref[...])
 
     def unpack(packed):
-        left = packed[:, :, 0:HALF].reshape(96, HALF)
-        right = packed[:, :, HALF:K].reshape(96, HALF)
-        return jnp.concatenate([left, right[0:32]], axis=0), right[32:96]
+        low = packed[0:64, HALF:K]
+        corner = [packed[64:PACKED, 64 * q : 64 * (q + 1)] for q in range(4)]
+        top = jnp.concatenate([jnp.concatenate(corner, axis=0), low[:, 0:64].T], axis=1)
+        return jnp.concatenate([top, low], axis=0), packed[0:64, 0:HALF]
 
     a[...], upper = unpack(zero)
     corner, lower = unpack(one)

time: 81.1 us -> 80.4 us (level)
  waiting for transfers between devices: 23.7 us -> 22.8 us
    ppermute x9, waiting for transfers between devices: 19.9 us -> 19 us  [along(): lax.ppermute(m, every, ring_pairs(axes, k))]
where the time goes in v5:
time: 80.4 us; the launch traced here: 80.3 us
  Pallas kernels  35.7 us (44%)
  waiting for transfers between devices  22.8 us (28%)
  starting transfers between devices  21.7 us (27%)
    pallas_call x1, Pallas kernels, local_products(): pl.pallas_call(functools.partial(local_kernel, steps), grid_spec=pl.GridS...  27.1 us
    ppermute x9, waiting for transfers between devices, along(): lax.ppermute(m, every, ring_pairs(axes, k))  19 us
    ppermute x9, starting transfers between devices, along(): lax.ppermute(m, every, ring_pairs(axes, k))  13.8 us
    pallas_call x1, Pallas kernels, finish(): pl.pallas_call(finish_kernel, out_shape=blocks(), in_specs=[vmem] * 3, ou...  8.09 us
    ppermute x1, starting transfers between devices, local(): return finish(m, g, lax.ppermute(g, 'core', swap))  3.94 us
    ppermute x3, starting transfers between devices, local(): got[k] = lax.ppermute(send[k], 'core', swap)  2.34 us
  transfers between devices with their start and end apart: 15, of which 11 were waited for; matrix products, arithmetic and copies ran while one was open for 0% of the time, Pallas kernels for 0%

profile of v5, /device:TPU:1, one launch (start us, length us, event | category | flops | bytes accessed | tf_op | source)
XLA Modules:
  0.0 80.3 jit_solution(2233136039270244897)
XLA Ops:
  0.0 0.1 pad_add_fusion.place_ref
  0.1 27.1 %local_products.1 = (f32[4,4,4,32,256]{4,3,2,1,0:T(8,128)S(1)}, f32[4,4,32,256]{3,2,1,0:T(8,128)S(1)}, f32[4,4,32,256]{3,2,1,0:T(8,128)S(1)}, f32[4,4,32,256]{3,...) custom-call(s32[4]{0:T(128)S(1)} %pad_add_fusion.place_ref, ...), custom_call_target="tpu_custom_call" | custom-call | flops 20937965568 | bytes 31457280 | tf_op jit(solution)/shard_map/local_products/pallas_call | solution.py:125
  27.2 1.5 %collective-permute-start = (f32[80,256]{1,0:T(8,128)S(1)}, f32[80,256]{1,0:T(8,128)S(1)}, u32[]{:S(2)}, u32[]{:S(2)}) collective-permute-start(f32[80,256]{1,0:T(8,128)S(1)} %get-tuple-element.30), channel_id=1, source_target_pairs={{0,1},{1,0},{2,3},{3,2},{4,5},{5,4},{6,7},{7,6},{8,9},{9,8},{10,11... | collective-permute-start | bytes 245768 | tf_op jit(solution)/shard_map/ppermute | solution.py:371
  28.6 0.1 collective-permute-start.2
  28.7 0.8 %collective-permute-done.gg_ref = f32[80,256]{1,0:T(8,128)S(1)} collective-permute-done((f32[80,256]{1,0:T(8,128)S(1)}, f32[80,256]{1,0:T(8,128)S(1)}, u32[]{:S(2)}, u32[]{:S(2)}) %collective-permute-start) | collective-permute-done | bytes 81952 | tf_op jit(solution)/shard_map/ppermute | solution.py:371
  29.6 0.4 collective-permute-start.6
  29.9 0.2 collective-permute-start.4
  30.1 0.5 collective-permute-done.2.got_ref
  30.6 2.9 %collective-permute-start.3 = (f32[592,256]{1,0:T(8,128)S(1)}, f32[592,256]{1,0:T(8,128)S(1)}, u32[]{:S(2)}, u32[]{:S(2)}) collective-permute-start(f32[592,256]{1,0:T(8,128)S(1)} %message.3), channel_id=1, source_target_pairs={{0,4},{1,17},{2,6},{3,19},{4,0},{5,21},{6,2},{7,23},{8,12},{9,25},... | collective-permute-start | bytes 1818632 | tf_op jit(solution)/shard_map/ppermute | solution.py:363
  33.5 0.1 message.5
  33.6 0.9 %collective-permute-start.7 = (f32[592,256]{1,0:T(8,128)S(1)}, f32[592,256]{1,0:T(8,128)S(1)}, u32[]{:S(2)}, u32[]{:S(2)}) collective-permute-start(f32[592,256]{1,0:T(8,128)S(1)} %message.5), channel_id=1, source_target_pairs={{0,6},{1,25},{2,0},{3,27},{4,2},{5,29},{6,4},{7,31},{8,14},{9,1},{... | collective-permute-start | bytes 1818632 | tf_op jit(solution)/shard_map/ppermute | solution.py:363
  34.5 0.1 message.4
  34.6 0.7 collective-permute-start.5
  35.3 1.8 %collective-permute-start.1 = (f32[4,4,32,256]{3,2,1,0:T(8,128)S(1)}, f32[4,4,32,256]{3,2,1,0:T(8,128)S(1)}, u32[]{:S(2)}, u32[]{:S(2)}) collective-permute-start(f32[4,4,32,256]{3,2,1,0:T(8,128)S(1)} %get-tuple-element.31), channel_id=1, source_target_pairs={{0,1},{1,0},{2,3},{3,2},{4,5},{5,4},{6,7},{7,6},{8,9},{9,8},{10,11... | collective-permute-start | bytes 1572872 | tf_op jit(solution)/shard_map/ppermute | solution.py:376
  37.1 1.5 %collective-permute-done.1.got_ref = f32[4,4,32,256]{3,2,1,0:T(8,128)S(1)} collective-permute-done((f32[4,4,32,256]{3,2,1,0:T(8,128)S(1)}, f32[4,4,32,256]{3,2,1,0:T(8,128)S(1)}, u32[]{:S(2)}, u32[]{:S(2)}) %collective-permute-start.1) | collective-permute-done | bytes 524320 | tf_op jit(solution)/shard_map/ppermute | solution.py:376
  38.6 2.8 %collective-permute-done.3.a = f32[592,256]{1,0:T(8,128)S(1)} collective-permute-done((f32[592,256]{1,0:T(8,128)S(1)}, f32[592,256]{1,0:T(8,128)S(1)}, u32[]{:S(2)}, u32[]{:S(2)}) %collective-permute-start.3) | collective-permute-done | bytes 606240 | tf_op jit(solution)/shard_map/ppermute | solution.py:363
  41.4 6.7 %collective-permute-done.7.c = f32[592,256]{1,0:T(8,128)S(1)} collective-permute-done((f32[592,256]{1,0:T(8,128)S(1)}, f32[592,256]{1,0:T(8,128)S(1)}, u32[]{:S(2)}, u32[]{:S(2)}) %collective-permute-start.7) | collective-permute-done | bytes 606240 | tf_op jit(solution)/shard_map/ppermute | solution.py:363
  48.1 0.2 second.1
  48.4 1.7 %collective-permute-start.9 = (f32[208,256]{1,0:T(8,128)S(1)}, f32[208,256]{1,0:T(8,128)S(1)}, u32[]{:S(2)}, u32[]{:S(2)}) collective-permute-start(f32[208,256]{1,0:T(8,128)S(1)} %get-tuple-element.39), channel_id=1, source_target_pairs={{0,32},{1,3},{2,34},{3,5},{4,36},{5,7},{6,38},{7,1},{8,40},{9,11},... | collective-permute-start | bytes 638984 | tf_op jit(solution)/shard_map/ppermute | solution.py:363
  50.1 2.2 %collective-permute-start.10 = (f32[208,256]{1,0:T(8,128)S(1)}, f32[208,256]{1,0:T(8,128)S(1)}, u32[]{:S(2)}, u32[]{:S(2)}) collective-permute-start(f32[208,256]{1,0:T(8,128)S(1)} %get-tuple-element.40), channel_id=1, source_target_pairs={{0,96},{1,7},{2,98},{3,1},{4,100},{5,3},{6,102},{7,5},{8,104},{9,1... | collective-permute-start | bytes 638984 | tf_op jit(solution)/shard_map/ppermute | solution.py:363
  52.3 1.2 %collective-permute-start.8 = (f32[208,256]{1,0:T(8,128)S(1)}, f32[208,256]{1,0:T(8,128)S(1)}, u32[]{:S(2)}, u32[]{:S(2)}) collective-permute-start(f32[208,256]{1,0:T(8,128)S(1)} %get-tuple-element.38.sent), channel_id=1, source_target_pairs={{0,64},{1,5},{2,66},{3,7},{4,68},{5,1},{6,70},{7,3},{8,72},{9,13},... | collective-permute-start | bytes 638984 | tf_op jit(solution)/shard_map/ppermute | solution.py:363
  53.5 2.2 %collective-permute-done.9.b = f32[208,256]{1,0:T(8,128)S(1)} collective-permute-done((f32[208,256]{1,0:T(8,128)S(1)}, f32[208,256]{1,0:T(8,128)S(1)}, u32[]{:S(2)}, u32[]{:S(2)}) %collective-permute-start.9) | collective-permute-done | bytes 213024 | tf_op jit(solution)/shard_map/ppermute | solution.py:363
  55.7 1.6 %collective-permute-done.10.c = f32[208,256]{1,0:T(8,128)S(1)} collective-permute-done((f32[208,256]{1,0:T(8,128)S(1)}, f32[208,256]{1,0:T(8,128)S(1)}, u32[]{:S(2)}, u32[]{:S(2)}) %collective-permute-start.10) | collective-permute-done | bytes 213024 | tf_op jit(solution)/shard_map/ppermute | solution.py:363
  57.4 1.8 %collective-permute-done.8.a = f32[208,256]{1,0:T(8,128)S(1)} collective-permute-done((f32[208,256]{1,0:T(8,128)S(1)}, f32[208,256]{1,0:T(8,128)S(1)}, u32[]{:S(2)}, u32[]{:S(2)}) %collective-permute-start.8) | collective-permute-done | bytes 213024 | tf_op jit(solution)/shard_map/ppermute | solution.py:363
  59.3 1.1 %collective-permute-start.12 = (f32[112,256]{1,0:T(8,128)S(1)}, f32[112,256]{1,0:T(8,128)S(1)}, u32[]{:S(2)}, u32[]{:S(2)}) collective-permute-start(f32[112,256]{1,0:T(8,128)S(1)} %get-tuple-element.43), channel_id=1, source_target_pairs={{0,8},{1,33},{2,10},{3,35},{4,12},{5,37},{6,14},{7,39},{8,16},{9,4... | collective-permute-start | bytes 344072 | tf_op jit(solution)/shard_map/ppermute | solution.py:363
  60.3 1.8 %collective-permute-start.13 = (f32[112,256]{1,0:T(8,128)S(1)}, f32[112,256]{1,0:T(8,128)S(1)}, u32[]{:S(2)}, u32[]{:S(2)}) collective-permute-start(f32[112,256]{1,0:T(8,128)S(1)} %get-tuple-element.44), channel_id=1, source_target_pairs={{0,24},{1,97},{2,26},{3,99},{4,28},{5,101},{6,30},{7,103},{8,0},{9... | collective-permute-start | bytes 344072 | tf_op jit(solution)/shard_map/ppermute | solution.py:363
  62.1 1.3 %collective-permute-start.11 = (f32[112,256]{1,0:T(8,128)S(1)}, f32[112,256]{1,0:T(8,128)S(1)}, u32[]{:S(2)}, u32[]{:S(2)}) collective-permute-start(f32[112,256]{1,0:T(8,128)S(1)} %get-tuple-element.42.sent), channel_id=1, source_target_pairs={{0,16},{1,65},{2,18},{3,67},{4,20},{5,69},{6,22},{7,71},{8,24},{9,... | collective-permute-start | bytes 344072 | tf_op jit(solution)/shard_map/ppermute | solution.py:363
  63.4 0.8 %collective-permute-done.12.b = f32[112,256]{1,0:T(8,128)S(1)} collective-permute-done((f32[112,256]{1,0:T(8,128)S(1)}, f32[112,256]{1,0:T(8,128)S(1)}, u32[]{:S(2)}, u32[]{:S(2)}) %collective-permute-start.12) | collective-permute-done | bytes 114720 | tf_op jit(solution)/shard_map/ppermute | solution.py:363
  64.2 3.0 %collective-permute-done.11.a = f32[112,256]{1,0:T(8,128)S(1)} collective-permute-done((f32[112,256]{1,0:T(8,128)S(1)}, f32[112,256]{1,0:T(8,128)S(1)}, u32[]{:S(2)}, u32[]{:S(2)}) %collective-permute-start.11) | collective-permute-done | bytes 114720 | tf_op jit(solution)/shard_map/ppermute | solution.py:363
  67.3 3.9 %collective-permute-start.14 = (f32[80,256]{1,0:T(8,128)S(1)}, f32[80,256]{1,0:T(8,128)S(1)}, u32[]{:S(2)}, u32[]{:S(2)}) collective-permute-start(f32[80,256]{1,0:T(8,128)S(1)} %get-tuple-element.46.own_ref), channel_id=1, source_target_pairs={{0,1},{1,0},{2,3},{3,2},{4,5},{5,4},{6,7},{7,6},{8,9},{9,8},{10,11... | collective-permute-start | bytes 245768 | tf_op jit(solution)/shard_map/ppermute | solution.py:384
  71.3 0.9 %collective-permute-done.14.other_ref = f32[80,256]{1,0:T(8,128)S(1)} collective-permute-done((f32[80,256]{1,0:T(8,128)S(1)}, f32[80,256]{1,0:T(8,128)S(1)}, u32[]{:S(2)}, u32[]{:S(2)}) %collective-permute-start.14) | collective-permute-done | bytes 81952 | tf_op jit(solution)/shard_map/ppermute | solution.py:384
  72.2 8.1 %finish.1 = f32[32,256]{1,0:T(8,128)} custom-call(f32[32,256]{1,0:T(8,128)S(1)} %get-tuple-element.45.m_ref, f32[80,256]{1,0:T(8,128)S(1)} %get-tuple-element.46.own_ref, f32[80,256]{1,0:T(8,128)S(1)} %collective-permute-done.14.other_ref), custom_call_target="tpu_custom_call" | custom-call | tf_op jit(solution)/shard_map/finish/pallas_call | solution.py:331
  (7 shorter events, 0.2 us)
Async XLA Ops:
  27.2 2.4 %collective-permute-start = (f32[80,256]{1,0:T(8,128)S(1)}, f32[80,256]{1,0:T(8,128)S(1)}, u32[]{:S(2)}, u32[]{:S(2)}) collective-permute-start(f32[80,256]{1,0:T(8,128)S(1)} %get-tuple-element.30), channel_id=1, source_target_pairs={{0,1},{1,0},{2,3},{3,2},{4,5},{5,4},{6,7},{7,6},{8,9},{9,8},{10,11... | collective-permute-start | bytes 245768 | tf_op jit(solution)/shard_map/ppermute | solution.py:371
  28.6 1.9 %collective-permute-start.2 = (f32[4,4,32,256]{3,2,1,0:T(8,128)S(1)}, f32[4,4,32,256]{3,2,1,0:T(8,128)S(1)}, u32[]{:S(2)}, u32[]{:S(2)}) collective-permute-start(f32[4,4,32,256]{3,2,1,0:T(8,128)S(1)} %get-tuple-element.34), channel_id=1, source_target_pairs={{0,1},{1,0},{2,3},{3,2},{4,5},{5,4},{6,7},{7,6},{8,9},{9,8},{10,11... | collective-permute-start | bytes 1572872 | tf_op jit(solution)/shard_map/ppermute | solution.py:370
  29.6 4.0 %collective-permute-start.6 = (f32[4,4,32,256]{3,2,1,0:T(8,128)S(1)}, f32[4,4,32,256]{3,2,1,0:T(8,128)S(1)}, u32[]{:S(2)}, u32[]{:S(2)}) collective-permute-start(f32[4,4,32,256]{3,2,1,0:T(8,128)S(1)} %get-tuple-element.36), channel_id=1, source_target_pairs={{0,1},{1,0},{2,3},{3,2},{4,5},{5,4},{6,7},{7,6},{8,9},{9,8},{10,11... | collective-permute-start | bytes 1572872 | tf_op jit(solution)/shard_map/ppermute | solution.py:376
  29.9 4.6 %collective-permute-start.4 = (f32[4,4,32,256]{3,2,1,0:T(8,128)S(1)}, f32[4,4,32,256]{3,2,1,0:T(8,128)S(1)}, u32[]{:S(2)}, u32[]{:S(2)}) collective-permute-start(f32[4,4,32,256]{3,2,1,0:T(8,128)S(1)} %get-tuple-element.35), channel_id=1, source_target_pairs={{0,1},{1,0},{2,3},{3,2},{4,5},{5,4},{6,7},{7,6},{8,9},{9,8},{10,11... | collective-permute-start | bytes 1572872 | tf_op jit(solution)/shard_map/ppermute | solution.py:376
  30.6 10.8 %collective-permute-start.3 = (f32[592,256]{1,0:T(8,128)S(1)}, f32[592,256]{1,0:T(8,128)S(1)}, u32[]{:S(2)}, u32[]{:S(2)}) collective-permute-start(f32[592,256]{1,0:T(8,128)S(1)} %message.3), channel_id=1, source_target_pairs={{0,4},{1,17},{2,6},{3,19},{4,0},{5,21},{6,2},{7,23},{8,12},{9,25},... | collective-permute-start | bytes 1818632 | tf_op jit(solution)/shard_map/ppermute | solution.py:363
  33.6 14.5 %collective-permute-start.7 = (f32[592,256]{1,0:T(8,128)S(1)}, f32[592,256]{1,0:T(8,128)S(1)}, u32[]{:S(2)}, u32[]{:S(2)}) collective-permute-start(f32[592,256]{1,0:T(8,128)S(1)} %message.5), channel_id=1, source_target_pairs={{0,6},{1,25},{2,0},{3,27},{4,2},{5,29},{6,4},{7,31},{8,14},{9,1},{... | collective-permute-start | bytes 1818632 | tf_op jit(solution)/shard_map/ppermute | solution.py:363
  34.6 13.5 %collective-permute-start.5 = (f32[592,256]{1,0:T(8,128)S(1)}, f32[592,256]{1,0:T(8,128)S(1)}, u32[]{:S(2)}, u32[]{:S(2)}) collective-permute-start(f32[592,256]{1,0:T(8,128)S(1)} %message.4), channel_id=1, source_target_pairs={{0,2},{1,9},{2,4},{3,11},{4,6},{5,13},{6,0},{7,15},{8,10},{9,17},{... | collective-permute-start | bytes 1818632 | tf_op jit(solution)/shard_map/ppermute | solution.py:363
  35.3 3.4 %collective-permute-start.1 = (f32[4,4,32,256]{3,2,1,0:T(8,128)S(1)}, f32[4,4,32,256]{3,2,1,0:T(8,128)S(1)}, u32[]{:S(2)}, u32[]{:S(2)}) collective-permute-start(f32[4,4,32,256]{3,2,1,0:T(8,128)S(1)} %get-tuple-element.31), channel_id=1, source_target_pairs={{0,1},{1,0},{2,3},{3,2},{4,5},{5,4},{6,7},{7,6},{8,9},{9,8},{10,11... | collective-permute-start | bytes 1572872 | tf_op jit(solution)/shard_map/ppermute | solution.py:376
  48.4 7.4 %collective-permute-start.9 = (f32[208,256]{1,0:T(8,128)S(1)}, f32[208,256]{1,0:T(8,128)S(1)}, u32[]{:S(2)}, u32[]{:S(2)}) collective-permute-start(f32[208,256]{1,0:T(8,128)S(1)} %get-tuple-element.39), channel_id=1, source_target_pairs={{0,32},{1,3},{2,34},{3,5},{4,36},{5,7},{6,38},{7,1},{8,40},{9,11},... | collective-permute-start | bytes 638984 | tf_op jit(solution)/shard_map/ppermute | solution.py:363
  50.1 7.3 %collective-permute-start.10 = (f32[208,256]{1,0:T(8,128)S(1)}, f32[208,256]{1,0:T(8,128)S(1)}, u32[]{:S(2)}, u32[]{:S(2)}) collective-permute-start(f32[208,256]{1,0:T(8,128)S(1)} %get-tuple-element.40), channel_id=1, source_target_pairs={{0,96},{1,7},{2,98},{3,1},{4,100},{5,3},{6,102},{7,5},{8,104},{9,1... | collective-permute-start | bytes 638984 | tf_op jit(solution)/shard_map/ppermute | solution.py:363
  52.3 6.9 %collective-permute-start.8 = (f32[208,256]{1,0:T(8,128)S(1)}, f32[208,256]{1,0:T(8,128)S(1)}, u32[]{:S(2)}, u32[]{:S(2)}) collective-permute-start(f32[208,256]{1,0:T(8,128)S(1)} %get-tuple-element.38.sent), channel_id=1, source_target_pairs={{0,64},{1,5},{2,66},{3,7},{4,68},{5,1},{6,70},{7,3},{8,72},{9,13},... | collective-permute-start | bytes 638984 | tf_op jit(solution)/shard_map/ppermute | solution.py:363
  59.3 5.0 %collective-permute-start.12 = (f32[112,256]{1,0:T(8,128)S(1)}, f32[112,256]{1,0:T(8,128)S(1)}, u32[]{:S(2)}, u32[]{:S(2)}) collective-permute-start(f32[112,256]{1,0:T(8,128)S(1)} %get-tuple-element.43), channel_id=1, source_target_pairs={{0,8},{1,33},{2,10},{3,35},{4,12},{5,37},{6,14},{7,39},{8,16},{9,4... | collective-permute-start | bytes 344072 | tf_op jit(solution)/shard_map/ppermute | solution.py:363
  60.3 3.9 %collective-permute-start.13 = (f32[112,256]{1,0:T(8,128)S(1)}, f32[112,256]{1,0:T(8,128)S(1)}, u32[]{:S(2)}, u32[]{:S(2)}) collective-permute-start(f32[112,256]{1,0:T(8,128)S(1)} %get-tuple-element.44), channel_id=1, source_target_pairs={{0,24},{1,97},{2,26},{3,99},{4,28},{5,101},{6,30},{7,103},{8,0},{9... | collective-permute-start | bytes 344072 | tf_op jit(solution)/shard_map/ppermute | solution.py:363
  62.1 5.1 %collective-permute-start.11 = (f32[112,256]{1,0:T(8,128)S(1)}, f32[112,256]{1,0:T(8,128)S(1)}, u32[]{:S(2)}, u32[]{:S(2)}) collective-permute-start(f32[112,256]{1,0:T(8,128)S(1)} %get-tuple-element.42.sent), channel_id=1, source_target_pairs={{0,16},{1,65},{2,18},{3,67},{4,20},{5,69},{6,22},{7,71},{8,24},{9,... | collective-permute-start | bytes 344072 | tf_op jit(solution)/shard_map/ppermute | solution.py:363
  67.3 4.9 %collective-permute-start.14 = (f32[80,256]{1,0:T(8,128)S(1)}, f32[80,256]{1,0:T(8,128)S(1)}, u32[]{:S(2)}, u32[]{:S(2)}) collective-permute-start(f32[80,256]{1,0:T(8,128)S(1)} %get-tuple-element.46.own_ref), channel_id=1, source_target_pairs={{0,1},{1,0},{2,3},{3,2},{4,5},{5,4},{6,7},{7,6},{8,9},{9,8},{10,11... | collective-permute-start | bytes 245768 | tf_op jit(solution)/shard_map/ppermute | solution.py:384

commit v6 on v5

--- a/solution.py
+++ b/solution.py
@@ -22,7 +22,7 @@
     return terms[0]
 
 
-ROWS_STEP = 768
+ROWS_STEP = 512
 COLS_STEP = 1024
 CHIPS_STEP = COLS_STEP // 64
 PACKED = 80
@@ -49,22 +49,21 @@
         table.wait()
         fetch(1).start()
 
-    @pl.when(i < steps)
-    def _():
-        fetch(i).wait()
-
-        @pl.when(i + 2 < steps)
-        def _():
-            fetch(i + 2).start()
-
-        r = pl.ds(pl.multiple_of(i * ROWS_STEP, ROWS_STEP), ROWS_STEP)
-        s = jnp.dot(held[r, :], t_held[...], preferred_element_type=f32)
-        hi = s.astype(jnp.bfloat16)
-        s_ref[r, 0:K] = hi
-        s_ref[r, K : 2 * K] = (s - hi.astype(f32)).astype(jnp.bfloat16)
-
-    @pl.when(i == steps)
-    def _():
+        def sketch(step, carry):
+            fetch(step).wait()
+
+            @pl.when(step + 2 < steps)
+            def _():
+                fetch(step + 2).start()
+
+            r = pl.ds(pl.multiple_of(step * ROWS_STEP, ROWS_STEP), ROWS_STEP)
+            s = jnp.dot(held[r, :], t_held[...], preferred_element_type=f32)
+            hi = s.astype(jnp.bfloat16)
+            s_ref[r, 0:K] = hi
+            s_ref[r, K : 2 * K] = (s - hi.astype(f32)).astype(jnp.bfloat16)
+            return carry
+
+        lax.fori_loop(0, steps, sketch, 0)
         g = lax.dot_general(
             s_ref[:, 0:K], s_ref[...], OVER_ROWS, preferred_element_type=f32
         )
@@ -91,9 +90,9 @@
             pack(gram_keep_ref, 1)
             pack(gram_send_ref, 0)
 
-    @pl.when(i >= steps)
+    @pl.when(i > 0)
     def _():
-        c = pl.ds(pl.multiple_of((i - steps) * COLS_STEP, COLS_STEP), COLS_STEP)
+        c = pl.ds(pl.multiple_of((i - 1) * COLS_STEP, COLS_STEP), COLS_STEP)
         m = lax.dot_general(held[:, c], s_ref[...], OVER_ROWS, preferred_element_type=f32)
         parts[...] = (m[:, 0:K] + m[:, K : 2 * K]).reshape(CHIPS_STEP, 2, 32, K)
         for k, send_ref in enumerate((s0, s1, s2, s3)):
@@ -117,7 +116,7 @@
     steps = rows // ROWS_STEP
 
     def column(i):
-        return jnp.maximum(i - steps, 0)
+        return jnp.maximum(i - 1, 0)
 
     kept = pl.BlockSpec((4, 1, 4, 32, K), lambda i: (0, column(i), 0, 0, 0))
     sent = pl.BlockSpec((1, 4, 32, K), lambda i: (column(i), 0, 0, 0))
@@ -125,7 +124,7 @@
     return pl.pallas_call(
         functools.partial(local_kernel, steps),
         grid_spec=pl.GridSpec(
-            grid=(steps + d // COLS_STEP,),
+            grid=(1 + d // COLS_STEP,),
             in_specs=[
                 pl.BlockSpec(memory_space=pltpu.SMEM),
                 pl.BlockSpec(memory_space=pl.ANY),
@@ -339,7 +338,8 @@
     )(m, own, other)
 
 
-DISTANCES = (2, 1, 3)
+FIRST = (2, 1, 3)
+DISTANCES = (3, 1, 2)
 
 
 def ring_pairs(axes, distance):
@@ -358,9 +358,9 @@
     fine = Mesh(mesh.devices.reshape(4, 4, 4, 2), every)
     swap = [(0, 1), (1, 0)]
 
-    def along(axes, messages):
+    def along(axes, messages, distances=DISTANCES):
         return [
-            lax.ppermute(m, every, ring_pairs(axes, k)) for m, k in zip(messages, DISTANCES)
+            lax.ppermute(m, every, ring_pairs(axes, k)) for m, k in zip(messages, distances)
         ]
 
     def local(embedding, test_matrix):
@@ -374,8 +374,8 @@
         )
         for k in (1, 3, 0):
             got[k] = lax.ppermute(send[k], "core", swap)
-        messages = [message(k, keep, got[k], gk, gg) for k in DISTANCES]
-        arrived = along(("z", "x"), messages)
+        messages = [message(k, keep, got[k], gk, gg) for k in FIRST]
+        arrived = along(("z", "x"), messages, FIRST)
         own, *messages = second(keep, got[0], gk, gg, arrived)
         arrived = along(("y", "z"), messages)
         own, *messages_3 = third(own, messages[0], arrived)

time: 80.4 us -> 79.4 us (0.988)
  waiting for transfers between devices: 22.8 us -> 21.2 us
  starting transfers between devices: 21.7 us -> 22.8 us
    ppermute x9, waiting for transfers between devices: 19 us -> 17.4 us  [along(): lax.ppermute(m, every, ring_pairs(axes, k))]
    ppermute x9, starting transfers between devices: 13.8 us -> 15 us  [along(): lax.ppermute(m, every, ring_pairs(axes, k))]
where the time goes in v6:
time: 79.4 us; the launch traced here: 79.3 us
  Pallas kernels  35.3 us (44%)
  starting transfers between devices  22.8 us (29%)
  waiting for transfers between devices  21.2 us (27%)
    pallas_call x1, Pallas kernels, local_products(): pl.pallas_call(functools.partial(local_kernel, steps), grid_spec=pl.GridS...  26.6 us
    ppermute x9, waiting for transfers between devices, along(): lax.ppermute(m, every, ring_pairs(axes, k))  17.4 us
    ppermute x9, starting transfers between devices, along(): lax.ppermute(m, every, ring_pairs(axes, k))  15 us
    pallas_call x1, Pallas kernels, finish(): pl.pallas_call(finish_kernel, out_shape=blocks(), in_specs=[vmem] * 3, ou...  8.09 us
    ppermute x1, starting transfers between devices, local(): return finish(m, g, lax.ppermute(g, 'core', swap))  3.82 us
    ppermute x3, starting transfers between devices, local(): got[k] = lax.ppermute(send[k], 'core', swap)  2.33 us
  transfers between devices with their start and end apart: 15, of which 11 were waited for; matrix products, arithmetic and copies ran while one was open for 0% of the time, Pallas kernels for 0%

profile of v6, /device:TPU:1, one launch (start us, length us, event | category | flops | bytes accessed | tf_op | source)
XLA Modules:
  0.0 79.3 jit_solution(9346841513228370620)
XLA Ops:
  0.0 0.1 pad_add_fusion.place_ref
  0.1 26.6 %local_products.1 = (f32[4,4,4,32,256]{4,3,2,1,0:T(8,128)S(1)}, f32[4,4,32,256]{3,2,1,0:T(8,128)S(1)}, f32[4,4,32,256]{3,2,1,0:T(8,128)S(1)}, f32[4,4,32,256]{3,...) custom-call(s32[4]{0:T(128)S(1)} %pad_add_fusion.place_ref, ...), custom_call_target="tpu_custom_call" | custom-call | flops 20937965568 | bytes 31457280 | tf_op jit(solution)/shard_map/local_products/pallas_call | solution.py:124
  26.7 1.5 %collective-permute-start = (f32[80,256]{1,0:T(8,128)S(1)}, f32[80,256]{1,0:T(8,128)S(1)}, u32[]{:S(2)}, u32[]{:S(2)}) collective-permute-start(f32[80,256]{1,0:T(8,128)S(1)} %get-tuple-element.30), channel_id=1, source_target_pairs={{0,1},{1,0},{2,3},{3,2},{4,5},{5,4},{6,7},{7,6},{8,9},{9,8},{10,11... | collective-permute-start | bytes 245768 | tf_op jit(solution)/shard_map/ppermute | solution.py:371
  28.2 0.1 collective-permute-start.2
  28.3 0.8 %collective-permute-done.gg_ref = f32[80,256]{1,0:T(8,128)S(1)} collective-permute-done((f32[80,256]{1,0:T(8,128)S(1)}, f32[80,256]{1,0:T(8,128)S(1)}, u32[]{:S(2)}, u32[]{:S(2)}) %collective-permute-start) | collective-permute-done | bytes 81952 | tf_op jit(solution)/shard_map/ppermute | solution.py:371
  29.2 0.4 collective-permute-start.6
  29.5 0.2 collective-permute-start.4
  29.7 0.5 collective-permute-done.2.got_ref
  30.1 0.1 message.3
  30.2 2.9 %collective-permute-start.3 = (f32[592,256]{1,0:T(8,128)S(1)}, f32[592,256]{1,0:T(8,128)S(1)}, u32[]{:S(2)}, u32[]{:S(2)}) collective-permute-start(f32[592,256]{1,0:T(8,128)S(1)} %message.3), channel_id=1, source_target_pairs={{0,4},{1,17},{2,6},{3,19},{4,0},{5,21},{6,2},{7,23},{8,12},{9,25},... | collective-permute-start | bytes 1818632 | tf_op jit(solution)/shard_map/ppermute | solution.py:363
  33.1 0.1 message.5
  33.2 0.9 %collective-permute-start.7 = (f32[592,256]{1,0:T(8,128)S(1)}, f32[592,256]{1,0:T(8,128)S(1)}, u32[]{:S(2)}, u32[]{:S(2)}) collective-permute-start(f32[592,256]{1,0:T(8,128)S(1)} %message.5), channel_id=1, source_target_pairs={{0,6},{1,25},{2,0},{3,27},{4,2},{5,29},{6,4},{7,31},{8,14},{9,1},{... | collective-permute-start | bytes 1818632 | tf_op jit(solution)/shard_map/ppermute | solution.py:363
  34.2 0.7 collective-permute-start.5
  34.9 1.8 %collective-permute-start.1 = (f32[4,4,32,256]{3,2,1,0:T(8,128)S(1)}, f32[4,4,32,256]{3,2,1,0:T(8,128)S(1)}, u32[]{:S(2)}, u32[]{:S(2)}) collective-permute-start(f32[4,4,32,256]{3,2,1,0:T(8,128)S(1)} %get-tuple-element.31), channel_id=1, source_target_pairs={{0,1},{1,0},{2,3},{3,2},{4,5},{5,4},{6,7},{7,6},{8,9},{9,8},{10,11... | collective-permute-start | bytes 1572872 | tf_op jit(solution)/shard_map/ppermute | solution.py:376
  36.7 1.5 %collective-permute-done.1.got_ref = f32[4,4,32,256]{3,2,1,0:T(8,128)S(1)} collective-permute-done((f32[4,4,32,256]{3,2,1,0:T(8,128)S(1)}, f32[4,4,32,256]{3,2,1,0:T(8,128)S(1)}, u32[]{:S(2)}, u32[]{:S(2)}) %collective-permute-start.1) | collective-permute-done | bytes 524320 | tf_op jit(solution)/shard_map/ppermute | solution.py:376
  38.2 2.8 %collective-permute-done.3.a = f32[592,256]{1,0:T(8,128)S(1)} collective-permute-done((f32[592,256]{1,0:T(8,128)S(1)}, f32[592,256]{1,0:T(8,128)S(1)}, u32[]{:S(2)}, u32[]{:S(2)}) %collective-permute-start.3) | collective-permute-done | bytes 606240 | tf_op jit(solution)/shard_map/ppermute | solution.py:363
  41.0 6.7 %collective-permute-done.7.c = f32[592,256]{1,0:T(8,128)S(1)} collective-permute-done((f32[592,256]{1,0:T(8,128)S(1)}, f32[592,256]{1,0:T(8,128)S(1)}, u32[]{:S(2)}, u32[]{:S(2)}) %collective-permute-start.7) | collective-permute-done | bytes 606240 | tf_op jit(solution)/shard_map/ppermute | solution.py:363
  47.7 0.2 second.1
  48.0 1.7 %collective-permute-start.9 = (f32[208,256]{1,0:T(8,128)S(1)}, f32[208,256]{1,0:T(8,128)S(1)}, u32[]{:S(2)}, u32[]{:S(2)}) collective-permute-start(f32[208,256]{1,0:T(8,128)S(1)} %get-tuple-element.39), channel_id=1, source_target_pairs={{0,32},{1,3},{2,34},{3,5},{4,36},{5,7},{6,38},{7,1},{8,40},{9,11},... | collective-permute-start | bytes 638984 | tf_op jit(solution)/shard_map/ppermute | solution.py:363
  49.7 3.3 %collective-permute-start.10 = (f32[208,256]{1,0:T(8,128)S(1)}, f32[208,256]{1,0:T(8,128)S(1)}, u32[]{:S(2)}, u32[]{:S(2)}) collective-permute-start(f32[208,256]{1,0:T(8,128)S(1)} %get-tuple-element.40), channel_id=1, source_target_pairs={{0,64},{1,5},{2,66},{3,7},{4,68},{5,1},{6,70},{7,3},{8,72},{9,13},... | collective-permute-start | bytes 638984 | tf_op jit(solution)/shard_map/ppermute | solution.py:363
  53.0 0.7 collective-permute-start.8
  53.7 1.6 %collective-permute-done.9.b = f32[208,256]{1,0:T(8,128)S(1)} collective-permute-done((f32[208,256]{1,0:T(8,128)S(1)}, f32[208,256]{1,0:T(8,128)S(1)}, u32[]{:S(2)}, u32[]{:S(2)}) %collective-permute-start.9) | collective-permute-done | bytes 213024 | tf_op jit(solution)/shard_map/ppermute | solution.py:363
  55.3 3.5 %collective-permute-done.10.c = f32[208,256]{1,0:T(8,128)S(1)} collective-permute-done((f32[208,256]{1,0:T(8,128)S(1)}, f32[208,256]{1,0:T(8,128)S(1)}, u32[]{:S(2)}, u32[]{:S(2)}) %collective-permute-start.10) | collective-permute-done | bytes 213024 | tf_op jit(solution)/shard_map/ppermute | solution.py:363
  58.8 1.1 %collective-permute-start.12 = (f32[112,256]{1,0:T(8,128)S(1)}, f32[112,256]{1,0:T(8,128)S(1)}, u32[]{:S(2)}, u32[]{:S(2)}) collective-permute-start(f32[112,256]{1,0:T(8,128)S(1)} %get-tuple-element.43), channel_id=1, source_target_pairs={{0,8},{1,33},{2,10},{3,35},{4,12},{5,37},{6,14},{7,39},{8,16},{9,4... | collective-permute-start | bytes 344072 | tf_op jit(solution)/shard_map/ppermute | solution.py:363
  59.9 2.6 %collective-permute-start.13 = (f32[112,256]{1,0:T(8,128)S(1)}, f32[112,256]{1,0:T(8,128)S(1)}, u32[]{:S(2)}, u32[]{:S(2)}) collective-permute-start(f32[112,256]{1,0:T(8,128)S(1)} %get-tuple-element.44), channel_id=1, source_target_pairs={{0,16},{1,65},{2,18},{3,67},{4,20},{5,69},{6,22},{7,71},{8,24},{9,... | collective-permute-start | bytes 344072 | tf_op jit(solution)/shard_map/ppermute | solution.py:363
  62.5 1.1 %collective-permute-start.11 = (f32[112,256]{1,0:T(8,128)S(1)}, f32[112,256]{1,0:T(8,128)S(1)}, u32[]{:S(2)}, u32[]{:S(2)}) collective-permute-start(f32[112,256]{1,0:T(8,128)S(1)} %get-tuple-element.42.sent), channel_id=1, source_target_pairs={{0,24},{1,97},{2,26},{3,99},{4,28},{5,101},{6,30},{7,103},{8,0},{9... | collective-permute-start | bytes 344072 | tf_op jit(solution)/shard_map/ppermute | solution.py:363
  63.6 0.2 collective-permute-done.12.b
  63.8 2.2 %collective-permute-done.13.c = f32[112,256]{1,0:T(8,128)S(1)} collective-permute-done((f32[112,256]{1,0:T(8,128)S(1)}, f32[112,256]{1,0:T(8,128)S(1)}, u32[]{:S(2)}, u32[]{:S(2)}) %collective-permute-start.13) | collective-permute-done | bytes 114720 | tf_op jit(solution)/shard_map/ppermute | solution.py:363
  66.0 0.5 collective-permute-done.11.a
  66.5 3.8 %collective-permute-start.14 = (f32[80,256]{1,0:T(8,128)S(1)}, f32[80,256]{1,0:T(8,128)S(1)}, u32[]{:S(2)}, u32[]{:S(2)}) collective-permute-start(f32[80,256]{1,0:T(8,128)S(1)} %get-tuple-element.46.own_ref), channel_id=1, source_target_pairs={{0,1},{1,0},{2,3},{3,2},{4,5},{5,4},{6,7},{7,6},{8,9},{9,8},{10,11... | collective-permute-start | bytes 245768 | tf_op jit(solution)/shard_map/ppermute | solution.py:384
  70.3 0.9 %collective-permute-done.14.other_ref = f32[80,256]{1,0:T(8,128)S(1)} collective-permute-done((f32[80,256]{1,0:T(8,128)S(1)}, f32[80,256]{1,0:T(8,128)S(1)}, u32[]{:S(2)}, u32[]{:S(2)}) %collective-permute-start.14) | collective-permute-done | bytes 81952 | tf_op jit(solution)/shard_map/ppermute | solution.py:384
  71.3 8.1 %finish.1 = f32[32,256]{1,0:T(8,128)} custom-call(f32[32,256]{1,0:T(8,128)S(1)} %get-tuple-element.45.m_ref, f32[80,256]{1,0:T(8,128)S(1)} %get-tuple-element.46.own_ref, f32[80,256]{1,0:T(8,128)S(1)} %collective-permute-done.14.other_ref), custom_call_target="tpu_custom_call" | custom-call | tf_op jit(solution)/shard_map/finish/pallas_call | solution.py:330
  (7 shorter events, 0.2 us)
Async XLA Ops:
  26.7 2.4 %collective-permute-start = (f32[80,256]{1,0:T(8,128)S(1)}, f32[80,256]{1,0:T(8,128)S(1)}, u32[]{:S(2)}, u32[]{:S(2)}) collective-permute-start(f32[80,256]{1,0:T(8,128)S(1)} %get-tuple-element.30), channel_id=1, source_target_pairs={{0,1},{1,0},{2,3},{3,2},{4,5},{5,4},{6,7},{7,6},{8,9},{9,8},{10,11... | collective-permute-start | bytes 245768 | tf_op jit(solution)/shard_map/ppermute | solution.py:371
  28.2 1.9 %collective-permute-start.2 = (f32[4,4,32,256]{3,2,1,0:T(8,128)S(1)}, f32[4,4,32,256]{3,2,1,0:T(8,128)S(1)}, u32[]{:S(2)}, u32[]{:S(2)}) collective-permute-start(f32[4,4,32,256]{3,2,1,0:T(8,128)S(1)} %get-tuple-element.34), channel_id=1, source_target_pairs={{0,1},{1,0},{2,3},{3,2},{4,5},{5,4},{6,7},{7,6},{8,9},{9,8},{10,11... | collective-permute-start | bytes 1572872 | tf_op jit(solution)/shard_map/ppermute | solution.py:370
  29.2 4.0 %collective-permute-start.6 = (f32[4,4,32,256]{3,2,1,0:T(8,128)S(1)}, f32[4,4,32,256]{3,2,1,0:T(8,128)S(1)}, u32[]{:S(2)}, u32[]{:S(2)}) collective-permute-start(f32[4,4,32,256]{3,2,1,0:T(8,128)S(1)} %get-tuple-element.36), channel_id=1, source_target_pairs={{0,1},{1,0},{2,3},{3,2},{4,5},{5,4},{6,7},{7,6},{8,9},{9,8},{10,11... | collective-permute-start | bytes 1572872 | tf_op jit(solution)/shard_map/ppermute | solution.py:376
  29.5 4.6 %collective-permute-start.4 = (f32[4,4,32,256]{3,2,1,0:T(8,128)S(1)}, f32[4,4,32,256]{3,2,1,0:T(8,128)S(1)}, u32[]{:S(2)}, u32[]{:S(2)}) collective-permute-start(f32[4,4,32,256]{3,2,1,0:T(8,128)S(1)} %get-tuple-element.35), channel_id=1, source_target_pairs={{0,1},{1,0},{2,3},{3,2},{4,5},{5,4},{6,7},{7,6},{8,9},{9,8},{10,11... | collective-permute-start | bytes 1572872 | tf_op jit(solution)/shard_map/ppermute | solution.py:376
  30.2 10.8 %collective-permute-start.3 = (f32[592,256]{1,0:T(8,128)S(1)}, f32[592,256]{1,0:T(8,128)S(1)}, u32[]{:S(2)}, u32[]{:S(2)}) collective-permute-start(f32[592,256]{1,0:T(8,128)S(1)} %message.3), channel_id=1, source_target_pairs={{0,4},{1,17},{2,6},{3,19},{4,0},{5,21},{6,2},{7,23},{8,12},{9,25},... | collective-permute-start | bytes 1818632 | tf_op jit(solution)/shard_map/ppermute | solution.py:363
  33.2 14.5 %collective-permute-start.7 = (f32[592,256]{1,0:T(8,128)S(1)}, f32[592,256]{1,0:T(8,128)S(1)}, u32[]{:S(2)}, u32[]{:S(2)}) collective-permute-start(f32[592,256]{1,0:T(8,128)S(1)} %message.5), channel_id=1, source_target_pairs={{0,6},{1,25},{2,0},{3,27},{4,2},{5,29},{6,4},{7,31},{8,14},{9,1},{... | collective-permute-start | bytes 1818632 | tf_op jit(solution)/shard_map/ppermute | solution.py:363
  34.2 13.5 %collective-permute-start.5 = (f32[592,256]{1,0:T(8,128)S(1)}, f32[592,256]{1,0:T(8,128)S(1)}, u32[]{:S(2)}, u32[]{:S(2)}) collective-permute-start(f32[592,256]{1,0:T(8,128)S(1)} %message.4), channel_id=1, source_target_pairs={{0,2},{1,9},{2,4},{3,11},{4,6},{5,13},{6,0},{7,15},{8,10},{9,17},{... | collective-permute-start | bytes 1818632 | tf_op jit(solution)/shard_map/ppermute | solution.py:363
  34.9 3.4 %collective-permute-start.1 = (f32[4,4,32,256]{3,2,1,0:T(8,128)S(1)}, f32[4,4,32,256]{3,2,1,0:T(8,128)S(1)}, u32[]{:S(2)}, u32[]{:S(2)}) collective-permute-start(f32[4,4,32,256]{3,2,1,0:T(8,128)S(1)} %get-tuple-element.31), channel_id=1, source_target_pairs={{0,1},{1,0},{2,3},{3,2},{4,5},{5,4},{6,7},{7,6},{8,9},{9,8},{10,11... | collective-permute-start | bytes 1572872 | tf_op jit(solution)/shard_map/ppermute | solution.py:376
  48.0 7.3 %collective-permute-start.9 = (f32[208,256]{1,0:T(8,128)S(1)}, f32[208,256]{1,0:T(8,128)S(1)}, u32[]{:S(2)}, u32[]{:S(2)}) collective-permute-start(f32[208,256]{1,0:T(8,128)S(1)} %get-tuple-element.39), channel_id=1, source_target_pairs={{0,32},{1,3},{2,34},{3,5},{4,36},{5,7},{6,38},{7,1},{8,40},{9,11},... | collective-permute-start | bytes 638984 | tf_op jit(solution)/shard_map/ppermute | solution.py:363
  49.7 9.1 %collective-permute-start.10 = (f32[208,256]{1,0:T(8,128)S(1)}, f32[208,256]{1,0:T(8,128)S(1)}, u32[]{:S(2)}, u32[]{:S(2)}) collective-permute-start(f32[208,256]{1,0:T(8,128)S(1)} %get-tuple-element.40), channel_id=1, source_target_pairs={{0,64},{1,5},{2,66},{3,7},{4,68},{5,1},{6,70},{7,3},{8,72},{9,13},... | collective-permute-start | bytes 638984 | tf_op jit(solution)/shard_map/ppermute | solution.py:363
  53.0 5.8 %collective-permute-start.8 = (f32[208,256]{1,0:T(8,128)S(1)}, f32[208,256]{1,0:T(8,128)S(1)}, u32[]{:S(2)}, u32[]{:S(2)}) collective-permute-start(f32[208,256]{1,0:T(8,128)S(1)} %get-tuple-element.38.sent), channel_id=1, source_target_pairs={{0,96},{1,7},{2,98},{3,1},{4,100},{5,3},{6,102},{7,5},{8,104},{9,1... | collective-permute-start | bytes 638984 | tf_op jit(solution)/shard_map/ppermute | solution.py:363
  58.8 4.9 %collective-permute-start.12 = (f32[112,256]{1,0:T(8,128)S(1)}, f32[112,256]{1,0:T(8,128)S(1)}, u32[]{:S(2)}, u32[]{:S(2)}) collective-permute-start(f32[112,256]{1,0:T(8,128)S(1)} %get-tuple-element.43), channel_id=1, source_target_pairs={{0,8},{1,33},{2,10},{3,35},{4,12},{5,37},{6,14},{7,39},{8,16},{9,4... | collective-permute-start | bytes 344072 | tf_op jit(solution)/shard_map/ppermute | solution.py:363
  59.9 6.0 %collective-permute-start.13 = (f32[112,256]{1,0:T(8,128)S(1)}, f32[112,256]{1,0:T(8,128)S(1)}, u32[]{:S(2)}, u32[]{:S(2)}) collective-permute-start(f32[112,256]{1,0:T(8,128)S(1)} %get-tuple-element.44), channel_id=1, source_target_pairs={{0,16},{1,65},{2,18},{3,67},{4,20},{5,69},{6,22},{7,71},{8,24},{9,... | collective-permute-start | bytes 344072 | tf_op jit(solution)/shard_map/ppermute | solution.py:363
  62.5 3.9 %collective-permute-start.11 = (f32[112,256]{1,0:T(8,128)S(1)}, f32[112,256]{1,0:T(8,128)S(1)}, u32[]{:S(2)}, u32[]{:S(2)}) collective-permute-start(f32[112,256]{1,0:T(8,128)S(1)} %get-tuple-element.42.sent), channel_id=1, source_target_pairs={{0,24},{1,97},{2,26},{3,99},{4,28},{5,101},{6,30},{7,103},{8,0},{9... | collective-permute-start | bytes 344072 | tf_op jit(solution)/shard_map/ppermute | solution.py:363
  66.5 4.7 %collective-permute-start.14 = (f32[80,256]{1,0:T(8,128)S(1)}, f32[80,256]{1,0:T(8,128)S(1)}, u32[]{:S(2)}, u32[]{:S(2)}) collective-permute-start(f32[80,256]{1,0:T(8,128)S(1)} %get-tuple-element.46.own_ref), channel_id=1, source_target_pairs={{0,1},{1,0},{2,3},{3,2},{4,5},{5,4},{6,7},{7,6},{8,9},{9,8},{10,11... | collective-permute-start | bytes 245768 | tf_op jit(solution)/shard_map/ppermute | solution.py:384

commit v7 on v6

--- a/solution.py
+++ b/solution.py
@@ -237,10 +237,10 @@
 def chol_inverse(x):
     lane = lax.broadcasted_iota(jnp.int32, (B, HALF), 1)
     n = HALF // B
+    panel = x[0:B, :]
     for j in range(n):
         o = j * B
         inside = (lane >= o) & (lane < o + B)
-        panel = x[o : o + B, :]
         cols = [across(panel, o + b) for b in range(B)]
         d = [
             [jnp.broadcast_to(cols[b][a : a + 1, :], (B, HALF)) for b in range(a + 1)]
@@ -275,6 +275,7 @@
                 following = following - scaled * v[i]
         if more:
             x[o + B : o + 2 * B, :] = following
+            panel = following
         if j + 2 < n:
             y = [None] * B
             for i in reversed(range(B)):

time: 79.4 us -> 79.4 us (level)
  no operation moved by 1% of the time
where the time goes in v7:
time: 79.4 us; the launch traced here: 79.3 us
  Pallas kernels  35.2 us (44%)
  starting transfers between devices  22.8 us (29%)
  waiting for transfers between devices  21.2 us (27%)
    pallas_call x1, Pallas kernels, local_products(): pl.pallas_call(functools.partial(local_kernel, steps), grid_spec=pl.GridS...  26.6 us
    ppermute x9, waiting for transfers between devices, along(): lax.ppermute(m, every, ring_pairs(axes, k))  17.4 us
    ppermute x9, starting transfers between devices, along(): lax.ppermute(m, every, ring_pairs(axes, k))  15 us
    pallas_call x1, Pallas kernels, finish(): pl.pallas_call(finish_kernel, out_shape=blocks(), in_specs=[vmem] * 3, ou...  8.05 us
    ppermute x1, starting transfers between devices, local(): return finish(m, g, lax.ppermute(g, 'core', swap))  3.82 us
    ppermute x3, starting transfers between devices, local(): got[k] = lax.ppermute(send[k], 'core', swap)  2.33 us
  transfers between devices with their start and end apart: 15, of which 11 were waited for; matrix products, arithmetic and copies ran while one was open for 0% of the time, Pallas kernels for 0%

profile of v7, /device:TPU:1, one launch (start us, length us, event | category | flops | bytes accessed | tf_op | source)
XLA Modules:
  0.0 79.3 jit_solution(6081513411382810334)
XLA Ops:
  0.0 0.1 pad_add_fusion.place_ref
  0.1 26.6 %local_products.1 = (f32[4,4,4,32,256]{4,3,2,1,0:T(8,128)S(1)}, f32[4,4,32,256]{3,2,1,0:T(8,128)S(1)}, f32[4,4,32,256]{3,2,1,0:T(8,128)S(1)}, f32[4,4,32,256]{3,...) custom-call(s32[4]{0:T(128)S(1)} %pad_add_fusion.place_ref, ...), custom_call_target="tpu_custom_call" | custom-call | flops 20937965568 | bytes 31457280 | tf_op jit(solution)/shard_map/local_products/pallas_call | solution.py:124
  26.7 1.5 %collective-permute-start = (f32[80,256]{1,0:T(8,128)S(1)}, f32[80,256]{1,0:T(8,128)S(1)}, u32[]{:S(2)}, u32[]{:S(2)}) collective-permute-start(f32[80,256]{1,0:T(8,128)S(1)} %get-tuple-element.30), channel_id=1, source_target_pairs={{0,1},{1,0},{2,3},{3,2},{4,5},{5,4},{6,7},{7,6},{8,9},{9,8},{10,11... | collective-permute-start | bytes 245768 | tf_op jit(solution)/shard_map/ppermute | solution.py:372
  28.2 0.1 collective-permute-start.2
  28.3 0.8 %collective-permute-done.gg_ref = f32[80,256]{1,0:T(8,128)S(1)} collective-permute-done((f32[80,256]{1,0:T(8,128)S(1)}, f32[80,256]{1,0:T(8,128)S(1)}, u32[]{:S(2)}, u32[]{:S(2)}) %collective-permute-start) | collective-permute-done | bytes 81952 | tf_op jit(solution)/shard_map/ppermute | solution.py:372
  29.2 0.4 collective-permute-start.6
  29.5 0.2 collective-permute-start.4
  29.7 0.5 collective-permute-done.2.got_ref
  30.1 0.1 message.3
  30.2 2.9 %collective-permute-start.3 = (f32[592,256]{1,0:T(8,128)S(1)}, f32[592,256]{1,0:T(8,128)S(1)}, u32[]{:S(2)}, u32[]{:S(2)}) collective-permute-start(f32[592,256]{1,0:T(8,128)S(1)} %message.3), channel_id=1, source_target_pairs={{0,4},{1,17},{2,6},{3,19},{4,0},{5,21},{6,2},{7,23},{8,12},{9,25},... | collective-permute-start | bytes 1818632 | tf_op jit(solution)/shard_map/ppermute | solution.py:364
  33.2 0.9 %collective-permute-start.7 = (f32[592,256]{1,0:T(8,128)S(1)}, f32[592,256]{1,0:T(8,128)S(1)}, u32[]{:S(2)}, u32[]{:S(2)}) collective-permute-start(f32[592,256]{1,0:T(8,128)S(1)} %message.5), channel_id=1, source_target_pairs={{0,6},{1,25},{2,0},{3,27},{4,2},{5,29},{6,4},{7,31},{8,14},{9,1},{... | collective-permute-start | bytes 1818632 | tf_op jit(solution)/shard_map/ppermute | solution.py:364
  34.1 0.1 message.4
  34.2 0.7 collective-permute-start.5
  34.9 1.8 %collective-permute-start.1 = (f32[4,4,32,256]{3,2,1,0:T(8,128)S(1)}, f32[4,4,32,256]{3,2,1,0:T(8,128)S(1)}, u32[]{:S(2)}, u32[]{:S(2)}) collective-permute-start(f32[4,4,32,256]{3,2,1,0:T(8,128)S(1)} %get-tuple-element.31), channel_id=1, source_target_pairs={{0,1},{1,0},{2,3},{3,2},{4,5},{5,4},{6,7},{7,6},{8,9},{9,8},{10,11... | collective-permute-start | bytes 1572872 | tf_op jit(solution)/shard_map/ppermute | solution.py:377
  36.7 1.5 %collective-permute-done.1.got_ref = f32[4,4,32,256]{3,2,1,0:T(8,128)S(1)} collective-permute-done((f32[4,4,32,256]{3,2,1,0:T(8,128)S(1)}, f32[4,4,32,256]{3,2,1,0:T(8,128)S(1)}, u32[]{:S(2)}, u32[]{:S(2)}) %collective-permute-start.1) | collective-permute-done | bytes 524320 | tf_op jit(solution)/shard_map/ppermute | solution.py:377
  38.2 2.8 %collective-permute-done.3.a = f32[592,256]{1,0:T(8,128)S(1)} collective-permute-done((f32[592,256]{1,0:T(8,128)S(1)}, f32[592,256]{1,0:T(8,128)S(1)}, u32[]{:S(2)}, u32[]{:S(2)}) %collective-permute-start.3) | collective-permute-done | bytes 606240 | tf_op jit(solution)/shard_map/ppermute | solution.py:364
  41.0 6.7 %collective-permute-done.7.c = f32[592,256]{1,0:T(8,128)S(1)} collective-permute-done((f32[592,256]{1,0:T(8,128)S(1)}, f32[592,256]{1,0:T(8,128)S(1)}, u32[]{:S(2)}, u32[]{:S(2)}) %collective-permute-start.7) | collective-permute-done | bytes 606240 | tf_op jit(solution)/shard_map/ppermute | solution.py:364
  47.7 0.2 second.1
  48.0 1.7 %collective-permute-start.9 = (f32[208,256]{1,0:T(8,128)S(1)}, f32[208,256]{1,0:T(8,128)S(1)}, u32[]{:S(2)}, u32[]{:S(2)}) collective-permute-start(f32[208,256]{1,0:T(8,128)S(1)} %get-tuple-element.39), channel_id=1, source_target_pairs={{0,32},{1,3},{2,34},{3,5},{4,36},{5,7},{6,38},{7,1},{8,40},{9,11},... | collective-permute-start | bytes 638984 | tf_op jit(solution)/shard_map/ppermute | solution.py:364
  49.7 3.3 %collective-permute-start.10 = (f32[208,256]{1,0:T(8,128)S(1)}, f32[208,256]{1,0:T(8,128)S(1)}, u32[]{:S(2)}, u32[]{:S(2)}) collective-permute-start(f32[208,256]{1,0:T(8,128)S(1)} %get-tuple-element.40), channel_id=1, source_target_pairs={{0,64},{1,5},{2,66},{3,7},{4,68},{5,1},{6,70},{7,3},{8,72},{9,13},... | collective-permute-start | bytes 638984 | tf_op jit(solution)/shard_map/ppermute | solution.py:364
  53.0 0.7 collective-permute-start.8
  53.7 1.6 %collective-permute-done.9.b = f32[208,256]{1,0:T(8,128)S(1)} collective-permute-done((f32[208,256]{1,0:T(8,128)S(1)}, f32[208,256]{1,0:T(8,128)S(1)}, u32[]{:S(2)}, u32[]{:S(2)}) %collective-permute-start.9) | collective-permute-done | bytes 213024 | tf_op jit(solution)/shard_map/ppermute | solution.py:364
  55.3 3.5 %collective-permute-done.10.c = f32[208,256]{1,0:T(8,128)S(1)} collective-permute-done((f32[208,256]{1,0:T(8,128)S(1)}, f32[208,256]{1,0:T(8,128)S(1)}, u32[]{:S(2)}, u32[]{:S(2)}) %collective-permute-start.10) | collective-permute-done | bytes 213024 | tf_op jit(solution)/shard_map/ppermute | solution.py:364
  58.8 1.1 %collective-permute-start.12 = (f32[112,256]{1,0:T(8,128)S(1)}, f32[112,256]{1,0:T(8,128)S(1)}, u32[]{:S(2)}, u32[]{:S(2)}) collective-permute-start(f32[112,256]{1,0:T(8,128)S(1)} %get-tuple-element.43), channel_id=1, source_target_pairs={{0,8},{1,33},{2,10},{3,35},{4,12},{5,37},{6,14},{7,39},{8,16},{9,4... | collective-permute-start | bytes 344072 | tf_op jit(solution)/shard_map/ppermute | solution.py:364
  59.9 2.6 %collective-permute-start.13 = (f32[112,256]{1,0:T(8,128)S(1)}, f32[112,256]{1,0:T(8,128)S(1)}, u32[]{:S(2)}, u32[]{:S(2)}) collective-permute-start(f32[112,256]{1,0:T(8,128)S(1)} %get-tuple-element.44), channel_id=1, source_target_pairs={{0,16},{1,65},{2,18},{3,67},{4,20},{5,69},{6,22},{7,71},{8,24},{9,... | collective-permute-start | bytes 344072 | tf_op jit(solution)/shard_map/ppermute | solution.py:364
  62.5 1.1 %collective-permute-start.11 = (f32[112,256]{1,0:T(8,128)S(1)}, f32[112,256]{1,0:T(8,128)S(1)}, u32[]{:S(2)}, u32[]{:S(2)}) collective-permute-start(f32[112,256]{1,0:T(8,128)S(1)} %get-tuple-element.42.sent), channel_id=1, source_target_pairs={{0,24},{1,97},{2,26},{3,99},{4,28},{5,101},{6,30},{7,103},{8,0},{9... | collective-permute-start | bytes 344072 | tf_op jit(solution)/shard_map/ppermute | solution.py:364
  63.6 0.2 collective-permute-done.12.b
  63.8 2.2 %collective-permute-done.13.c = f32[112,256]{1,0:T(8,128)S(1)} collective-permute-done((f32[112,256]{1,0:T(8,128)S(1)}, f32[112,256]{1,0:T(8,128)S(1)}, u32[]{:S(2)}, u32[]{:S(2)}) %collective-permute-start.13) | collective-permute-done | bytes 114720 | tf_op jit(solution)/shard_map/ppermute | solution.py:364
  66.0 0.5 collective-permute-done.11.a
  66.5 3.8 %collective-permute-start.14 = (f32[80,256]{1,0:T(8,128)S(1)}, f32[80,256]{1,0:T(8,128)S(1)}, u32[]{:S(2)}, u32[]{:S(2)}) collective-permute-start(f32[80,256]{1,0:T(8,128)S(1)} %get-tuple-element.46.own_ref), channel_id=1, source_target_pairs={{0,1},{1,0},{2,3},{3,2},{4,5},{5,4},{6,7},{7,6},{8,9},{9,8},{10,11... | collective-permute-start | bytes 245768 | tf_op jit(solution)/shard_map/ppermute | solution.py:385
  70.3 0.9 %collective-permute-done.14.other_ref = f32[80,256]{1,0:T(8,128)S(1)} collective-permute-done((f32[80,256]{1,0:T(8,128)S(1)}, f32[80,256]{1,0:T(8,128)S(1)}, u32[]{:S(2)}, u32[]{:S(2)}) %collective-permute-start.14) | collective-permute-done | bytes 81952 | tf_op jit(solution)/shard_map/ppermute | solution.py:385
  71.3 8.0 %finish.1 = f32[32,256]{1,0:T(8,128)} custom-call(f32[32,256]{1,0:T(8,128)S(1)} %get-tuple-element.45.m_ref, f32[80,256]{1,0:T(8,128)S(1)} %get-tuple-element.46.own_ref, f32[80,256]{1,0:T(8,128)S(1)} %collective-permute-done.14.other_ref), custom_call_target="tpu_custom_call" | custom-call | tf_op jit(solution)/shard_map/finish/pallas_call | solution.py:331
  (7 shorter events, 0.2 us)
Async XLA Ops:
  26.7 2.4 %collective-permute-start = (f32[80,256]{1,0:T(8,128)S(1)}, f32[80,256]{1,0:T(8,128)S(1)}, u32[]{:S(2)}, u32[]{:S(2)}) collective-permute-start(f32[80,256]{1,0:T(8,128)S(1)} %get-tuple-element.30), channel_id=1, source_target_pairs={{0,1},{1,0},{2,3},{3,2},{4,5},{5,4},{6,7},{7,6},{8,9},{9,8},{10,11... | collective-permute-start | bytes 245768 | tf_op jit(solution)/shard_map/ppermute | solution.py:372
  28.2 1.9 %collective-permute-start.2 = (f32[4,4,32,256]{3,2,1,0:T(8,128)S(1)}, f32[4,4,32,256]{3,2,1,0:T(8,128)S(1)}, u32[]{:S(2)}, u32[]{:S(2)}) collective-permute-start(f32[4,4,32,256]{3,2,1,0:T(8,128)S(1)} %get-tuple-element.34), channel_id=1, source_target_pairs={{0,1},{1,0},{2,3},{3,2},{4,5},{5,4},{6,7},{7,6},{8,9},{9,8},{10,11... | collective-permute-start | bytes 1572872 | tf_op jit(solution)/shard_map/ppermute | solution.py:371
  29.2 4.0 %collective-permute-start.6 = (f32[4,4,32,256]{3,2,1,0:T(8,128)S(1)}, f32[4,4,32,256]{3,2,1,0:T(8,128)S(1)}, u32[]{:S(2)}, u32[]{:S(2)}) collective-permute-start(f32[4,4,32,256]{3,2,1,0:T(8,128)S(1)} %get-tuple-element.36), channel_id=1, source_target_pairs={{0,1},{1,0},{2,3},{3,2},{4,5},{5,4},{6,7},{7,6},{8,9},{9,8},{10,11... | collective-permute-start | bytes 1572872 | tf_op jit(solution)/shard_map/ppermute | solution.py:377
  29.5 4.6 %collective-permute-start.4 = (f32[4,4,32,256]{3,2,1,0:T(8,128)S(1)}, f32[4,4,32,256]{3,2,1,0:T(8,128)S(1)}, u32[]{:S(2)}, u32[]{:S(2)}) collective-permute-start(f32[4,4,32,256]{3,2,1,0:T(8,128)S(1)} %get-tuple-element.35), channel_id=1, source_target_pairs={{0,1},{1,0},{2,3},{3,2},{4,5},{5,4},{6,7},{7,6},{8,9},{9,8},{10,11... | collective-permute-start | bytes 1572872 | tf_op jit(solution)/shard_map/ppermute | solution.py:377
  30.2 10.8 %collective-permute-start.3 = (f32[592,256]{1,0:T(8,128)S(1)}, f32[592,256]{1,0:T(8,128)S(1)}, u32[]{:S(2)}, u32[]{:S(2)}) collective-permute-start(f32[592,256]{1,0:T(8,128)S(1)} %message.3), channel_id=1, source_target_pairs={{0,4},{1,17},{2,6},{3,19},{4,0},{5,21},{6,2},{7,23},{8,12},{9,25},... | collective-permute-start | bytes 1818632 | tf_op jit(solution)/shard_map/ppermute | solution.py:364
  33.2 14.5 %collective-permute-start.7 = (f32[592,256]{1,0:T(8,128)S(1)}, f32[592,256]{1,0:T(8,128)S(1)}, u32[]{:S(2)}, u32[]{:S(2)}) collective-permute-start(f32[592,256]{1,0:T(8,128)S(1)} %message.5), channel_id=1, source_target_pairs={{0,6},{1,25},{2,0},{3,27},{4,2},{5,29},{6,4},{7,31},{8,14},{9,1},{... | collective-permute-start | bytes 1818632 | tf_op jit(solution)/shard_map/ppermute | solution.py:364
  34.2 13.5 %collective-permute-start.5 = (f32[592,256]{1,0:T(8,128)S(1)}, f32[592,256]{1,0:T(8,128)S(1)}, u32[]{:S(2)}, u32[]{:S(2)}) collective-permute-start(f32[592,256]{1,0:T(8,128)S(1)} %message.4), channel_id=1, source_target_pairs={{0,2},{1,9},{2,4},{3,11},{4,6},{5,13},{6,0},{7,15},{8,10},{9,17},{... | collective-permute-start | bytes 1818632 | tf_op jit(solution)/shard_map/ppermute | solution.py:364
  34.9 3.4 %collective-permute-start.1 = (f32[4,4,32,256]{3,2,1,0:T(8,128)S(1)}, f32[4,4,32,256]{3,2,1,0:T(8,128)S(1)}, u32[]{:S(2)}, u32[]{:S(2)}) collective-permute-start(f32[4,4,32,256]{3,2,1,0:T(8,128)S(1)} %get-tuple-element.31), channel_id=1, source_target_pairs={{0,1},{1,0},{2,3},{3,2},{4,5},{5,4},{6,7},{7,6},{8,9},{9,8},{10,11... | collective-permute-start | bytes 1572872 | tf_op jit(solution)/shard_map/ppermute | solution.py:377
  48.0 7.3 %collective-permute-start.9 = (f32[208,256]{1,0:T(8,128)S(1)}, f32[208,256]{1,0:T(8,128)S(1)}, u32[]{:S(2)}, u32[]{:S(2)}) collective-permute-start(f32[208,256]{1,0:T(8,128)S(1)} %get-tuple-element.39), channel_id=1, source_target_pairs={{0,32},{1,3},{2,34},{3,5},{4,36},{5,7},{6,38},{7,1},{8,40},{9,11},... | collective-permute-start | bytes 638984 | tf_op jit(solution)/shard_map/ppermute | solution.py:364
  49.7 9.1 %collective-permute-start.10 = (f32[208,256]{1,0:T(8,128)S(1)}, f32[208,256]{1,0:T(8,128)S(1)}, u32[]{:S(2)}, u32[]{:S(2)}) collective-permute-start(f32[208,256]{1,0:T(8,128)S(1)} %get-tuple-element.40), channel_id=1, source_target_pairs={{0,64},{1,5},{2,66},{3,7},{4,68},{5,1},{6,70},{7,3},{8,72},{9,13},... | collective-permute-start | bytes 638984 | tf_op jit(solution)/shard_map/ppermute | solution.py:364
  53.0 5.8 %collective-permute-start.8 = (f32[208,256]{1,0:T(8,128)S(1)}, f32[208,256]{1,0:T(8,128)S(1)}, u32[]{:S(2)}, u32[]{:S(2)}) collective-permute-start(f32[208,256]{1,0:T(8,128)S(1)} %get-tuple-element.38.sent), channel_id=1, source_target_pairs={{0,96},{1,7},{2,98},{3,1},{4,100},{5,3},{6,102},{7,5},{8,104},{9,1... | collective-permute-start | bytes 638984 | tf_op jit(solution)/shard_map/ppermute | solution.py:364
  58.8 4.9 %collective-permute-start.12 = (f32[112,256]{1,0:T(8,128)S(1)}, f32[112,256]{1,0:T(8,128)S(1)}, u32[]{:S(2)}, u32[]{:S(2)}) collective-permute-start(f32[112,256]{1,0:T(8,128)S(1)} %get-tuple-element.43), channel_id=1, source_target_pairs={{0,8},{1,33},{2,10},{3,35},{4,12},{5,37},{6,14},{7,39},{8,16},{9,4... | collective-permute-start | bytes 344072 | tf_op jit(solution)/shard_map/ppermute | solution.py:364
  59.9 6.0 %collective-permute-start.13 = (f32[112,256]{1,0:T(8,128)S(1)}, f32[112,256]{1,0:T(8,128)S(1)}, u32[]{:S(2)}, u32[]{:S(2)}) collective-permute-start(f32[112,256]{1,0:T(8,128)S(1)} %get-tuple-element.44), channel_id=1, source_target_pairs={{0,16},{1,65},{2,18},{3,67},{4,20},{5,69},{6,22},{7,71},{8,24},{9,... | collective-permute-start | bytes 344072 | tf_op jit(solution)/shard_map/ppermute | solution.py:364
  62.5 3.9 %collective-permute-start.11 = (f32[112,256]{1,0:T(8,128)S(1)}, f32[112,256]{1,0:T(8,128)S(1)}, u32[]{:S(2)}, u32[]{:S(2)}) collective-permute-start(f32[112,256]{1,0:T(8,128)S(1)} %get-tuple-element.42.sent), channel_id=1, source_target_pairs={{0,24},{1,97},{2,26},{3,99},{4,28},{5,101},{6,30},{7,103},{8,0},{9... | collective-permute-start | bytes 344072 | tf_op jit(solution)/shard_map/ppermute | solution.py:364
  66.5 4.7 %collective-permute-start.14 = (f32[80,256]{1,0:T(8,128)S(1)}, f32[80,256]{1,0:T(8,128)S(1)}, u32[]{:S(2)}, u32[]{:S(2)}) collective-permute-start(f32[80,256]{1,0:T(8,128)S(1)} %get-tuple-element.46.own_ref), channel_id=1, source_target_pairs={{0,1},{1,0},{2,3},{3,2},{4,5},{5,4},{6,7},{7,6},{8,9},{9,8},{10,11... | collective-permute-start | bytes 245768 | tf_op jit(solution)/shard_map/ppermute | solution.py:385
